TPU v7x, 32 devices: a whole 2x2x4 slice. The times are simulated.
32 devices in a mesh: groups: 2 (over y), expert: 8 (over z, x), tensor: 2 (over core).
Axes of the slice: x: 2, y: 2, z: 4, core: 2. Of those that a mesh axis runs over, the one named last changes fastest.
Arguments:
- attn_out: bfloat16 [2048, 16384], P(('groups', 'expert'), 'tensor'), parts along dimension 0, may hold values from -6 to 6
- out_weight: bfloat16 [16384, 3584], P('tensor', 'expert'), may hold values from -0.0625 to 0.0625
- residual: bfloat16 [2048, 3584], P(('groups', 'expert'), 'tensor'), parts along dimension 0, may hold values from -6 to 6
- norm_gain: bfloat16 [3584], P('tensor'), may hold values from 0.25 to 1.75
- router_weight: float32 [3584, 8], P('tensor'), may hold values from -0.3 to 0.3
- routes: int32 [2048, 3], P(('groups', 'expert')), parts along dimension 0, may hold values from 0 to 7, all different within a row; in each aligned block of 128 rows (0 to 127, 128 to 255, ...) at most 50 rows name the same one
- gate_weight: bfloat16 [8, 3584, 2048], P('expert', None, 'tensor'), may hold values from -0.09375 to 0.09375
- up_weight: bfloat16 [8, 3584, 2048], P('expert', None, 'tensor'), may hold values from -0.09375 to 0.09375
- down_weight: bfloat16 [8, 2048, 3584], P('expert', None, 'tensor'), may hold values from -0.125 to 0.125
Outputs:
- mixed: bfloat16 [2048, 3584], P(('groups', 'expert'), 'tensor'), parts along dimension 0
There are 2 independent parts, one for each index of `groups`. A program takes and returns all parts, laid end to end along the dimension named above; an argument that names none is the same for every part. Nothing has to cross between parts.
Inputs may be any that keep to these rules, and one draw needn't show every extreme that they name: `routes`: each row names 3 different experts. Within the 128 rows of one index of expert (aligned blocks), no expert is named by more than 50 rows, and in every draw some block has an expert named by exactly 50 rows.
All inputs are finite; a program needn't handle non-finite values.
Results may differ from a plain program's by a relative error of at most 0.0053.
Values may be sent and summed in bfloat16 or wider, within the bound.
No kernel may reach another device: no remote copies, remote signals or barrier semaphores. Data moves between devices by JAX's collectives and lax.ppermute only.
A program may use at most 192 MiB of HBM per device.

v0:
```python
import jax
import jax.numpy as jnp
from jax import lax
from jax.sharding import PartitionSpec as P

EPS = 1e-06
ROUTE_SCALE = 2.5


def on_device(
    attn_out,
    out_weight,
    residual,
    norm_gain,
    router_weight,
    routes,
    gate_weight,
    up_weight,
    down_weight,
):
    token_count = attn_out.shape[0]
    partial_proj = jnp.dot(
        attn_out,
        lax.all_gather(out_weight, "expert", axis=1, tiled=True),
        preferred_element_type=jnp.float32,
    )
    branch = lax.psum_scatter(partial_proj, "tensor", scatter_dimension=1, tiled=True)
    hidden = residual.astype(jnp.float32) + branch
    tensor_count = lax.axis_size("tensor")
    features = tensor_count * hidden.shape[1]
    scaled = hidden * norm_gain.astype(jnp.float32)
    squares = jnp.sum(hidden * hidden, axis=1)
    raw_logits = jnp.dot(scaled, router_weight, precision=lax.Precision.HIGHEST)
    total_squares, total_logits = lax.psum((squares, raw_logits), "tensor")
    inverse_rms = lax.rsqrt(total_squares / features + EPS)
    logits = total_logits * inverse_rms[:, None]
    normed_rows = (scaled * inverse_rms[:, None]).astype(jnp.bfloat16)
    expert_total = logits.shape[1]
    per_token = routes.shape[1]
    capacity = tensor_count * (token_count * per_token // expert_total // tensor_count + 1)
    scores = jax.nn.sigmoid(logits)
    picked = routes[:, :, None] == jnp.arange(expert_total, dtype=jnp.int32)[None, None, :]
    chosen = jnp.sum(jnp.where(picked, scores[:, None, :], 0.0), axis=2)
    gate_values = ROUTE_SCALE * chosen / jnp.sum(chosen, axis=1, keepdims=True)
    flat_hits = picked.reshape(token_count * per_token, expert_total).astype(jnp.int32)
    earlier = jnp.cumsum(flat_hits, axis=0) - flat_hits
    slot_rank = jnp.sum(earlier * flat_hits, axis=1)
    target = routes.reshape(-1) * capacity + slot_rank
    placed = jnp.arange(expert_total * capacity, dtype=jnp.int32)[:, None] == target[None, :]
    dispatch_matrix = jnp.any(
        placed.reshape(expert_total * capacity, token_count, per_token), axis=2
    ).astype(jnp.bfloat16)
    gate_matrix = jnp.sum(
        jnp.where(placed, gate_values.reshape(-1)[None, :], 0.0).reshape(
            expert_total * capacity, token_count, per_token
        ),
        axis=2,
    )
    buffer = jnp.dot(dispatch_matrix, normed_rows, preferred_element_type=jnp.float32).astype(
        jnp.bfloat16
    )
    arrived = lax.all_to_all(
        buffer.reshape(expert_total, capacity, -1),
        "expert",
        split_axis=0,
        concat_axis=0,
        tiled=True,
    )
    slot_rows = lax.all_gather(
        arrived.reshape(expert_total * capacity, -1), "tensor", axis=1, tiled=True
    )
    gate_part = jnp.dot(slot_rows, gate_weight[0], preferred_element_type=jnp.float32)
    up_part = jnp.dot(slot_rows, up_weight[0], preferred_element_type=jnp.float32)
    activated = (jax.nn.silu(gate_part) * up_part).astype(jnp.bfloat16)
    whole_units = lax.all_gather(activated, "tensor", axis=1, tiled=True)
    out_rows = jnp.dot(whole_units, down_weight[0], preferred_element_type=jnp.float32).astype(
        jnp.bfloat16
    )
    returned = lax.all_to_all(
        out_rows.reshape(expert_total, capacity, -1),
        "expert",
        split_axis=0,
        concat_axis=0,
        tiled=True,
    )
    returned_rows = returned.reshape(expert_total * capacity, -1).astype(jnp.float32)
    expert_sum = jnp.einsum(
        "st,sd->td", gate_matrix, returned_rows, precision=lax.Precision.HIGHEST
    )
    return (hidden + expert_sum).astype(jnp.bfloat16)


def solution(mesh):
    placed = (
        P(("groups", "expert"), "tensor"),
        P("tensor", "expert"),
        P(("groups", "expert"), "tensor"),
        P("tensor"),
        P("tensor", None),
        P(("groups", "expert"), None),
        P("expert", None, "tensor"),
        P("expert", None, "tensor"),
        P("expert", None, "tensor"),
    )
    return jax.shard_map(
        on_device,
        mesh=mesh,
        in_specs=placed,
        out_specs=P(("groups", "expert"), "tensor"),
        check_vma=False,
    )
```

profile of v0, /device:TPU:19, one launch (start us, length us, event | category | flops | bytes accessed | tf_op | source)
XLA Modules:
  0.0 1308.6 jit_solution(8989927854063917188)
XLA Ops:
  6.5 0.7 all-gather.4.cloned.1.call-update
  7.3 1111.4 %all-gather.4.cloned.1.call-done = bf16[8192,3584]{0,1:T(8,128)(2,1)} async-done(((bf16[8192,448]{0,1:T(8,128)(2,1)}), bf16[8192,3584]{0,1:T(8,128)(2,1)}) %all-gather.4.cloned.1.call-update) | async-done | bytes 58720272 | tf_op jit(solution)/shard_map/all_gather | solution.py:24
  1118.7 26.5 %fusion.21 = f32[128,3584]{1,0:T(8,128)} fusion(bf16[128,8192]{1,0:T(8,128)(2,1)S(1)} %copy-done, bf16[8192,3584]{0,1:T(8,128)(2,1)} %all-gather.4.cloned.1.call-done), kind=kOutput, calls=%fused_computation.36 | convolution fusion | flops 7516192768 | bytes 62652416 | tf_op jit(solution)/shard_map/dot_general | solution.py:22
  1145.3 0.1 copy.24
  1145.4 0.2 eq.52
  1145.6 0.2 eq.48
  1145.8 0.9 reduce-window.6
  1146.7 0.2 slice_reduce_fusion
  1146.9 0.1 fusion.19
  1147.0 0.2 reduce_sum.48
  1147.2 0.1 copy.26
  1147.3 0.1 fusion.14
  1147.4 8.9 reduce-scatter.2.cloned.1.call-done
  1156.3 1.5 multiply_reduce_fusion
  1157.8 2.0 fusion.12
  1159.8 2.5 all-reduce
  1162.3 1.7 convolution_convert_fusion
  1164.0 1.5 reshape.77
  1165.6 41.1 %all_to_all.10 = bf16[8,50,1792]{2,1,0:T(8,128)(2,1)} all-to-all(bf16[8,50,1792]{2,1,0:T(8,128)(2,1)S(1)} %reshape.77), channel_id=1, replica_groups=mesh['groups'=2,'expert'=8,'tensor'=2] {'expert'}, dimensions={0} | all-to-all | bytes 2867200 | tf_op jit(solution)/shard_map/all_to_all | solution.py:62
  1206.6 2.4 reshape.78
  1209.1 0.2 all-gather.8.cloned.1.call-start
  1209.3 13.4 %all-gather.6.cloned.1.call-done = bf16[400,3584]{1,0:T(8,128)(2,1)} async-done(((bf16[400,1792]{1,0:T(8,128)(2,1)}), bf16[400,3584]{1,0:T(8,128)(2,1)}) %all-gather.6.cloned.1.call-update) | async-done | bytes 2867216 | tf_op jit(solution)/shard_map/all_gather | solution.py:69
  1222.7 7.1 fusion.4
  1229.9 7.2 multiply_convert_fusion
  1237.2 11.2 all-gather.8.cloned.1.call-done
  1248.4 6.7 fusion.6
  1255.1 1.4 reshape.79
  1256.5 5.5 all-to-all-start.1
  1262.0 0.7 select_reduce_fusion
  1262.7 33.6 %all-to-all-done.1 = bf16[8,50,1792]{2,1,0:T(8,128)(2,1)} async-done(((bf16[8,50,1792]{2,1,0:T(8,128)(2,1)}), bf16[8,50,1792]{2,1,0:T(8,128)(2,1)}, u32[]{:S(2)}, u32[]{:S(2)}) %all-to-all-start.1) | async-done | bytes 1433632 | tf_op jit(solution)/shard_map/all_to_all | solution.py:79
  1296.3 2.6 reshape.80
  1298.9 3.2 fusion.9
  (30 shorter events, 0.3 us)
Async XLA Ops:
  6.5 1112.2 %copy-start = (bf16[128,8192]{1,0:T(8,128)(2,1)S(1)}, bf16[128,8192]{1,0:T(8,128)(2,1)}, u32[]{:S(2)}) copy-start(bf16[128,8192]{1,0:T(8,128)(2,1)} %param.9) | copy-start | bytes 6291460
  6.5 1112.2 %all-gather.4.cloned.1.call-start = ((), (), s32[]{:S(2)}) async-start(), calls=%async_computation.3 | async-start | bytes 66060288 | tf_op jit(solution)/shard_map/all_gather | solution.py:24
  7.3 1138.0 %copy-start.5 = (s32[128,3]{0,1:T(4,128)S(1)}, s32[128,3]{0,1:T(4,128)}, u32[]{:S(2)}) copy-start(s32[128,3]{0,1:T(4,128)} %param.14) | copy-start | bytes 4612
  7.3 1138.5 %copy-start.6 = (bf16[1792]{0:T(1024)(128)(2,1)S(1)}, bf16[1792]{0:T(1024)(128)(2,1)}, u32[]{:S(2)}) copy-start(bf16[1792]{0:T(1024)(128)(2,1)} %param.12) | copy-start | bytes 10756
  7.3 1149.0 %reduce-scatter.2.cloned.1.call-start = ((), (), s32[]{:S(2)}) async-start(), calls=%async_computation.4 | async-start | bytes 2752512 | tf_op jit(solution)/shard_map/reduce_scatter | solution.py:27
  1145.2 11.1 copy-start.3
  1145.2 12.6 copy-start.4
  1145.2 77.5 %all-gather.6.cloned.1.call-start = ((), (), s32[]{:S(2)}) async-start(), calls=%async_computation.5 | async-start | bytes 4300800 | tf_op jit(solution)/shard_map/all_gather | solution.py:69
  1156.3 6.0 copy-start.2
  1209.1 39.3 %all-gather.8.cloned.1.call-start = ((), (), s32[]{:S(2)}) async-start(), calls=%async_computation.6 | async-start | bytes 2457600 | tf_op jit(solution)/shard_map/all_gather | solution.py:75
  1222.7 7.2 copy-start.7
  1256.5 39.8 %all-to-all-start.1 = ((bf16[8,50,1792]{2,1,0:T(8,128)(2,1)}), bf16[8,50,1792]{2,1,0:T(8,128)(2,1)}, u32[]{:S(2)}, u32[]{:S(2)}) async-start(bf16[8,50,1792]{2,1,0:T(8,128)(2,1)} %reshape.79), calls=%async_computation.2 | async-start | bytes 3211264 | tf_op jit(solution)/shard_map/all_to_all | solution.py:79
  1296.3 5.8 copy-start.1
Sparse Core Ops, SparseCore 0:
  8.9 1109.7 all-gather.3
  1145.3 10.9 reduce-scatter.1
  1209.2 13.4 all-gather.5
  1237.3 11.0 all-gather.7
where the time goes:
time: 1310 us
  waiting for transfers between devices  1180 us (90%)
  matrix products  54.5 us (4%)
  blocking collectives  43.6 us (3%)
  between operations  13.3 us (1%)
    all_gather x1, waiting for transfers between devices, on_device(): lax.all_gather(out_weight, 'expert', axis=1, tiled=True)  1110 us
    all_to_all x1, blocking collectives, on_device(): lax.all_to_all(buffer.reshape(expert_total, capacity, -1), 'expert', spli...  41.1 us
    all_to_all x1, waiting for transfers between devices, on_device(): lax.all_to_all(out_rows.reshape(expert_total, capacity, -1), 'expert', sp...  33.6 us
    dot_general x1, matrix products, on_device(): jnp.dot(attn_out, lax.all_gather(out_weight, 'expert', axis=1, tiled=True...  26.5 us
  transfers between devices with their start and end apart: 5, of which 5 were waited for; matrix products, arithmetic and copies ran while one was open for 0% of the time, Pallas kernels for 0%

commit v1 on v0

--- a/solution.py
+++ b/solution.py
@@ -5,6 +5,133 @@
 
 EPS = 1e-06
 ROUTE_SCALE = 2.5
+PIECES = 2
+
+
+def swap_halves(array, axis_name):
+    return lax.ppermute(array, axis_name, [(0, 1), (1, 0)])
+
+
+def gather_tensor(rows):
+    if lax.axis_size("tensor") != 2:
+        return lax.all_gather(rows, "tensor", axis=1, tiled=True)
+    other = swap_halves(rows, "tensor")
+    first = lax.axis_index("tensor") == 0
+    return jnp.concatenate(
+        [jnp.where(first, rows, other), jnp.where(first, other, rows)], axis=1
+    )
+
+
+def pair_columns(out_weight):
+    expert_count = lax.axis_size("expert")
+    pair_swap = [(i, i ^ 1) for i in range(expert_count)]
+    depth = out_weight.shape[0]
+    even = lax.axis_index("expert") % 2 == 0
+    if lax.axis_size("groups") != 2:
+        other = lax.ppermute(out_weight, "expert", pair_swap)
+    else:
+        group = lax.axis_index("groups")
+        half = depth // 2
+        piece = half // PIECES
+        near, far = [], []
+        for i in range(PIECES):
+            block = lax.dynamic_slice_in_dim(out_weight, group * half + i * piece, piece, 0)
+            near.append(lax.ppermute(block, "expert", pair_swap))
+        for i in range(PIECES):
+            far.append(swap_halves(near[i], "groups"))
+        first = group == 0
+        other = jnp.concatenate(
+            [jnp.where(first, near[i], far[i]) for i in range(PIECES)]
+            + [jnp.where(first, far[i], near[i]) for i in range(PIECES)],
+            axis=0,
+        )
+    return jnp.concatenate(
+        [jnp.where(even, out_weight, other), jnp.where(even, other, out_weight)], axis=1
+    )
+
+
+def line_perm(step, right, width):
+    pairs = []
+    for h in range(width):
+        to = h + 1 if right else h - 1
+        origin = h - step if right else h + step
+        if 0 <= to < width and 0 <= origin < width:
+            pairs += [(2 * h + lo, 2 * to + lo) for lo in range(2)]
+    return pairs
+
+
+def return_perm(step, width, sides):
+    pairs = []
+    for h in range(width):
+        for side in sides:
+            to = h - 1 - step if side == "right" else h + 1 + step
+            if 0 <= to < width:
+                pairs += [(2 * h + lo, 2 * to + lo) for lo in range(2)]
+    return pairs
+
+
+def project(attn_out, out_weight):
+    width = lax.axis_size("expert") // 2
+    place = lax.axis_index("expert") // 2
+    tensor_count = lax.axis_size("tensor")
+    rows, depth = attn_out.shape
+    columns = pair_columns(out_weight)
+    span = columns.shape[1]
+    reduce_first = tensor_count == 2 and width % 2 == 0
+    core = lax.axis_index("tensor")
+    part = depth // PIECES
+    own = [attn_out[:, i * part : (i + 1) * part] for i in range(PIECES)]
+
+    arrivals = []
+    up, down = own, own
+    for step in range(width - 1):
+        up = [lax.ppermute(b, "expert", line_perm(step, True, width)) for b in up]
+        down = [lax.ppermute(b, "expert", line_perm(step, False, width)) for b in down]
+        if step > (width - 3) / 2:
+            from_below = place >= step + 1
+            merged = [jnp.where(from_below, u, d) for u, d in zip(up, down)]
+            arrivals.append((step, ("right", "left"), merged))
+        else:
+            arrivals.append((step, ("right",), up))
+            arrivals.append((step, ("left",), down))
+
+    def product(blocks):
+        total = sum(
+            jnp.dot(
+                block, columns[i * part : (i + 1) * part], preferred_element_type=jnp.float32
+            )
+            for i, block in enumerate(blocks)
+        )
+        if not reduce_first:
+            return total
+        half = span // 2
+        mine = lax.dynamic_slice_in_dim(total, core * half, half, 1)
+        other = lax.dynamic_slice_in_dim(total, (1 - core) * half, half, 1)
+        return (mine + swap_halves(other, "tensor")).astype(jnp.bfloat16)
+
+    own_sum = product(own)
+    share = own_sum.shape[1]
+    whole = jnp.zeros((width + 1, rows, share), own_sum.dtype)
+    whole = lax.dynamic_update_index_in_dim(whole, own_sum, place, 0)
+    for step, sides, blocks in arrivals:
+        back = lax.ppermute(product(blocks), "expert", return_perm(step, width, sides))
+        above, below = place + 1 + step, place - 1 - step
+        spot = jnp.int32(width)
+        if "right" in sides:
+            spot = jnp.where(above < width, above, spot)
+        if "left" in sides:
+            spot = jnp.where(below >= 0, below, spot)
+        whole = lax.dynamic_update_index_in_dim(whole, back, spot, 0)
+    whole = whole[:width]
+    if not reduce_first:
+        flat = whole.transpose(1, 0, 2).reshape(rows, width * share)
+        return lax.psum_scatter(flat, "tensor", scatter_dimension=1, tiled=True)
+    few = width // 2
+    mine = lax.dynamic_slice_in_dim(whole, core * few, few, 0)
+    other = swap_halves(lax.dynamic_slice_in_dim(whole, (1 - core) * few, few, 0), "tensor")
+    first = core == 0
+    pair = jnp.stack([jnp.where(first, mine, other), jnp.where(first, other, mine)], axis=1)
+    return pair.transpose(2, 0, 1, 3).reshape(rows, few * 2 * share).astype(jnp.float32)
 
 
 def on_device(
@@ -19,13 +146,7 @@
     down_weight,
 ):
     token_count = attn_out.shape[0]
-    partial_proj = jnp.dot(
-        attn_out,
-        lax.all_gather(out_weight, "expert", axis=1, tiled=True),
-        preferred_element_type=jnp.float32,
-    )
-    branch = lax.psum_scatter(partial_proj, "tensor", scatter_dimension=1, tiled=True)
-    hidden = residual.astype(jnp.float32) + branch
+    hidden = residual.astype(jnp.float32) + project(attn_out, out_weight)
     tensor_count = lax.axis_size("tensor")
     features = tensor_count * hidden.shape[1]
     scaled = hidden * norm_gain.astype(jnp.float32)
@@ -38,6 +159,7 @@
     expert_total = logits.shape[1]
     per_token = routes.shape[1]
     capacity = tensor_count * (token_count * per_token // expert_total // tensor_count + 1)
+    capacity = -(-capacity // 8) * 8
     scores = jax.nn.sigmoid(logits)
     picked = routes[:, :, None] == jnp.arange(expert_total, dtype=jnp.int32)[None, None, :]
     chosen = jnp.sum(jnp.where(picked, scores[:, None, :], 0.0), axis=2)
@@ -66,13 +188,11 @@
         concat_axis=0,
         tiled=True,
     )
-    slot_rows = lax.all_gather(
-        arrived.reshape(expert_total * capacity, -1), "tensor", axis=1, tiled=True
-    )
+    slot_rows = gather_tensor(arrived.reshape(expert_total * capacity, -1))
     gate_part = jnp.dot(slot_rows, gate_weight[0], preferred_element_type=jnp.float32)
     up_part = jnp.dot(slot_rows, up_weight[0], preferred_element_type=jnp.float32)
     activated = (jax.nn.silu(gate_part) * up_part).astype(jnp.bfloat16)
-    whole_units = lax.all_gather(activated, "tensor", axis=1, tiled=True)
+    whole_units = gather_tensor(activated)
     out_rows = jnp.dot(whole_units, down_weight[0], preferred_element_type=jnp.float32).astype(
         jnp.bfloat16
     )

time: 1310 us -> 339 us (0.26)
  waiting for transfers between devices: 1180 us -> 140 us
  starting transfers between devices: 5.77 us -> 80.3 us
    all_gather x3 -> x0, waiting for transfers between devices: 1140 us -> none  [the longest x1 1110 us: on_device(): lax.all_gather(out_weight, 'expert', axis=1, tiled=True)]
    ppermute x0 -> x28, waiting for transfers between devices: none -> 106 us  [the longest x2 46.7 us: pair_columns(): near.append(lax.ppermute(block, 'expert', pair_swap))]
    ppermute x0 -> x28, starting transfers between devices: none -> 73.8 us  [the longest x4 31.1 us: project(): lax.ppermute(product(blocks), 'expert', return_perm(step, width, sides))]
    dot_general x1 -> x10, matrix products: 26.5 us -> 30.3 us  [product(): jnp.dot(block, columns[i * part:(i + 1) * part], preferred_element_type=j...]
  transfers between devices with their start and end apart: 5 -> 29, of which waited for: 5 -> 14; matrix products, arithmetic and copies ran while one was open for 0% -> 13% of each run, Pallas kernels for 0% -> 0%
where the time goes in v1:
time: 339 us; the launch traced here: 333 us
  waiting for transfers between devices  140 us (41%)
  starting transfers between devices  80.3 us (24%)
  matrix products  47.9 us (14%)
  blocking collectives  43.5 us (13%)
  other arithmetic  15.3 us (5%)
  local copies, waits for them, and re-layouts  5.04 us (1%)
    ppermute x2, waiting for transfers between devices, pair_columns(): near.append(lax.ppermute(block, 'expert', pair_swap))  46.7 us
    all_to_all x1, blocking collectives, on_device(): lax.all_to_all(buffer.reshape(expert_total, capacity, -1), 'expert', spli...  41 us
    all_to_all x1, waiting for transfers between devices, on_device(): lax.all_to_all(out_rows.reshape(expert_total, capacity, -1), 'expert', sp...  34.3 us
    ppermute x4, starting transfers between devices, project(): lax.ppermute(product(blocks), 'expert', return_perm(step, width, sides))  31.1 us
    dot_general x10, matrix products, product(): jnp.dot(block, columns[i * part:(i + 1) * part], preferred_element_type=j...  30.3 us
    ppermute x6, waiting for transfers between devices, project(): lax.ppermute(b, 'expert', line_perm(step, False, width))  27.6 us
    ppermute x6, waiting for transfers between devices, project(): up = [lax.ppermute(b, 'expert', line_perm(step, True, width)) for b in up]  20.3 us
    ppermute x6, starting transfers between devices, project(): up = [lax.ppermute(b, 'expert', line_perm(step, True, width)) for b in up]  17.2 us
  transfers between devices with their start and end apart: 29, of which 14 were waited for; matrix products, arithmetic and copies ran while one was open for 13% of the time, Pallas kernels for 0%

profile of v1, /device:TPU:19, one launch (start us, length us, event | category | flops | bytes accessed | tf_op | source)
XLA Modules:
  0.0 332.9 jit_solution(15798136523536586594)
XLA Ops:
  0.0 2.7 constant_dynamic-slice_fusion.4
  3.2 3.2 collective-permute-start.6
  9.8 4.2 %collective-permute-start.5 = (bf16[128,4096]{1,0:T(8,128)(2,1)S(1)}, bf16[128,4096]{1,0:T(8,128)(2,1)}, u32[]{:S(2)}, u32[]{:S(2)}) collective-permute-start(bf16[128,4096]{1,0:T(8,128)(2,1)S(1)} %get-tuple-element.21), channel_id=1, source_target_pairs={{0,4},{2,6},{4,8},{6,10},{8,12},{10,14},{1,5},{3,7},{5,9},{7,11},{... | collective-permute-start | bytes 3145736 | tf_op jit(solution)/shard_map/ppermute | solution.py:88
  14.0 14.9 %collective-permute-done.6 = bf16[128,4096]{1,0:T(8,128)(2,1)S(1)} collective-permute-done((bf16[128,4096]{1,0:T(8,128)(2,1)S(1)}, bf16[128,4096]{1,0:T(8,128)(2,1)S(1)}, u32[]{:S(2)}, u32[]{:S(2)}) %collective-permute-start.6) | collective-permute-done | bytes 1048608 | tf_op jit(solution)/shard_map/ppermute | solution.py:88
  31.8 3.3 %collective-permute-start.15 = (bf16[128,4096]{1,0:T(8,128)(2,1)S(1)}, bf16[128,4096]{1,0:T(8,128)(2,1)S(1)}, u32[]{:S(2)}, u32[]{:S(2)}) collective-permute-start(bf16[128,4096]{1,0:T(8,128)(2,1)S(1)} %collective-permute-done.6), channel_id=1, source_target_pairs={{4,8},{6,10},{8,12},{10,14},{5,9},{7,11},{9,13},{11,15},{20,24},{2... | collective-permute-start | bytes 3145736 | tf_op jit(solution)/shard_map/ppermute | solution.py:88
  35.2 8.6 %collective-permute-done = bf16[2048,448]{0,1:T(8,128)(2,1)} collective-permute-done((bf16[2048,448]{0,1:T(8,128)(2,1)S(1)}, bf16[2048,448]{0,1:T(8,128)(2,1)}, u32[]{:S(2)}, u32[]{:S(2)}) %collective-permute-start) | collective-permute-done | bytes 1835040 | tf_op jit(solution)/shard_map/ppermute | solution.py:39
  45.0 38.1 %collective-permute-done.2 = bf16[2048,448]{0,1:T(8,128)(2,1)S(1)} collective-permute-done((bf16[2048,448]{0,1:T(8,128)(2,1)S(1)}, bf16[2048,448]{0,1:T(8,128)(2,1)S(1)}, u32[]{:S(2)}, u32[]{:S(2)}) %collective-permute-start.2) | collective-permute-done | bytes 1835040 | tf_op jit(solution)/shard_map/ppermute | solution.py:39
  84.3 3.0 collective-permute-start.16
  89.3 5.3 %collective-permute-start.14 = (bf16[128,4096]{1,0:T(8,128)(2,1)}, bf16[128,4096]{1,0:T(8,128)(2,1)}, u32[]{:S(2)}, u32[]{:S(2)}) collective-permute-start(bf16[128,4096]{1,0:T(8,128)(2,1)} %collective-permute-done.9), channel_id=1, source_target_pairs={{4,0},{6,2},{8,4},{10,6},{5,1},{7,3},{9,5},{11,7},{20,16},{22,18},... | collective-permute-start | bytes 3145736 | tf_op jit(solution)/shard_map/ppermute | solution.py:89
  96.7 10.7 %collective-permute-done.16 = bf16[128,4096]{1,0:T(8,128)(2,1)} collective-permute-done((bf16[128,4096]{1,0:T(8,128)(2,1)}, bf16[128,4096]{1,0:T(8,128)(2,1)}, u32[]{:S(2)}, u32[]{:S(2)}) %collective-permute-start.16) | collective-permute-done | bytes 1048608 | tf_op jit(solution)/shard_map/ppermute | solution.py:89
  113.9 16.0 %collective-permute-done.14 = bf16[128,4096]{1,0:T(8,128)(2,1)} collective-permute-done((bf16[128,4096]{1,0:T(8,128)(2,1)}, bf16[128,4096]{1,0:T(8,128)(2,1)}, u32[]{:S(2)}, u32[]{:S(2)}) %collective-permute-start.14) | collective-permute-done | bytes 1048608 | tf_op jit(solution)/shard_map/ppermute | solution.py:89
  137.9 5.6 %broadcast_select_fusion.1 = (bf16[8192,448]{0,1:T(8,128)(2,1)S(1)}, bf16[8192,448]{0,1:T(8,128)(2,1)S(1)}) fusion(bf16[8192,448]{0,1:T(8,128)(2,1)} %param.10, pred[]{:T(512)S(6)} %eq.61, bf16[2048,448]{0,1:T(8,128)(2,1)S(1)} %get-tuple-element.18, bf16[2048,448]{0,1:T(8,128)(2,1)S(1)} %get-tuple-element.16, bf16[2048,448]{0,1:T(8,128)(2,1)S(1)} %get-tuple-element.17, ...), kind=kLoop, calls=%fused_computation.12 | loop fusion | flops 36700160 | bytes 29360128 | tf_op jit(solution)/shard_map/jit(_where)/select_n | solution.py:49
  143.6 3.1 fusion
  148.8 3.7 %fusion.14 = f32[128,896]{1,0:T(8,128)S(1)} fusion(bf16[4096,896]{0,1:T(8,128)(2,1)S(1)} %get-tuple-element.10, bf16[128,4096]{1,0:T(8,128)(2,1)} %collective-permute-done.21, bf16[128,4096]{1,0:T(8,128)(2,1)} %collective-permute-done.22, pred[]{:T(512)S(6)} %ge.18), kind=kOutput, calls=%fused_computation.33 | convolution fusion | flops 940048384 | bytes 9895937 | tf_op jit(solution)/shard_map/dot_general | solution.py:100
  152.5 2.8 collective-permute-done.19
  155.3 3.7 %convolution_add_fusion.1 = f32[128,896]{1,0:T(8,128)S(1)} fusion(f32[128,896]{1,0:T(8,128)S(1)} %fusion.14, bf16[4096,896]{0,1:T(8,128)(2,1)S(1)} %get-tuple-element.9, bf16[128,4096]{1,0:T(8,128)(2,1)} %collective-permute-done.19, bf16[128,4096]{1,0:T(8,128)(2,1)} %collective-permute-done.20, pred[]{:T(512)S(6)} %ge.18), kind=kOutput, calls=%fused_computation.28 | convolution fusion | flops 940163072 | bytes 10354689 | tf_op jit(solution)/shard_map/dot_general | solution.py:100
  159.1 2.7 collective-permute-start.23
  164.3 3.7 %convolution_add_fusion.2 = f32[128,896]{1,0:T(8,128)S(1)} fusion(f32[128,896]{1,0:T(8,128)S(1)} %fusion.17, bf16[4096,896]{0,1:T(8,128)(2,1)S(1)} %get-tuple-element.9, bf16[128,4096]{1,0:T(8,128)(2,1)} %collective-permute-done.13, bf16[128,4096]{1,0:T(8,128)(2,1)} %collective-permute-done.14, pred[]{:T(512)S(6)} %ge.16), kind=kOutput, calls=%fused_computation.29 | convolution fusion | flops 940163072 | bytes 10354689 | tf_op jit(solution)/shard_map/dot_general | solution.py:100
  168.3 3.3 %fusion.48 = f32[896,128]{1,0:T(8,128)S(1)} fusion(bf16[4096,896]{0,1:T(8,128)(2,1)S(1)} %get-tuple-element.10, bf16[128,4096]{1,0:T(8,128)(2,1)} %collective-permute-done.10), kind=kOutput, calls=%fused_computation.103 | convolution fusion | flops 939524096 | bytes 8847360 | tf_op jit(solution)/shard_map/dot_general | solution.py:100
  171.6 3.7 %convolution_add_fusion.3 = f32[896,128]{1,0:T(8,128)S(1)} fusion(f32[896,128]{1,0:T(8,128)S(1)} %fusion.48, bf16[4096,896]{0,1:T(8,128)(2,1)S(1)} %get-tuple-element.9, bf16[128,4096]{1,0:T(8,128)(2,1)} %collective-permute-done.9), kind=kOutput, calls=%fused_computation.30 | convolution fusion | flops 939638784 | bytes 9306112 | tf_op jit(solution)/shard_map/dot_general | solution.py:100
  178.0 3.5 %convolution_add_fusion.4 = f32[896,128]{1,0:T(8,128)S(1)} fusion(f32[896,128]{1,0:T(8,128)S(1)} %fusion.47, bf16[4096,896]{0,1:T(8,128)(2,1)S(1)} %get-tuple-element.9, bf16[128,4096]{1,0:T(8,128)(2,1)} %collective-permute-done.5), kind=kOutput, calls=%fused_computation.31 | convolution fusion | flops 939638784 | bytes 9306112 | tf_op jit(solution)/shard_map/dot_general | solution.py:100
  185.3 24.2 %collective-permute-start.18 = (bf16[128,448]{1,0:T(8,128)(2,1)S(1)}, bf16[128,448]{1,0:T(8,128)(2,1)S(1)}, u32[]{:S(2)}, u32[]{:S(2)}) collective-permute-start(bf16[128,448]{1,0:T(8,128)(2,1)S(1)} %add_convert_fusion.1), channel_id=1, source_target_pairs={{0,8},{2,10},{4,12},{6,14},{8,0},{10,2},{12,4},{14,6},{1,9},{3,11}... | collective-permute-start | bytes 344072 | tf_op jit(solution)/shard_map/ppermute | solution.py:117
  209.5 3.1 collective-permute-start.12
  212.7 3.1 collective-permute-start.8
  215.9 4.5 %collective-permute-done.8 = bf16[128,448]{0,1:T(8,128)(2,1)S(1)} collective-permute-done((bf16[128,448]{0,1:T(8,128)(2,1)S(1)}, bf16[128,448]{0,1:T(8,128)(2,1)S(1)}, u32[]{:S(2)}, u32[]{:S(2)}) %collective-permute-start.8) | collective-permute-done | bytes 114720 | tf_op jit(solution)/shard_map/ppermute | solution.py:117
  227.8 41.0 %all_to_all.10 = bf16[8,56,1792]{2,1,0:T(8,128)(2,1)S(1)} all-to-all(bf16[8,56,1792]{2,1,0:T(8,128)(2,1)S(1)} %bitcast.87), channel_id=1, replica_groups=mesh['groups'=2,'expert'=8,'tensor'=2] {'expert'}, dimensions={0} | all-to-all | bytes 3211264 | tf_op jit(solution)/shard_map/all_to_all | solution.py:184
  269.5 3.1 collective-permute-done.26
  273.1 6.0 %fusion.5 = f32[448,1024]{1,0:T(8,128)S(1)} fusion(bf16[1,3584,1024]{2,1,0:T(8,128)(2,1)} %param.15, bf16[448,1792]{1,0:T(8,128)(2,1)S(1)} %get-tuple-element.20, bf16[448,1792]{1,0:T(8,128)(2,1)S(1)} %get-tuple-element.19), kind=kOutput, calls=%fused_computation.9 | convolution fusion | flops 3294756864 | bytes 12386304 | tf_op jit(solution)/shard_map/dot_general | solution.py:192
  279.2 3.6 %multiply_convert_fusion = bf16[448,1024]{1,0:T(8,128)(2,1)S(1)} fusion(f32[448,1024]{1,0:T(8,128)S(1)} %fusion.5, bf16[1,3584,1024]{2,1,0:T(8,128)(2,1)S(1)} %bitcast.94, bf16[448,1792]{1,0:T(8,128)(2,1)S(1)} %get-tuple-element.20, bf16[448,1792]{1,0:T(8,128)(2,1)S(1)} %get-tuple-element.19), kind=kOutput, calls=%fused_computation.21 | convolution fusion | flops 3297509376 | bytes 13303808 | tf_op jit(solution)/shard_map/dot_general | solution.py:193
  285.5 4.7 %fusion.7 = bf16[448,1792]{1,0:T(8,128)(2,1)} fusion(bf16[1,2048,1792]{2,1,0:T(8,128)(2,1)S(1)} %bitcast.96, bf16[448,1024]{1,0:T(8,128)(2,1)S(1)} %get-tuple-element.24, bf16[448,1024]{1,0:T(8,128)(2,1)S(1)} %get-tuple-element.23), kind=kOutput, calls=%fused_computation.14 | convolution fusion | flops 3292807168 | bytes 10780672 | tf_op jit(solution)/shard_map/dot_general | solution.py:196
  290.2 6.5 %all-to-all-start.1 = ((bf16[8,56,1792]{2,1,0:T(8,128)(2,1)}), bf16[8,56,1792]{2,1,0:T(8,128)(2,1)S(1)}, u32[]{:S(2)}, u32[]{:S(2)}) async-start(bf16[8,56,1792]{2,1,0:T(8,128)(2,1)} %bitcast.89), calls=%async_computation.1 | async-start | bytes 3211264 | tf_op jit(solution)/shard_map/all_to_all | solution.py:199
  296.8 34.3 %all-to-all-done.1 = bf16[8,56,1792]{2,1,0:T(8,128)(2,1)S(1)} async-done(((bf16[8,56,1792]{2,1,0:T(8,128)(2,1)}), bf16[8,56,1792]{2,1,0:T(8,128)(2,1)S(1)}, u32[]{:S(2)}, u32[]{:S(2)}) %all-to-all-start.1) | async-done | bytes 1605664 | tf_op jit(solution)/shard_map/all_to_all | solution.py:199
  (121 shorter events, 52.2 us)
Async XLA Ops:
  0.0 223.8 %copy-start = (f32[1792,8]{0,1:T(8,128)S(1)}, f32[1792,8]{0,1:T(8,128)}, u32[]{:S(2)}) copy-start(f32[1792,8]{0,1:T(8,128)} %param.13) | copy-start | bytes 172036
  0.0 94.7 %copy-start.5 = (s32[128,3]{0,1:T(4,128)S(1)}, s32[128,3]{0,1:T(4,128)}, u32[]{:S(2)}) copy-start(s32[128,3]{0,1:T(4,128)} %param.14) | copy-start | bytes 4612
  2.7 41.1 %collective-permute-start = (bf16[2048,448]{0,1:T(8,128)(2,1)S(1)}, bf16[2048,448]{0,1:T(8,128)(2,1)}, u32[]{:S(2)}, u32[]{:S(2)}) collective-permute-start(bf16[2048,448]{0,1:T(8,128)(2,1)S(1)} %get-tuple-element.13), channel_id=1, source_target_pairs={{0,2},{2,0},{4,6},{6,4},{8,10},{10,8},{12,14},{14,12},{1,3},{3,1},... | collective-permute-start | bytes 5505032 | tf_op jit(solution)/shard_map/ppermute | solution.py:39
  3.2 25.7 %collective-permute-start.6 = (bf16[128,4096]{1,0:T(8,128)(2,1)S(1)}, bf16[128,4096]{1,0:T(8,128)(2,1)S(1)}, u32[]{:S(2)}, u32[]{:S(2)}) collective-permute-start(bf16[128,4096]{1,0:T(8,128)(2,1)S(1)} %get-tuple-element.22), channel_id=1, source_target_pairs={{0,4},{2,6},{4,8},{6,10},{8,12},{10,14},{1,5},{3,7},{5,9},{7,11},{... | collective-permute-start | bytes 3145736 | tf_op jit(solution)/shard_map/ppermute | solution.py:88
  6.4 25.4 %collective-permute-start.10 = (bf16[128,4096]{1,0:T(8,128)(2,1)S(1)}, bf16[128,4096]{1,0:T(8,128)(2,1)}, u32[]{:S(2)}, u32[]{:S(2)}) collective-permute-start(bf16[128,4096]{1,0:T(8,128)(2,1)S(1)} %get-tuple-element.22), channel_id=1, source_target_pairs={{4,0},{6,2},{8,4},{10,6},{12,8},{14,10},{5,1},{7,3},{9,5},{11,7},{... | collective-permute-start | bytes 3145736 | tf_op jit(solution)/shard_map/ppermute | solution.py:89
  8.5 74.6 %collective-permute-start.2 = (bf16[2048,448]{0,1:T(8,128)(2,1)S(1)}, bf16[2048,448]{0,1:T(8,128)(2,1)S(1)}, u32[]{:S(2)}, u32[]{:S(2)}) collective-permute-start(bf16[2048,448]{0,1:T(8,128)(2,1)S(1)} %get-tuple-element.14), channel_id=1, source_target_pairs={{0,2},{2,0},{4,6},{6,4},{8,10},{10,8},{12,14},{14,12},{1,3},{3,1},... | collective-permute-start | bytes 5505032 | tf_op jit(solution)/shard_map/ppermute | solution.py:39
  9.8 74.6 %collective-permute-start.5 = (bf16[128,4096]{1,0:T(8,128)(2,1)S(1)}, bf16[128,4096]{1,0:T(8,128)(2,1)}, u32[]{:S(2)}, u32[]{:S(2)}) collective-permute-start(bf16[128,4096]{1,0:T(8,128)(2,1)S(1)} %get-tuple-element.21), channel_id=1, source_target_pairs={{0,4},{2,6},{4,8},{6,10},{8,12},{10,14},{1,5},{3,7},{5,9},{7,11},{... | collective-permute-start | bytes 3145736 | tf_op jit(solution)/shard_map/ppermute | solution.py:88
  28.9 60.4 %copy-start.7 = (bf16[128,4096]{1,0:T(8,128)(2,1)}, bf16[128,4096]{1,0:T(8,128)(2,1)S(1)}, u32[]{:S(2)}) copy-start(bf16[128,4096]{1,0:T(8,128)(2,1)S(1)} %collective-permute-done.6) | copy-start | bytes 3145732
  28.9 58.5 %collective-permute-start.9 = (bf16[128,4096]{1,0:T(8,128)(2,1)S(1)}, bf16[128,4096]{1,0:T(8,128)(2,1)}, u32[]{:S(2)}, u32[]{:S(2)}) collective-permute-start(bf16[128,4096]{1,0:T(8,128)(2,1)S(1)} %get-tuple-element.21), channel_id=1, source_target_pairs={{4,0},{6,2},{8,4},{10,6},{12,8},{14,10},{5,1},{7,3},{9,5},{11,7},{... | collective-permute-start | bytes 3145736 | tf_op jit(solution)/shard_map/ppermute | solution.py:89
  31.8 57.5 %collective-permute-start.15 = (bf16[128,4096]{1,0:T(8,128)(2,1)S(1)}, bf16[128,4096]{1,0:T(8,128)(2,1)S(1)}, u32[]{:S(2)}, u32[]{:S(2)}) collective-permute-start(bf16[128,4096]{1,0:T(8,128)(2,1)S(1)} %collective-permute-done.6), channel_id=1, source_target_pairs={{4,8},{6,10},{8,12},{10,14},{5,9},{7,11},{9,13},{11,15},{20,24},{2... | collective-permute-start | bytes 3145736 | tf_op jit(solution)/shard_map/ppermute | solution.py:88
  43.8 88.4 %collective-permute-start.1 = (bf16[2048,448]{0,1:T(8,128)(2,1)}, bf16[2048,448]{0,1:T(8,128)(2,1)}, u32[]{:S(2)}, u32[]{:S(2)}) collective-permute-start(bf16[2048,448]{0,1:T(8,128)(2,1)} %collective-permute-done), channel_id=1, source_target_pairs={{0,16},{16,0},{1,17},{17,1},{2,18},{18,2},{3,19},{19,3},{4,20},{20... | collective-permute-start | bytes 5505032 | tf_op jit(solution)/shard_map/ppermute | solution.py:12
  83.1 53.1 %collective-permute-start.3 = (bf16[2048,448]{0,1:T(8,128)(2,1)S(1)}, bf16[2048,448]{0,1:T(8,128)(2,1)}, u32[]{:S(2)}, u32[]{:S(2)}) collective-permute-start(bf16[2048,448]{0,1:T(8,128)(2,1)S(1)} %collective-permute-done.2), channel_id=1, source_target_pairs={{0,16},{16,0},{1,17},{17,1},{2,18},{18,2},{3,19},{19,3},{4,20},{20... | collective-permute-start | bytes 5505032 | tf_op jit(solution)/shard_map/ppermute | solution.py:12
  84.3 23.1 %collective-permute-start.16 = (bf16[128,4096]{1,0:T(8,128)(2,1)}, bf16[128,4096]{1,0:T(8,128)(2,1)}, u32[]{:S(2)}, u32[]{:S(2)}) collective-permute-start(bf16[128,4096]{1,0:T(8,128)(2,1)} %collective-permute-done.10), channel_id=1, source_target_pairs={{4,0},{6,2},{8,4},{10,6},{5,1},{7,3},{9,5},{11,7},{20,16},{22,18},... | collective-permute-start | bytes 3145736 | tf_op jit(solution)/shard_map/ppermute | solution.py:89
  87.4 24.9 %collective-permute-start.13 = (bf16[128,4096]{1,0:T(8,128)(2,1)}, bf16[128,4096]{1,0:T(8,128)(2,1)}, u32[]{:S(2)}, u32[]{:S(2)}) collective-permute-start(bf16[128,4096]{1,0:T(8,128)(2,1)} %collective-permute-done.5), channel_id=1, source_target_pairs={{4,8},{6,10},{8,12},{10,14},{5,9},{7,11},{9,13},{11,15},{20,24},{2... | collective-permute-start | bytes 3145736 | tf_op jit(solution)/shard_map/ppermute | solution.py:88
  89.3 40.6 %collective-permute-start.14 = (bf16[128,4096]{1,0:T(8,128)(2,1)}, bf16[128,4096]{1,0:T(8,128)(2,1)}, u32[]{:S(2)}, u32[]{:S(2)}) collective-permute-start(bf16[128,4096]{1,0:T(8,128)(2,1)} %collective-permute-done.9), channel_id=1, source_target_pairs={{4,0},{6,2},{8,4},{10,6},{5,1},{7,3},{9,5},{11,7},{20,16},{22,18},... | collective-permute-start | bytes 3145736 | tf_op jit(solution)/shard_map/ppermute | solution.py:89
  107.4 41.4 %collective-permute-start.21 = (bf16[128,4096]{1,0:T(8,128)(2,1)S(1)}, bf16[128,4096]{1,0:T(8,128)(2,1)}, u32[]{:S(2)}, u32[]{:S(2)}) collective-permute-start(bf16[128,4096]{1,0:T(8,128)(2,1)S(1)} %collective-permute-done.15), channel_id=1, source_target_pairs={{8,12},{10,14},{9,13},{11,15},{24,28},{26,30},{25,29},{27,31}} | collective-permute-start | bytes 3145736 | tf_op jit(solution)/shard_map/ppermute | solution.py:88
  112.2 36.6 %collective-permute-start.22 = (bf16[128,4096]{1,0:T(8,128)(2,1)}, bf16[128,4096]{1,0:T(8,128)(2,1)}, u32[]{:S(2)}, u32[]{:S(2)}) collective-permute-start(bf16[128,4096]{1,0:T(8,128)(2,1)} %collective-permute-done.16), channel_id=1, source_target_pairs={{4,0},{6,2},{5,1},{7,3},{20,16},{22,18},{21,17},{23,19}} | collective-permute-start | bytes 3145736 | tf_op jit(solution)/shard_map/ppermute | solution.py:89
  129.9 25.4 %collective-permute-start.19 = (bf16[128,4096]{1,0:T(8,128)(2,1)}, bf16[128,4096]{1,0:T(8,128)(2,1)}, u32[]{:S(2)}, u32[]{:S(2)}) collective-permute-start(bf16[128,4096]{1,0:T(8,128)(2,1)} %collective-permute-done.13), channel_id=1, source_target_pairs={{8,12},{10,14},{9,13},{11,15},{24,28},{26,30},{25,29},{27,31}} | collective-permute-start | bytes 3145736 | tf_op jit(solution)/shard_map/ppermute | solution.py:88
  132.2 23.1 %collective-permute-start.20 = (bf16[128,4096]{1,0:T(8,128)(2,1)}, bf16[128,4096]{1,0:T(8,128)(2,1)}, u32[]{:S(2)}, u32[]{:S(2)}) collective-permute-start(bf16[128,4096]{1,0:T(8,128)(2,1)} %collective-permute-done.14), channel_id=1, source_target_pairs={{4,0},{6,2},{5,1},{7,3},{20,16},{22,18},{21,17},{23,19}} | collective-permute-start | bytes 3145736 | tf_op jit(solution)/shard_map/ppermute | solution.py:89
  159.1 25.2 %collective-permute-start.23 = (f32[128,448]{1,0:T(8,128)S(1)}, f32[128,448]{1,0:T(8,128)S(1)}, u32[]{:S(2)}, u32[]{:S(2)}) collective-permute-start(f32[128,448]{1,0:T(8,128)S(1)} %constant_dynamic-slice_fusion.1), channel_id=1, source_target_pairs={{0,1},{1,0},{2,3},{3,2},{4,5},{5,4},{6,7},{7,6},{8,9},{9,8},{10,11... | collective-permute-start | bytes 688136 | tf_op jit(solution)/shard_map/ppermute | solution.py:12
  168.2 16.9 %collective-permute-start.17 = (f32[128,448]{1,0:T(8,128)S(1)}, f32[128,448]{1,0:T(8,128)S(1)}, u32[]{:S(2)}, u32[]{:S(2)}) collective-permute-start(f32[128,448]{1,0:T(8,128)S(1)} %constant_dynamic-slice_fusion.2), channel_id=1, source_target_pairs={{0,1},{1,0},{2,3},{3,2},{4,5},{5,4},{6,7},{7,6},{8,9},{9,8},{10,11... | collective-permute-start | bytes 688136 | tf_op jit(solution)/shard_map/ppermute | solution.py:12
  175.3 34.2 %collective-permute-start.11 = (f32[128,448]{0,1:T(8,128)S(1)}, f32[128,448]{0,1:T(8,128)S(1)}, u32[]{:S(2)}, u32[]{:S(2)}) collective-permute-start(f32[128,448]{0,1:T(8,128)S(1)} %dynamic-slice_bitcast_fusion), channel_id=1, source_target_pairs={{0,1},{1,0},{2,3},{3,2},{4,5},{5,4},{6,7},{7,6},{8,9},{9,8},{10,11... | collective-permute-start | bytes 688136 | tf_op jit(solution)/shard_map/ppermute | solution.py:12
  181.5 31.1 %collective-permute-start.7 = (f32[128,448]{0,1:T(8,128)S(1)}, f32[128,448]{0,1:T(8,128)S(1)}, u32[]{:S(2)}, u32[]{:S(2)}) collective-permute-start(f32[128,448]{0,1:T(8,128)S(1)} %dynamic-slice_bitcast_fusion.1), channel_id=1, source_target_pairs={{0,1},{1,0},{2,3},{3,2},{4,5},{5,4},{6,7},{7,6},{8,9},{9,8},{10,11... | collective-permute-start | bytes 688136 | tf_op jit(solution)/shard_map/ppermute | solution.py:12
  183.8 32.0 %collective-permute-start.4 = (f32[128,448]{0,1:T(8,128)S(1)}, f32[128,448]{0,1:T(8,128)S(1)}, u32[]{:S(2)}, u32[]{:S(2)}) collective-permute-start(f32[128,448]{0,1:T(8,128)S(1)} %dynamic-slice_bitcast_fusion.2), channel_id=1, source_target_pairs={{0,1},{1,0},{2,3},{3,2},{4,5},{5,4},{6,7},{7,6},{8,9},{9,8},{10,11... | collective-permute-start | bytes 688136 | tf_op jit(solution)/shard_map/ppermute | solution.py:12
  184.4 36.0 %collective-permute-start.24 = (bf16[128,448]{1,0:T(8,128)(2,1)S(1)}, bf16[128,448]{1,0:T(8,128)(2,1)S(1)}, u32[]{:S(2)}, u32[]{:S(2)}) collective-permute-start(bf16[128,448]{1,0:T(8,128)(2,1)S(1)} %add_convert_fusion), channel_id=1, source_target_pairs={{0,12},{2,14},{12,0},{14,2},{1,13},{3,15},{13,1},{15,3},{16,28},{1... | collective-permute-start | bytes 344072 | tf_op jit(solution)/shard_map/ppermute | solution.py:117
  185.3 35.3 %collective-permute-start.18 = (bf16[128,448]{1,0:T(8,128)(2,1)S(1)}, bf16[128,448]{1,0:T(8,128)(2,1)S(1)}, u32[]{:S(2)}, u32[]{:S(2)}) collective-permute-start(bf16[128,448]{1,0:T(8,128)(2,1)S(1)} %add_convert_fusion.1), channel_id=1, source_target_pairs={{0,8},{2,10},{4,12},{6,14},{8,0},{10,2},{12,4},{14,6},{1,9},{3,11}... | collective-permute-start | bytes 344072 | tf_op jit(solution)/shard_map/ppermute | solution.py:117
  209.5 11.8 %collective-permute-start.12 = (bf16[128,448]{0,1:T(8,128)(2,1)S(1)}, bf16[128,448]{0,1:T(8,128)(2,1)S(1)}, u32[]{:S(2)}, u32[]{:S(2)}) collective-permute-start(bf16[128,448]{0,1:T(8,128)(2,1)S(1)} %fusion.30), channel_id=1, source_target_pairs={{0,4},{2,6},{4,8},{6,10},{8,12},{10,14},{1,5},{3,7},{5,9},{7,11},{... | collective-permute-start | bytes 344072 | tf_op jit(solution)/shard_map/ppermute | solution.py:117
  212.7 7.8 %collective-permute-start.8 = (bf16[128,448]{0,1:T(8,128)(2,1)S(1)}, bf16[128,448]{0,1:T(8,128)(2,1)S(1)}, u32[]{:S(2)}, u32[]{:S(2)}) collective-permute-start(bf16[128,448]{0,1:T(8,128)(2,1)S(1)} %fusion.31), channel_id=1, source_target_pairs={{4,0},{6,2},{8,4},{10,6},{12,8},{14,10},{5,1},{7,3},{9,5},{11,7},{... | collective-permute-start | bytes 344072 | tf_op jit(solution)/shard_map/ppermute | solution.py:117
  221.5 1.7 collective-permute-start.25
  268.8 3.8 %collective-permute-start.26 = (bf16[448,1792]{1,0:T(8,128)(2,1)S(1)}, bf16[448,1792]{1,0:T(8,128)(2,1)S(1)}, u32[]{:S(2)}, u32[]{:S(2)}) collective-permute-start(bf16[448,1792]{1,0:T(8,128)(2,1)S(1)} %bitcast.86), channel_id=1, source_target_pairs={{0,1},{1,0},{2,3},{3,2},{4,5},{5,4},{6,7},{7,6},{8,9},{9,8},{10,11... | collective-permute-start | bytes 4816904 | tf_op jit(solution)/shard_map/ppermute | solution.py:12
  282.8 2.5 collective-permute-start.27
  290.2 40.9 %all-to-all-start.1 = ((bf16[8,56,1792]{2,1,0:T(8,128)(2,1)}), bf16[8,56,1792]{2,1,0:T(8,128)(2,1)S(1)}, u32[]{:S(2)}, u32[]{:S(2)}) async-start(bf16[8,56,1792]{2,1,0:T(8,128)(2,1)} %bitcast.89), calls=%async_computation.1 | async-start | bytes 3211264 | tf_op jit(solution)/shard_map/all_to_all | solution.py:199
  (10 other events, 123.5 us)

commit v2 on v1

--- a/solution.py
+++ b/solution.py
@@ -134,6 +134,107 @@
     return pair.transpose(2, 0, 1, 3).reshape(rows, few * 2 * share).astype(jnp.float32)
 
 
+def chip_pairs(moves):
+    return [(2 * a + lo, 2 * b + lo) for a, b in moves for lo in range(2)]
+
+
+def core_pairs(moves):
+    return [
+        (2 * (2 * a + lo) + a // 2, 2 * (2 * b + lo) + a // 2)
+        for a, b in moves
+        for lo in range(2)
+    ]
+
+
+SWAP = ((0, 1), (1, 0), (2, 3), (3, 2))
+CROSS = ((1, 2), (2, 1))
+OUTWARD = ((1, 0), (2, 3))
+
+
+def project_line(attn_out, out_weight):
+    place = lax.axis_index("expert") // 2
+    even = lax.axis_index("expert") % 2 == 0
+    group, core = lax.axis_index("groups"), lax.axis_index("tensor")
+    rows, depth = attn_out.shape
+    half = depth // 2
+    unit = half // 32
+    bounds = [0, 9 * unit, 18 * unit, 26 * unit, half]
+    middle = (place == 1) | (place == 2)
+    partner = [(i, i ^ 1) for i in range(8)]
+    to_owner = [(2 * e + 1 - e // 4, 2 * e + e // 4) for e in range(8)]
+
+    def hop(block, moves):
+        return lax.ppermute(block, "expert", chip_pairs(moves))
+
+    def after(block, other):
+        return lax.optimization_barrier((block, other))[0]
+
+    def over_cores(sums):
+        return sums + lax.ppermute(sums, ("expert", "tensor"), to_owner)
+
+    def give_back(block, moves):
+        return lax.ppermute(block, ("expert", "tensor"), core_pairs(moves))
+
+    pieces = [
+        lax.dynamic_slice_in_dim(out_weight, group * half + lo, hi - lo, 0)
+        for lo, hi in zip(bounds, bounds[1:])
+    ]
+    swap = hop(attn_out, SWAP)
+    cross = hop(attn_out, CROSS)
+    near = [lax.ppermute(p, "expert", partner) for p in pieces[:2]]
+    far = [swap_halves(near[0], "groups")]
+    out_mid = hop(cross, OUTWARD)
+    cross_far = hop(swap, CROSS)
+    near += [lax.ppermute(after(p, swap), "expert", partner) for p in pieces[2:]]
+    far += [swap_halves(after(near[1], swap), "groups"), swap_halves(near[2], "groups")]
+    out_far = hop(cross_far, OUTWARD)
+    far += [swap_halves(after(near[3], cross_far), "groups")]
+
+    lower_half = group == 0
+    passed_rows = jnp.concatenate(
+        [jnp.where(lower_half, n, f) for n, f in zip(near, far)]
+        + [jnp.where(lower_half, f, n) for n, f in zip(near, far)],
+        axis=0,
+    )
+    columns = jnp.concatenate(
+        [jnp.where(even, out_weight, passed_rows), jnp.where(even, passed_rows, out_weight)],
+        axis=1,
+    )
+    blocks = jnp.concatenate(
+        [attn_out, swap, jnp.where(middle, cross, out_mid), cross_far], axis=0
+    )
+    early = over_cores(jnp.dot(blocks, columns, preferred_element_type=jnp.float32))
+    own_sum = early[:rows]
+    swap_sum = give_back(early[rows : 2 * rows], SWAP)
+    third = early[2 * rows : 3 * rows]
+    cross_sum, mid_sum = give_back(third, CROSS), give_back(third, ((0, 2), (3, 1)))
+    cross_far_sum = give_back(early[3 * rows :], ((1, 3), (2, 0)))
+    last = over_cores(jnp.dot(out_far, columns, preferred_element_type=jnp.float32))
+    far_sum = give_back(last.astype(jnp.bfloat16), ((0, 3), (3, 0)))
+    same = core == place // 2
+    inner = jnp.where(
+        same,
+        jnp.where(middle, own_sum, swap_sum),
+        jnp.where(middle, cross_sum, cross_far_sum),
+    )
+    outer = jnp.where(
+        same,
+        jnp.where(middle, swap_sum, own_sum),
+        jnp.where(middle, mid_sum, far_sum.astype(jnp.float32)),
+    )
+    lower = core == 0
+    return jnp.concatenate(
+        [jnp.where(lower, outer, inner), jnp.where(lower, inner, outer)], axis=1
+    )
+
+
+def projected_rows(attn_out, out_weight):
+    sizes = tuple(lax.axis_size(name) for name in ("groups", "expert", "tensor"))
+    if sizes == (2, 8, 2):
+        return project_line(attn_out, out_weight)
+    return project(attn_out, out_weight)
+
+
 def on_device(
     attn_out,
     out_weight,
@@ -146,7 +247,7 @@
     down_weight,
 ):
     token_count = attn_out.shape[0]
-    hidden = residual.astype(jnp.float32) + project(attn_out, out_weight)
+    hidden = residual.astype(jnp.float32) + projected_rows(attn_out, out_weight)
     tensor_count = lax.axis_size("tensor")
     features = tensor_count * hidden.shape[1]
     scaled = hidden * norm_gain.astype(jnp.float32)

time: 339 us -> 301 us (0.89)
  starting transfers between devices: 80.3 us -> 41.3 us
  matrix products: 47.9 us -> 41.5 us
  local copies, waits for them, and re-layouts: 5.04 us -> 9.02 us
    ppermute x18 -> x16, starting transfers between devices: 65.6 us -> 29.7 us  [the longest x5 13.2 us: give_back(): return lax.ppermute(block, ('expert', 'tensor'), core_pairs(moves))]
    ppermute x18 -> x16, waiting for transfers between devices: 99.7 us -> 67.9 us  [the longest x5 22.5 us: hop(): return lax.ppermute(block, 'expert', chip_pairs(moves))]
    ppermute x10 -> x6, waiting for transfers between devices: 6.23 us -> 36.7 us  [swap_halves(): return lax.ppermute(array, axis_name, [(0, 1), (1, 0)])]
    dot_general x10 -> x2, matrix products: 30.3 us -> 23.2 us  [the longest x1 14.2 us: project_line(): jnp.dot(blocks, columns, preferred_element_type=jnp.float32)]
    unnamed x2 -> x10, other arithmetic: 0.01 us -> 4.75 us
    select_n x3 -> x4, other arithmetic: 9.68 us -> 5.31 us  [the longest x1 1.96 us: project_line(): jnp.where(middle, cross, out_mid)]
    ppermute x10 -> x6, starting transfers between devices: 8.21 us -> 5.13 us  [swap_halves(): return lax.ppermute(array, axis_name, [(0, 1), (1, 0)])]
  transfers between devices with their start and end apart: 29 -> 23, of which waited for: 14 -> 13; matrix products, arithmetic and copies ran while one was open for 13% -> 16% of each run, Pallas kernels for 0% -> 0%
where the time goes in v2:
time: 301 us; the launch traced here: 295 us
  waiting for transfers between devices  139 us (46%)
  blocking collectives  45.9 us (15%)
  matrix products  41.5 us (14%)
  starting transfers between devices  41.3 us (14%)
  other arithmetic  17.8 us (6%)
  local copies, waits for them, and re-layouts  9.02 us (3%)
    all_to_all x1, blocking collectives, on_device(): lax.all_to_all(buffer.reshape(expert_total, capacity, -1), 'expert', spli...  43.4 us
    ppermute x6, waiting for transfers between devices, swap_halves(): return lax.ppermute(array, axis_name, [(0, 1), (1, 0)])  36.7 us
    all_to_all x1, waiting for transfers between devices, on_device(): lax.all_to_all(out_rows.reshape(expert_total, capacity, -1), 'expert', sp...  34.3 us
    ppermute x5, waiting for transfers between devices, hop(): return lax.ppermute(block, 'expert', chip_pairs(moves))  22.5 us
    ppermute x2, waiting for transfers between devices, project_line(): near = [lax.ppermute(p, 'expert', partner) for p in pieces[:2]]  22 us
    ppermute x2, waiting for transfers between devices, project_line(): lax.ppermute(after(p, swap), 'expert', partner)  15.2 us
    dot_general x1, matrix products, project_line(): jnp.dot(blocks, columns, preferred_element_type=jnp.float32)  14.2 us
    ppermute x5, starting transfers between devices, give_back(): return lax.ppermute(block, ('expert', 'tensor'), core_pairs(moves))  13.2 us
  transfers between devices with their start and end apart: 23, of which 13 were waited for; matrix products, arithmetic and copies ran while one was open for 16% of the time, Pallas kernels for 0%

profile of v2, /device:TPU:19, one launch (start us, length us, event | category | flops | bytes accessed | tf_op | source)
XLA Modules:
  0.0 294.9 jit_solution(5282244013526931163)
XLA Ops:
  1.3 1.9 collective-permute-start.1
  3.2 2.7 constant_dynamic-slice_fusion.2
  7.4 22.0 %collective-permute-done.4 = bf16[1152,448]{0,1:T(8,128)(2,1)S(1)} collective-permute-done((bf16[1152,448]{0,1:T(8,128)(2,1)S(1)}, bf16[1152,448]{0,1:T(8,128)(2,1)S(1)}, u32[]{:S(2)}, u32[]{:S(2)}) %collective-permute-start.4) | collective-permute-done | bytes 1032224 | tf_op jit(solution)/shard_map/ppermute | solution.py:184
  30.6 2.2 constant_dynamic-slice_fusion.1
  32.8 14.0 %collective-permute-done = bf16[128,8192]{1,0:T(8,128)(2,1)} collective-permute-done((bf16[128,8192]{1,0:T(8,128)(2,1)}, bf16[128,8192]{1,0:T(8,128)(2,1)}, u32[]{:S(2)}, u32[]{:S(2)}) %collective-permute-start) | collective-permute-done | bytes 2097184 | tf_op jit(solution)/shard_map/ppermute | solution.py:167
  47.1 2.1 collective-permute-start.3
  49.7 3.9 %collective-permute-start.2 = (bf16[128,8192]{1,0:T(8,128)(2,1)}, bf16[128,8192]{1,0:T(8,128)(2,1)}, u32[]{:S(2)}, u32[]{:S(2)}) collective-permute-start(bf16[128,8192]{1,0:T(8,128)(2,1)} %collective-permute-done.1), channel_id=1, source_target_pairs={{4,0},{6,2},{8,12},{10,14},{5,1},{7,3},{9,13},{11,15},{20,16},{22,... | collective-permute-start | bytes 6291464 | tf_op jit(solution)/shard_map/ppermute | solution.py:167
  56.0 15.2 %collective-permute-done.8 = bf16[1024,448]{0,1:T(8,128)(2,1)} collective-permute-done((bf16[1024,448]{0,1:T(8,128)(2,1)}, bf16[1024,448]{0,1:T(8,128)(2,1)}, u32[]{:S(2)}, u32[]{:S(2)}) %collective-permute-start.8) | collective-permute-done | bytes 917536 | tf_op jit(solution)/shard_map/ppermute | solution.py:188
  73.0 2.9 collective-permute-done.7
  76.2 19.3 %collective-permute-done.9 = bf16[1024,448]{0,1:T(8,128)(2,1)S(1)} collective-permute-done((bf16[1024,448]{0,1:T(8,128)(2,1)}, bf16[1024,448]{0,1:T(8,128)(2,1)S(1)}, u32[]{:S(2)}, u32[]{:S(2)}) %collective-permute-start.9) | collective-permute-done | bytes 917536 | tf_op jit(solution)/shard_map/ppermute | solution.py:12
  97.2 2.6 collective-permute-start.15
  99.8 2.0 broadcast_select_fusion.2
  101.8 9.4 %collective-permute-done.11 = bf16[768,448]{0,1:T(8,128)(2,1)S(1)} collective-permute-done((bf16[768,448]{0,1:T(8,128)(2,1)S(1)}, bf16[768,448]{0,1:T(8,128)(2,1)S(1)}, u32[]{:S(2)}, u32[]{:S(2)}) %collective-permute-start.11) | collective-permute-done | bytes 688160 | tf_op jit(solution)/shard_map/ppermute | solution.py:12
  114.0 1.9 broadcast_select_fusion.1
  116.0 14.2 %fusion.1 = f32[512,896]{1,0:T(8,128)} fusion(bf16[8192,448]{0,1:T(8,128)(2,1)S(1)} %get-tuple-element.21, bf16[8192,448]{0,1:T(8,128)(2,1)S(1)} %get-tuple-element.20, bf16[128,8192]{1,0:T(8,128)(2,1)} %collective-permute-done.3, bf16[128,8192]{1,0:T(8,128)(2,1)S(1)} %broadcast_select_fusion.2, bf16[128,8192]{1,0:T(8,128)(2,1)} %collective-permute-done, ...), kind=kOutput, calls=%fused_computation.2 | convolution fusion | flops 7579107328 | bytes 24903680 | tf_op jit(solution)/shard_map/dot_general | solution.py:206
  132.9 7.9 %collective-permute-done.15 = bf16[128,8192]{1,0:T(8,128)(2,1)} collective-permute-done((bf16[128,8192]{1,0:T(8,128)(2,1)}, bf16[128,8192]{1,0:T(8,128)(2,1)}, u32[]{:S(2)}, u32[]{:S(2)}) %collective-permute-start.15) | collective-permute-done | bytes 2097184 | tf_op jit(solution)/shard_map/ppermute | solution.py:167
  140.8 9.0 %fusion.22 = f32[128,896]{1,0:T(8,128)} fusion(bf16[128,8192]{1,0:T(8,128)(2,1)} %collective-permute-done.15, bf16[8192,448]{0,1:T(8,128)(2,1)} %copy-done.3, bf16[8192,448]{0,1:T(8,128)(2,1)} %copy-done.2), kind=kOutput, calls=%fused_computation.30 | convolution fusion | flops 1908408320 | bytes 17235968 | tf_op jit(solution)/shard_map/dot_general | solution.py:212
  151.9 2.3 add.77
  156.0 7.3 %collective-permute-start.18 = (f32[128,896]{1,0:T(8,128)}, f32[128,896]{1,0:T(8,128)S(1)}, u32[]{:S(2)}, u32[]{:S(2)}) collective-permute-start(f32[128,896]{1,0:T(8,128)} %get-tuple-element.29), channel_id=1, source_target_pairs={{4,8},{6,10},{9,5},{11,7},{20,24},{22,26},{25,21},{27,23}} | collective-permute-start | bytes 1376264 | tf_op jit(solution)/shard_map/ppermute | solution.py:176
  163.3 2.5 collective-permute-start.13
  165.8 2.1 collective-permute-start.19
  171.8 2.6 collective-permute-done.13
  175.3 5.6 %collective-permute-done.19 = f32[128,896]{1,0:T(8,128)} collective-permute-done((f32[128,896]{1,0:T(8,128)}, f32[128,896]{1,0:T(8,128)}, u32[]{:S(2)}, u32[]{:S(2)}) %collective-permute-start.19) | collective-permute-done | bytes 458784 | tf_op jit(solution)/shard_map/ppermute | solution.py:176
  183.4 2.5 all-reduce
  187.3 43.4 %all_to_all.10 = bf16[8,56,1792]{2,1,0:T(8,128)(2,1)S(1)} all-to-all(bf16[8,56,1792]{2,1,0:T(8,128)(2,1)S(1)} %bitcast.39), channel_id=1, replica_groups=mesh['groups'=2,'expert'=8,'tensor'=2] {'expert'}, dimensions={0} | all-to-all | bytes 3211264 | tf_op jit(solution)/shard_map/all_to_all | solution.py:285
  231.5 3.1 %collective-permute-done.20 = bf16[448,1792]{1,0:T(8,128)(2,1)S(1)} collective-permute-done((bf16[448,1792]{1,0:T(8,128)(2,1)S(1)}, bf16[448,1792]{1,0:T(8,128)(2,1)S(1)}, u32[]{:S(2)}, u32[]{:S(2)}) %collective-permute-start.20) | collective-permute-done | bytes 1605664 | tf_op jit(solution)/shard_map/ppermute | solution.py:12
  235.1 6.0 %fusion.13 = f32[448,1024]{1,0:T(8,128)S(1)} fusion(bf16[1,3584,1024]{2,1,0:T(8,128)(2,1)} %param.15, bf16[448,1792]{1,0:T(8,128)(2,1)S(1)} %get-tuple-element.25, bf16[448,1792]{1,0:T(8,128)(2,1)S(1)} %get-tuple-element.24), kind=kOutput, calls=%fused_computation.14 | convolution fusion | flops 3294756864 | bytes 12386304 | tf_op jit(solution)/shard_map/dot_general | solution.py:293
  241.2 3.6 %multiply_convert_fusion = bf16[448,1024]{1,0:T(8,128)(2,1)S(1)} fusion(f32[448,1024]{1,0:T(8,128)S(1)} %fusion.13, bf16[1,3584,1024]{2,1,0:T(8,128)(2,1)S(1)} %bitcast.43, bf16[448,1792]{1,0:T(8,128)(2,1)S(1)} %get-tuple-element.25, bf16[448,1792]{1,0:T(8,128)(2,1)S(1)} %get-tuple-element.24), kind=kOutput, calls=%fused_computation.27 | convolution fusion | flops 3297509376 | bytes 13303808 | tf_op jit(solution)/shard_map/dot_general | solution.py:294
  245.2 2.1 collective-permute-done.21
  247.5 4.7 %fusion.15 = bf16[448,1792]{1,0:T(8,128)(2,1)} fusion(bf16[1,2048,1792]{2,1,0:T(8,128)(2,1)S(1)} %bitcast.45, bf16[448,1024]{1,0:T(8,128)(2,1)S(1)} %get-tuple-element.27, bf16[448,1024]{1,0:T(8,128)(2,1)S(1)} %get-tuple-element.26), kind=kOutput, calls=%fused_computation.19 | convolution fusion | flops 3292807168 | bytes 10780672 | tf_op jit(solution)/shard_map/dot_general | solution.py:297
  252.2 6.5 %all-to-all-start.1 = ((bf16[8,56,1792]{2,1,0:T(8,128)(2,1)}), bf16[8,56,1792]{2,1,0:T(8,128)(2,1)S(1)}, u32[]{:S(2)}, u32[]{:S(2)}) async-start(bf16[8,56,1792]{2,1,0:T(8,128)(2,1)} %bitcast.40), calls=%async_computation.1 | async-start | bytes 3211264 | tf_op jit(solution)/shard_map/all_to_all | solution.py:300
  258.8 34.3 %all-to-all-done.1 = bf16[8,56,1792]{2,1,0:T(8,128)(2,1)S(1)} async-done(((bf16[8,56,1792]{2,1,0:T(8,128)(2,1)}), bf16[8,56,1792]{2,1,0:T(8,128)(2,1)S(1)}, u32[]{:S(2)}, u32[]{:S(2)}) %all-to-all-start.1) | async-done | bytes 1605664 | tf_op jit(solution)/shard_map/all_to_all | solution.py:300
  (100 shorter events, 32.8 us)
Async XLA Ops:
  0.0 182.5 %copy-start = (f32[1792,8]{0,1:T(8,128)S(1)}, f32[1792,8]{0,1:T(8,128)}, u32[]{:S(2)}) copy-start(f32[1792,8]{0,1:T(8,128)} %param.13) | copy-start | bytes 172036
  0.0 46.8 %collective-permute-start = (bf16[128,8192]{1,0:T(8,128)(2,1)}, bf16[128,8192]{1,0:T(8,128)(2,1)}, u32[]{:S(2)}, u32[]{:S(2)}) collective-permute-start(bf16[128,8192]{1,0:T(8,128)(2,1)} %param.9), channel_id=1, source_target_pairs={{0,4},{2,6},{4,0},{6,2},{8,12},{10,14},{12,8},{14,10},{1,5},{3,7},... | collective-permute-start | bytes 6291464 | tf_op jit(solution)/shard_map/ppermute | solution.py:167
  1.3 48.4 %collective-permute-start.1 = (bf16[128,8192]{1,0:T(8,128)(2,1)}, bf16[128,8192]{1,0:T(8,128)(2,1)}, u32[]{:S(2)}, u32[]{:S(2)}) collective-permute-start(bf16[128,8192]{1,0:T(8,128)(2,1)} %param.9), channel_id=1, source_target_pairs={{4,8},{6,10},{8,4},{10,6},{5,9},{7,11},{9,5},{11,7},{20,24},{22,26... | collective-permute-start | bytes 6291464 | tf_op jit(solution)/shard_map/ppermute | solution.py:167
  5.9 23.5 %collective-permute-start.4 = (bf16[1152,448]{0,1:T(8,128)(2,1)S(1)}, bf16[1152,448]{0,1:T(8,128)(2,1)S(1)}, u32[]{:S(2)}, u32[]{:S(2)}) collective-permute-start(bf16[1152,448]{0,1:T(8,128)(2,1)S(1)} %get-tuple-element.23), channel_id=1, source_target_pairs={{0,2},{2,0},{4,6},{6,4},{8,10},{10,8},{12,14},{14,12},{1,3},{3,1},... | collective-permute-start | bytes 3096584 | tf_op jit(solution)/shard_map/ppermute | solution.py:184
  6.2 47.4 %collective-permute-start.6 = (bf16[1152,448]{0,1:T(8,128)(2,1)}, bf16[1152,448]{0,1:T(8,128)(2,1)S(1)}, u32[]{:S(2)}, u32[]{:S(2)}) collective-permute-start(bf16[1152,448]{0,1:T(8,128)(2,1)} %get-tuple-element.22), channel_id=1, source_target_pairs={{0,2},{2,0},{4,6},{6,4},{8,10},{10,8},{12,14},{14,12},{1,3},{3,1},... | collective-permute-start | bytes 3096584 | tf_op jit(solution)/shard_map/ppermute | solution.py:184
  29.4 43.0 %collective-permute-start.5 = (bf16[1152,448]{0,1:T(8,128)(2,1)S(1)}, bf16[1152,448]{0,1:T(8,128)(2,1)S(1)}, u32[]{:S(2)}, u32[]{:S(2)}) collective-permute-start(bf16[1152,448]{0,1:T(8,128)(2,1)S(1)} %collective-permute-done.4), channel_id=1, source_target_pairs={{0,16},{16,0},{1,17},{17,1},{2,18},{18,2},{3,19},{19,3},{4,20},{20... | collective-permute-start | bytes 3096584 | tf_op jit(solution)/shard_map/ppermute | solution.py:12
  46.8 24.4 %collective-permute-start.8 = (bf16[1024,448]{0,1:T(8,128)(2,1)}, bf16[1024,448]{0,1:T(8,128)(2,1)}, u32[]{:S(2)}, u32[]{:S(2)}) collective-permute-start(bf16[1024,448]{0,1:T(8,128)(2,1)} %constant_dynamic-slice_fusion.1), channel_id=1, source_target_pairs={{0,2},{2,0},{4,6},{6,4},{8,10},{10,8},{12,14},{14,12},{1,3},{3,1},... | collective-permute-start | bytes 2752520 | tf_op jit(solution)/shard_map/ppermute | solution.py:188
  47.1 50.0 %collective-permute-start.3 = (bf16[128,8192]{1,0:T(8,128)(2,1)}, bf16[128,8192]{1,0:T(8,128)(2,1)}, u32[]{:S(2)}, u32[]{:S(2)}) collective-permute-start(bf16[128,8192]{1,0:T(8,128)(2,1)} %collective-permute-done), channel_id=1, source_target_pairs={{4,8},{6,10},{8,4},{10,6},{5,9},{7,11},{9,5},{11,7},{20,24},{22,26... | collective-permute-start | bytes 6291464 | tf_op jit(solution)/shard_map/ppermute | solution.py:167
  49.7 50.1 %collective-permute-start.2 = (bf16[128,8192]{1,0:T(8,128)(2,1)}, bf16[128,8192]{1,0:T(8,128)(2,1)}, u32[]{:S(2)}, u32[]{:S(2)}) collective-permute-start(bf16[128,8192]{1,0:T(8,128)(2,1)} %collective-permute-done.1), channel_id=1, source_target_pairs={{4,0},{6,2},{8,12},{10,14},{5,1},{7,3},{9,13},{11,15},{20,16},{22,... | collective-permute-start | bytes 6291464 | tf_op jit(solution)/shard_map/ppermute | solution.py:167
  53.6 22.3 %collective-permute-start.7 = (bf16[1152,448]{0,1:T(8,128)(2,1)S(1)}, bf16[1152,448]{0,1:T(8,128)(2,1)}, u32[]{:S(2)}, u32[]{:S(2)}) collective-permute-start(bf16[1152,448]{0,1:T(8,128)(2,1)S(1)} %collective-permute-done.6), channel_id=1, source_target_pairs={{0,16},{16,0},{1,17},{17,1},{2,18},{18,2},{3,19},{19,3},{4,20},{20... | collective-permute-start | bytes 3096584 | tf_op jit(solution)/shard_map/ppermute | solution.py:12
  71.2 24.4 %collective-permute-start.9 = (bf16[1024,448]{0,1:T(8,128)(2,1)}, bf16[1024,448]{0,1:T(8,128)(2,1)S(1)}, u32[]{:S(2)}, u32[]{:S(2)}) collective-permute-start(bf16[1024,448]{0,1:T(8,128)(2,1)} %collective-permute-done.8), channel_id=1, source_target_pairs={{0,16},{16,0},{1,17},{17,1},{2,18},{18,2},{3,19},{19,3},{4,20},{20... | collective-permute-start | bytes 2752520 | tf_op jit(solution)/shard_map/ppermute | solution.py:12
  72.7 24.4 %collective-permute-start.10 = (bf16[768,448]{0,1:T(8,128)(2,1)S(1)}, bf16[768,448]{0,1:T(8,128)(2,1)S(1)}, u32[]{:S(2)}, u32[]{:S(2)}) collective-permute-start(bf16[768,448]{0,1:T(8,128)(2,1)S(1)} %constant_dynamic-slice_fusion), channel_id=1, source_target_pairs={{0,2},{2,0},{4,6},{6,4},{8,10},{10,8},{12,14},{14,12},{1,3},{3,1},... | collective-permute-start | bytes 2064392 | tf_op jit(solution)/shard_map/ppermute | solution.py:188
  97.1 14.1 %collective-permute-start.11 = (bf16[768,448]{0,1:T(8,128)(2,1)S(1)}, bf16[768,448]{0,1:T(8,128)(2,1)S(1)}, u32[]{:S(2)}, u32[]{:S(2)}) collective-permute-start(bf16[768,448]{0,1:T(8,128)(2,1)S(1)} %collective-permute-done.10), channel_id=1, source_target_pairs={{0,16},{16,0},{1,17},{17,1},{2,18},{18,2},{3,19},{19,3},{4,20},{20... | collective-permute-start | bytes 2064392 | tf_op jit(solution)/shard_map/ppermute | solution.py:12
  97.2 43.6 %collective-permute-start.15 = (bf16[128,8192]{1,0:T(8,128)(2,1)}, bf16[128,8192]{1,0:T(8,128)(2,1)}, u32[]{:S(2)}, u32[]{:S(2)}) collective-permute-start(bf16[128,8192]{1,0:T(8,128)(2,1)} %collective-permute-done.3), channel_id=1, source_target_pairs={{4,0},{6,2},{8,12},{10,14},{5,1},{7,3},{9,13},{11,15},{20,16},{22,... | collective-permute-start | bytes 6291464 | tf_op jit(solution)/shard_map/ppermute | solution.py:167
  99.8 14.2 %slice-start = ((s8[7340032]{0:T(1024)(128)(4,1)}), s8[4194304]{0:T(1024)(128)(4,1)S(1)}, s32[]{:S(2)}) async-start(s8[7340032]{0:T(1024)(128)(4,1)} %bitcast.35), calls=%async_computation.2 | async-start | bytes 8388608
  115.9 14.2 %copy-start.2 = (bf16[8192,448]{0,1:T(8,128)(2,1)}, bf16[8192,448]{0,1:T(8,128)(2,1)S(1)}, u32[]{:S(2)}) copy-start(bf16[8192,448]{0,1:T(8,128)(2,1)S(1)} %get-tuple-element.20) | copy-start | bytes 22020100
  115.9 14.2 %copy-start.3 = (bf16[8192,448]{0,1:T(8,128)(2,1)}, bf16[8192,448]{0,1:T(8,128)(2,1)S(1)}, u32[]{:S(2)}) copy-start(bf16[8192,448]{0,1:T(8,128)(2,1)S(1)} %get-tuple-element.21) | copy-start | bytes 22020100
  116.0 15.5 %copy-start.6 = (s32[128,3]{0,1:T(4,128)S(1)}, s32[128,3]{0,1:T(4,128)}, u32[]{:S(2)}) copy-start(s32[128,3]{0,1:T(4,128)} %param.14) | copy-start | bytes 4612
  130.2 21.7 %collective-permute-start.12 = (f32[512,896]{1,0:T(8,128)}, f32[512,896]{1,0:T(8,128)}, u32[]{:S(2)}, u32[]{:S(2)}) collective-permute-start(f32[512,896]{1,0:T(8,128)} %fusion.1), channel_id=1, source_target_pairs={{1,0},{3,2},{5,4},{7,6},{8,9},{10,11},{12,13},{14,15},{17,16},{19,... | collective-permute-start | bytes 5505032 | tf_op jit(solution)/shard_map/ppermute | solution.py:173
  149.8 20.6 %copy-start.7 = (s32[128,3]{0,1:T(4,128)S(1)}, s32[128,3]{0,1:T(4,128)}, u32[]{:S(2)}) copy-start(s32[128,3]{0,1:T(4,128)} %param.14) | copy-start | bytes 4612
  149.8 21.2 %copy-start.10 = (bf16[1792]{0:T(1024)(128)(2,1)S(1)}, bf16[1792]{0:T(1024)(128)(2,1)}, u32[]{:S(2)}) copy-start(bf16[1792]{0:T(1024)(128)(2,1)} %param.12) | copy-start | bytes 10756
  149.8 18.0 %collective-permute-start.16 = (f32[128,896]{1,0:T(8,128)}, f32[128,896]{1,0:T(8,128)}, u32[]{:S(2)}, u32[]{:S(2)}) collective-permute-start(f32[128,896]{1,0:T(8,128)} %fusion.22), channel_id=1, source_target_pairs={{1,0},{3,2},{5,4},{7,6},{8,9},{10,11},{12,13},{14,15},{17,16},{19,... | collective-permute-start | bytes 1376264 | tf_op jit(solution)/shard_map/ppermute | solution.py:173
  151.9 30.4 %copy-start.1 = (bf16[128,1792]{1,0:T(8,128)(2,1)S(1)}, bf16[128,1792]{1,0:T(8,128)(2,1)}, u32[]{:S(2)}) copy-start(bf16[128,1792]{1,0:T(8,128)(2,1)} %param.11) | copy-start | bytes 1376260
  155.3 19.2 %collective-permute-start.14 = (f32[128,896]{1,0:T(8,128)}, f32[128,896]{1,0:T(8,128)S(1)}, u32[]{:S(2)}, u32[]{:S(2)}) collective-permute-start(f32[128,896]{1,0:T(8,128)} %get-tuple-element.29), channel_id=1, source_target_pairs={{0,8},{2,10},{13,5},{15,7},{16,24},{18,26},{29,21},{31,23}} | collective-permute-start | bytes 1376264 | tf_op jit(solution)/shard_map/ppermute | solution.py:176
  156.0 18.5 %collective-permute-start.18 = (f32[128,896]{1,0:T(8,128)}, f32[128,896]{1,0:T(8,128)S(1)}, u32[]{:S(2)}, u32[]{:S(2)}) collective-permute-start(f32[128,896]{1,0:T(8,128)} %get-tuple-element.29), channel_id=1, source_target_pairs={{4,8},{6,10},{9,5},{11,7},{20,24},{22,26},{25,21},{27,23}} | collective-permute-start | bytes 1376264 | tf_op jit(solution)/shard_map/ppermute | solution.py:176
  163.3 11.2 %collective-permute-start.13 = (f32[128,896]{1,0:T(8,128)}, f32[128,896]{1,0:T(8,128)}, u32[]{:S(2)}, u32[]{:S(2)}) collective-permute-start(f32[128,896]{1,0:T(8,128)} %get-tuple-element.30), channel_id=1, source_target_pairs={{0,4},{2,6},{4,0},{6,2},{9,13},{11,15},{13,9},{15,11},{16,20},{18,... | collective-permute-start | bytes 1376264 | tf_op jit(solution)/shard_map/ppermute | solution.py:176
  165.8 15.1 %collective-permute-start.19 = (f32[128,896]{1,0:T(8,128)}, f32[128,896]{1,0:T(8,128)}, u32[]{:S(2)}, u32[]{:S(2)}) collective-permute-start(f32[128,896]{1,0:T(8,128)} %get-tuple-element.28), channel_id=1, source_target_pairs={{4,12},{6,14},{9,1},{11,3},{20,28},{22,30},{25,17},{27,19}} | collective-permute-start | bytes 1376264 | tf_op jit(solution)/shard_map/ppermute | solution.py:176
  169.8 2.1 collective-permute-start.17
  230.7 3.9 %collective-permute-start.20 = (bf16[448,1792]{1,0:T(8,128)(2,1)S(1)}, bf16[448,1792]{1,0:T(8,128)(2,1)S(1)}, u32[]{:S(2)}, u32[]{:S(2)}) collective-permute-start(bf16[448,1792]{1,0:T(8,128)(2,1)S(1)} %bitcast.38), channel_id=1, source_target_pairs={{0,1},{1,0},{2,3},{3,2},{4,5},{5,4},{6,7},{7,6},{8,9},{9,8},{10,11... | collective-permute-start | bytes 4816904 | tf_op jit(solution)/shard_map/ppermute | solution.py:12
  235.1 12.3 %slice-start.4 = ((s8[7340032]{0:T(1024)(128)(4,1)}), s8[4194304]{0:T(1024)(128)(4,1)S(1)}, s32[]{:S(2)}) async-start(s8[7340032]{0:T(1024)(128)(4,1)} %bitcast.44), calls=%async_computation.6 | async-start | bytes 8388608
  244.8 2.5 collective-permute-start.21
  252.2 40.9 %all-to-all-start.1 = ((bf16[8,56,1792]{2,1,0:T(8,128)(2,1)}), bf16[8,56,1792]{2,1,0:T(8,128)(2,1)S(1)}, u32[]{:S(2)}, u32[]{:S(2)}) async-start(bf16[8,56,1792]{2,1,0:T(8,128)(2,1)} %bitcast.40), calls=%async_computation.1 | async-start | bytes 3211264 | tf_op jit(solution)/shard_map/all_to_all | solution.py:300
  (8 other events, 56.2 us)

commit v3 on v2

--- a/solution.py
+++ b/solution.py
@@ -169,8 +169,8 @@
     def after(block, other):
         return lax.optimization_barrier((block, other))[0]
 
-    def over_cores(sums):
-        return sums + lax.ppermute(sums, ("expert", "tensor"), to_owner)
+    def to_owners(sums):
+        return lax.ppermute(sums, ("expert", "tensor"), to_owner)
 
     def give_back(block, moves):
         return lax.ppermute(block, ("expert", "tensor"), core_pairs(moves))
@@ -203,24 +203,31 @@
     blocks = jnp.concatenate(
         [attn_out, swap, jnp.where(middle, cross, out_mid), cross_far], axis=0
     )
-    early = over_cores(jnp.dot(blocks, columns, preferred_element_type=jnp.float32))
-    own_sum = early[:rows]
-    swap_sum = give_back(early[rows : 2 * rows], SWAP)
-    third = early[2 * rows : 3 * rows]
-    cross_sum, mid_sum = give_back(third, CROSS), give_back(third, ((0, 2), (3, 1)))
-    cross_far_sum = give_back(early[3 * rows :], ((1, 3), (2, 0)))
-    last = over_cores(jnp.dot(out_far, columns, preferred_element_type=jnp.float32))
-    far_sum = give_back(last.astype(jnp.bfloat16), ((0, 3), (3, 0)))
+    early = jnp.dot(blocks, columns, preferred_element_type=jnp.float32)
+    third, fourth = early[2 * rows : 3 * rows], early[3 * rows :]
+    early = jnp.concatenate([early[: 2 * rows], jnp.where(middle, fourth, third)], axis=0)
+    early = after(early, out_far)
+    from_core = to_owners(early)
+    own_sum, swap_sum, cross_sum = (
+        early[i * rows : (i + 1) * rows] + from_core[i * rows : (i + 1) * rows]
+        for i in range(3)
+    )
+    swap_sum = give_back(swap_sum, SWAP)
+    cross_sum = give_back(cross_sum, ((0, 2), (3, 1), (1, 3), (2, 0)))
+    last = jnp.dot(out_far, columns, preferred_element_type=jnp.float32)
+    last = jnp.where(middle, third, last)
+    last = (last + to_owners(last)).astype(jnp.bfloat16)
+    last_sum = give_back(last, ((0, 3), (3, 0), (1, 2), (2, 1))).astype(jnp.float32)
     same = core == place // 2
     inner = jnp.where(
         same,
         jnp.where(middle, own_sum, swap_sum),
-        jnp.where(middle, cross_sum, cross_far_sum),
+        jnp.where(middle, last_sum, cross_sum),
     )
     outer = jnp.where(
         same,
         jnp.where(middle, swap_sum, own_sum),
-        jnp.where(middle, mid_sum, far_sum.astype(jnp.float32)),
+        jnp.where(middle, cross_sum, last_sum),
     )
     lower = core == 0
     return jnp.concatenate(
@@ -233,6 +240,12 @@
     if sizes == (2, 8, 2):
         return project_line(attn_out, out_weight)
     return project(attn_out, out_weight)
+
+
+def exchange(rows, expert_total):
+    split = rows.reshape(expert_total, rows.shape[0] // expert_total, -1)
+    moved = lax.all_to_all(split, "expert", split_axis=0, concat_axis=0, tiled=True)
+    return moved.reshape(rows.shape)
 
 
 def on_device(
@@ -253,62 +266,62 @@
     scaled = hidden * norm_gain.astype(jnp.float32)
     squares = jnp.sum(hidden * hidden, axis=1)
     raw_logits = jnp.dot(scaled, router_weight, precision=lax.Precision.HIGHEST)
-    total_squares, total_logits = lax.psum((squares, raw_logits), "tensor")
+    if tensor_count == 2:
+        sums = jnp.concatenate([raw_logits, squares[:, None]], axis=1)
+        sums = sums + swap_halves(sums, "tensor")
+        total_squares, total_logits = sums[:, -1], sums[:, :-1]
+    else:
+        total_squares, total_logits = lax.psum((squares, raw_logits), "tensor")
     inverse_rms = lax.rsqrt(total_squares / features + EPS)
     logits = total_logits * inverse_rms[:, None]
     normed_rows = (scaled * inverse_rms[:, None]).astype(jnp.bfloat16)
     expert_total = logits.shape[1]
     per_token = routes.shape[1]
     capacity = tensor_count * (token_count * per_token // expert_total // tensor_count + 1)
-    capacity = -(-capacity // 8) * 8
     scores = jax.nn.sigmoid(logits)
-    picked = routes[:, :, None] == jnp.arange(expert_total, dtype=jnp.int32)[None, None, :]
+    experts = jnp.arange(expert_total, dtype=jnp.int32)
+    picked = routes[:, :, None] == experts[None, None, :]
     chosen = jnp.sum(jnp.where(picked, scores[:, None, :], 0.0), axis=2)
     gate_values = ROUTE_SCALE * chosen / jnp.sum(chosen, axis=1, keepdims=True)
     flat_hits = picked.reshape(token_count * per_token, expert_total).astype(jnp.int32)
     earlier = jnp.cumsum(flat_hits, axis=0) - flat_hits
-    slot_rank = jnp.sum(earlier * flat_hits, axis=1)
-    target = routes.reshape(-1) * capacity + slot_rank
-    placed = jnp.arange(expert_total * capacity, dtype=jnp.int32)[:, None] == target[None, :]
-    dispatch_matrix = jnp.any(
-        placed.reshape(expert_total * capacity, token_count, per_token), axis=2
-    ).astype(jnp.bfloat16)
-    gate_matrix = jnp.sum(
-        jnp.where(placed, gate_values.reshape(-1)[None, :], 0.0).reshape(
-            expert_total * capacity, token_count, per_token
-        ),
-        axis=2,
-    )
-    buffer = jnp.dot(dispatch_matrix, normed_rows, preferred_element_type=jnp.float32).astype(
-        jnp.bfloat16
-    )
-    arrived = lax.all_to_all(
-        buffer.reshape(expert_total, capacity, -1),
-        "expert",
-        split_axis=0,
-        concat_axis=0,
-        tiled=True,
-    )
-    slot_rows = gather_tensor(arrived.reshape(expert_total * capacity, -1))
-    gate_part = jnp.dot(slot_rows, gate_weight[0], preferred_element_type=jnp.float32)
-    up_part = jnp.dot(slot_rows, up_weight[0], preferred_element_type=jnp.float32)
-    activated = (jax.nn.silu(gate_part) * up_part).astype(jnp.bfloat16)
-    whole_units = gather_tensor(activated)
-    out_rows = jnp.dot(whole_units, down_weight[0], preferred_element_type=jnp.float32).astype(
-        jnp.bfloat16
-    )
-    returned = lax.all_to_all(
-        out_rows.reshape(expert_total, capacity, -1),
-        "expert",
-        split_axis=0,
-        concat_axis=0,
-        tiled=True,
-    )
-    returned_rows = returned.reshape(expert_total * capacity, -1).astype(jnp.float32)
-    expert_sum = jnp.einsum(
-        "st,sd->td", gate_matrix, returned_rows, precision=lax.Precision.HIGHEST
-    )
-    return (hidden + expert_sum).astype(jnp.bfloat16)
+    slot_rank = jnp.sum(earlier * flat_hits, axis=1).reshape(token_count, per_token)
+
+    def slots_of(low, count):
+        rank = low + jnp.arange(count, dtype=jnp.int32)
+        hit = (routes.T[None, None] == experts[:, None, None, None]) & (
+            slot_rank.T[None, None] == rank[None, :, None, None]
+        )
+        return hit.reshape(expert_total * count, per_token, token_count)
+
+    parts = [(0, -(-capacity // 8) * 8)]
+    arrived = []
+    for low, count in parts:
+        dispatch_matrix = jnp.any(slots_of(low, count), axis=1).astype(jnp.bfloat16)
+        buffer = jnp.dot(
+            dispatch_matrix, normed_rows, preferred_element_type=jnp.float32
+        ).astype(jnp.bfloat16)
+        arrived.append(exchange(buffer, expert_total))
+    expert_sum, out_rows = hidden, None
+    for (low, count), part in zip(parts, arrived):
+        if out_rows is not None:
+            part = lax.optimization_barrier((part, out_rows))[0]
+        slot_rows = gather_tensor(part)
+        gate_part = jnp.dot(slot_rows, gate_weight[0], preferred_element_type=jnp.float32)
+        up_part = jnp.dot(slot_rows, up_weight[0], preferred_element_type=jnp.float32)
+        activated = (jax.nn.silu(gate_part) * up_part).astype(jnp.bfloat16)
+        whole_units = gather_tensor(activated)
+        out_rows = jnp.dot(
+            whole_units, down_weight[0], preferred_element_type=jnp.float32
+        ).astype(jnp.bfloat16)
+        returned = exchange(out_rows, expert_total).astype(jnp.float32)
+        gate_matrix = jnp.sum(
+            jnp.where(slots_of(low, count), gate_values.T[None], 0.0), axis=1
+        )
+        expert_sum = expert_sum + jnp.einsum(
+            "st,sd->td", gate_matrix, returned, precision=lax.Precision.HIGHEST
+        )
+    return expert_sum.astype(jnp.bfloat16)
 
 
 def solution(mesh):

time: 301 us -> 294 us (0.977)
  waiting for transfers between devices: 139 us -> 146 us
  matrix products: 41.5 us -> 35.6 us
  blocking collectives: 45.9 us -> 40.2 us
  other arithmetic: 17.8 us -> 14.4 us
    ppermute x5, waiting for transfers between devices: 22.5 us -> 26.5 us  [hop(): return lax.ppermute(block, 'expert', chip_pairs(moves))]
    ppermute x5 -> x3, waiting for transfers between devices: 8.24 us -> 12.1 us  [give_back(): return lax.ppermute(block, ('expert', 'tensor'), core_pairs(moves))]
    ppermute x6 -> x7, starting transfers between devices: 5.13 us -> 8.83 us  [swap_halves(): return lax.ppermute(array, axis_name, [(0, 1), (1, 0)])]
    all_to_all x1, blocking collectives: 43.4 us -> 40.2 us  [exchange(): lax.all_to_all(split, 'expert', split_axis=0, concat_axis=0, tiled=True)]
    ppermute x5 -> x3, starting transfers between devices: 13.2 us -> 10.9 us  [give_back(): return lax.ppermute(block, ('expert', 'tensor'), core_pairs(moves))]
    ppermute x6 -> x7, waiting for transfers between devices: 36.7 us -> 37.5 us  [swap_halves(): return lax.ppermute(array, axis_name, [(0, 1), (1, 0)])]
  transfers between devices with their start and end apart: 23 -> 22, of which waited for: 13 -> 13; matrix products, arithmetic and copies ran while one was open for 16% -> 14% of each run, Pallas kernels for 0% -> 0%
where the time goes in v3:
time: 294 us; the launch traced here: 289 us
  waiting for transfers between devices  146 us (50%)
  starting transfers between devices  42.7 us (15%)
  blocking collectives  40.2 us (14%)
  matrix products  35.6 us (12%)
  other arithmetic  14.4 us (5%)
  local copies, waits for them, and re-layouts  9.35 us (3%)
    all_to_all x1, blocking collectives, exchange(): lax.all_to_all(split, 'expert', split_axis=0, concat_axis=0, tiled=True)  40.2 us
    ppermute x7, waiting for transfers between devices, swap_halves(): return lax.ppermute(array, axis_name, [(0, 1), (1, 0)])  37.5 us
    all_to_all x1, waiting for transfers between devices, exchange(): lax.all_to_all(split, 'expert', split_axis=0, concat_axis=0, tiled=True)  34.3 us
    ppermute x5, waiting for transfers between devices, hop(): return lax.ppermute(block, 'expert', chip_pairs(moves))  26.5 us
    ppermute x2, waiting for transfers between devices, project_line(): near = [lax.ppermute(p, 'expert', partner) for p in pieces[:2]]  22 us
    ppermute x2, waiting for transfers between devices, project_line(): lax.ppermute(after(p, swap), 'expert', partner)  13.3 us
    ppermute x3, waiting for transfers between devices, give_back(): return lax.ppermute(block, ('expert', 'tensor'), core_pairs(moves))  12.1 us
    dot_general x1, matrix products, project_line(): early = jnp.dot(blocks, columns, preferred_element_type=jnp.float32)  12 us
  transfers between devices with their start and end apart: 22, of which 13 were waited for; matrix products, arithmetic and copies ran while one was open for 14% of the time, Pallas kernels for 0%

profile of v3, /device:TPU:19, one launch (start us, length us, event | category | flops | bytes accessed | tf_op | source)
XLA Modules:
  0.0 288.6 jit_solution(2703486950312806553)
XLA Ops:
  1.3 1.9 collective-permute-start.1
  3.2 2.7 constant_dynamic-slice_fusion.2
  7.4 22.0 %collective-permute-done.4 = bf16[1152,448]{0,1:T(8,128)(2,1)S(1)} collective-permute-done((bf16[1152,448]{0,1:T(8,128)(2,1)S(1)}, bf16[1152,448]{0,1:T(8,128)(2,1)S(1)}, u32[]{:S(2)}, u32[]{:S(2)}) %collective-permute-start.4) | collective-permute-done | bytes 1032224 | tf_op jit(solution)/shard_map/ppermute | solution.py:184
  30.6 2.2 constant_dynamic-slice_fusion.1
  32.8 14.0 %collective-permute-done = bf16[128,8192]{1,0:T(8,128)(2,1)} collective-permute-done((bf16[128,8192]{1,0:T(8,128)(2,1)}, bf16[128,8192]{1,0:T(8,128)(2,1)}, u32[]{:S(2)}, u32[]{:S(2)}) %collective-permute-start) | collective-permute-done | bytes 2097184 | tf_op jit(solution)/shard_map/ppermute | solution.py:167
  47.1 2.1 collective-permute-start.3
  49.7 3.9 %collective-permute-start.2 = (bf16[128,8192]{1,0:T(8,128)(2,1)}, bf16[128,8192]{1,0:T(8,128)(2,1)}, u32[]{:S(2)}, u32[]{:S(2)}) collective-permute-start(bf16[128,8192]{1,0:T(8,128)(2,1)} %collective-permute-done.1), channel_id=1, source_target_pairs={{4,0},{6,2},{8,12},{10,14},{5,1},{7,3},{9,13},{11,15},{20,16},{22,... | collective-permute-start | bytes 6291464 | tf_op jit(solution)/shard_map/ppermute | solution.py:167
  57.8 13.3 %collective-permute-done.8 = bf16[1024,448]{0,1:T(8,128)(2,1)} collective-permute-done((bf16[1024,448]{0,1:T(8,128)(2,1)}, bf16[1024,448]{0,1:T(8,128)(2,1)}, u32[]{:S(2)}, u32[]{:S(2)}) %collective-permute-start.8) | collective-permute-done | bytes 917536 | tf_op jit(solution)/shard_map/ppermute | solution.py:188
  73.0 2.8 collective-permute-done.7
  76.2 19.3 %collective-permute-done.9 = bf16[1024,448]{0,1:T(8,128)(2,1)S(1)} collective-permute-done((bf16[1024,448]{0,1:T(8,128)(2,1)}, bf16[1024,448]{0,1:T(8,128)(2,1)S(1)}, u32[]{:S(2)}, u32[]{:S(2)}) %collective-permute-start.9) | collective-permute-done | bytes 917536 | tf_op jit(solution)/shard_map/ppermute | solution.py:12
  95.5 1.5 select_dynamic-update-slice_fusion.5
  97.2 2.6 collective-permute-start.12
  99.8 2.0 broadcast_select_fusion.2
  101.8 9.4 %collective-permute-done.11 = bf16[768,448]{0,1:T(8,128)(2,1)S(1)} collective-permute-done((bf16[768,448]{0,1:T(8,128)(2,1)S(1)}, bf16[768,448]{0,1:T(8,128)(2,1)S(1)}, u32[]{:S(2)}, u32[]{:S(2)}) %collective-permute-start.11) | collective-permute-done | bytes 688160 | tf_op jit(solution)/shard_map/ppermute | solution.py:12
  111.7 1.7 select_dynamic-update-slice_fusion
  115.6 12.0 %fusion.1 = f32[512,896]{1,0:T(8,128)S(1)} fusion(bf16[8192,448]{0,1:T(8,128)(2,1)S(1)} %get-tuple-element.21, bf16[8192,448]{0,1:T(8,128)(2,1)S(1)} %get-tuple-element.20, bf16[128,8192]{1,0:T(8,128)(2,1)} %collective-permute-done.3, bf16[128,8192]{1,0:T(8,128)(2,1)S(1)} %broadcast_select_fusion.2, bf16[128,8192]{1,0:T(8,128)(2,1)} %collective-permute-done, ...), kind=kOutput, calls=%fused_computation.2 | convolution fusion | flops 7579107328 | bytes 24903680 | tf_op jit(solution)/shard_map/dot_general | solution.py:206
  128.9 11.9 %collective-permute-done.12 = bf16[128,8192]{1,0:T(8,128)(2,1)} collective-permute-done((bf16[128,8192]{1,0:T(8,128)(2,1)}, bf16[128,8192]{1,0:T(8,128)(2,1)}, u32[]{:S(2)}, u32[]{:S(2)}) %collective-permute-start.12) | collective-permute-done | bytes 2097184 | tf_op jit(solution)/shard_map/ppermute | solution.py:167
  142.6 8.5 %fusion.24 = f32[128,896]{1,0:T(8,128)S(1)} fusion(bf16[128,8192]{1,0:T(8,128)(2,1)} %collective-permute-done.12, bf16[8192,448]{0,1:T(8,128)(2,1)} %copy-done.3, bf16[8192,448]{0,1:T(8,128)(2,1)} %copy-done.2, f32[512,896]{1,0:T(8,128)} %copy-done.4, pred[]{:T(512)S(6)} %or.3), kind=kOutput, calls=%fused_computation.33 | convolution fusion | flops 1908523008 | bytes 17694720 | tf_op jit(solution)/shard_map/dot_general | solution.py:217
  152.5 2.3 slice_add_fusion.2
  154.8 4.1 %collective-permute-start.14 = (f32[128,896]{1,0:T(8,128)}, f32[128,896]{1,0:T(8,128)S(1)}, u32[]{:S(2)}, u32[]{:S(2)}) collective-permute-start(f32[128,896]{1,0:T(8,128)} %get-tuple-element.26), channel_id=1, source_target_pairs={{0,4},{2,6},{4,0},{6,2},{9,13},{11,15},{13,9},{15,11},{16,20},{18,... | collective-permute-start | bytes 1376264 | tf_op jit(solution)/shard_map/ppermute | solution.py:176
  158.9 5.6 %collective-permute-start.15 = (f32[128,896]{1,0:T(8,128)}, f32[128,896]{1,0:T(8,128)S(1)}, u32[]{:S(2)}, u32[]{:S(2)}) collective-permute-start(f32[128,896]{1,0:T(8,128)} %get-tuple-element.27), channel_id=1, source_target_pairs={{0,8},{2,10},{13,5},{15,7},{4,12},{6,14},{9,1},{11,3},{16,24},{18,... | collective-permute-start | bytes 1376264 | tf_op jit(solution)/shard_map/ppermute | solution.py:176
  166.9 12.1 %collective-permute-done.17 = bf16[128,896]{1,0:T(8,128)(2,1)S(1)} collective-permute-done((bf16[128,896]{1,0:T(8,128)(2,1)}, bf16[128,896]{1,0:T(8,128)(2,1)S(1)}, u32[]{:S(2)}, u32[]{:S(2)}) %collective-permute-start.17) | collective-permute-done | bytes 229408 | tf_op jit(solution)/shard_map/ppermute | solution.py:176
  181.4 3.7 %collective-permute-start.18 = (f32[128,9]{0,1:T(8,128)S(1)}, f32[128,9]{0,1:T(8,128)S(1)}, u32[]{:S(2)}, u32[]{:S(2)}) collective-permute-start(f32[128,9]{0,1:T(8,128)S(1)} %pad_maximum_fusion.11), channel_id=1, source_target_pairs={{0,1},{1,0},{2,3},{3,2},{4,5},{5,4},{6,7},{7,6},{8,9},{9,8},{10,11... | collective-permute-start | bytes 13832 | tf_op jit(solution)/shard_map/ppermute | solution.py:12
  186.7 40.2 %all_to_all.10 = bf16[8,56,1792]{2,1,0:T(8,128)(2,1)S(1)} all-to-all(bf16[8,56,1792]{2,1,0:T(8,128)(2,1)S(1)} %bitcast.53), channel_id=1, replica_groups=mesh['groups'=2,'expert'=8,'tensor'=2] {'expert'}, dimensions={0} | all-to-all | bytes 3211264 | tf_op jit(solution)/shard_map/all_to_all | solution.py:247
  227.7 3.1 %collective-permute-done.19 = bf16[448,1792]{1,0:T(8,128)(2,1)S(1)} collective-permute-done((bf16[448,1792]{1,0:T(8,128)(2,1)S(1)}, bf16[448,1792]{1,0:T(8,128)(2,1)S(1)}, u32[]{:S(2)}, u32[]{:S(2)}) %collective-permute-start.19) | collective-permute-done | bytes 1605664 | tf_op jit(solution)/shard_map/ppermute | solution.py:12
  231.4 3.5 %fusion.13 = f32[448,1024]{1,0:T(8,128)S(1)} fusion(bf16[1,3584,1024]{2,1,0:T(8,128)(2,1)S(1)} %bitcast.62, bf16[448,1792]{1,0:T(8,128)(2,1)S(1)} %get-tuple-element.25, bf16[448,1792]{1,0:T(8,128)(2,1)S(1)} %get-tuple-element.24), kind=kOutput, calls=%fused_computation.14 | convolution fusion | flops 3294756864 | bytes 12386304 | tf_op jit(solution)/shard_map/dot_general | solution.py:310
  234.9 3.6 %multiply_convert_fusion = bf16[448,1024]{1,0:T(8,128)(2,1)S(1)} fusion(f32[448,1024]{1,0:T(8,128)S(1)} %fusion.13, bf16[1,3584,1024]{2,1,0:T(8,128)(2,1)S(1)} %bitcast.64, bf16[448,1792]{1,0:T(8,128)(2,1)S(1)} %get-tuple-element.25, bf16[448,1792]{1,0:T(8,128)(2,1)S(1)} %get-tuple-element.24), kind=kOutput, calls=%fused_computation.28 | convolution fusion | flops 3297509376 | bytes 13303808 | tf_op jit(solution)/shard_map/dot_general | solution.py:311
  239.0 2.1 collective-permute-done.20
  241.2 4.7 %fusion.15 = bf16[448,1792]{1,0:T(8,128)(2,1)} fusion(bf16[1,2048,1792]{2,1,0:T(8,128)(2,1)S(1)} %bitcast.66, bf16[448,1024]{1,0:T(8,128)(2,1)S(1)} %get-tuple-element.29, bf16[448,1024]{1,0:T(8,128)(2,1)S(1)} %get-tuple-element.28), kind=kOutput, calls=%fused_computation.19 | convolution fusion | flops 3292807168 | bytes 10780672 | tf_op jit(solution)/shard_map/dot_general | solution.py:314
  245.9 6.4 %all-to-all-start.1 = ((bf16[8,56,1792]{2,1,0:T(8,128)(2,1)}), bf16[8,56,1792]{2,1,0:T(8,128)(2,1)S(1)}, u32[]{:S(2)}, u32[]{:S(2)}) async-start(bf16[8,56,1792]{2,1,0:T(8,128)(2,1)} %bitcast.54), calls=%async_computation.1 | async-start | bytes 3211264 | tf_op jit(solution)/shard_map/all_to_all | solution.py:247
  252.5 34.3 %all-to-all-done.1 = bf16[8,56,1792]{2,1,0:T(8,128)(2,1)S(1)} async-done(((bf16[8,56,1792]{2,1,0:T(8,128)(2,1)}), bf16[8,56,1792]{2,1,0:T(8,128)(2,1)S(1)}, u32[]{:S(2)}, u32[]{:S(2)}) %all-to-all-start.1) | async-done | bytes 1605664 | tf_op jit(solution)/shard_map/all_to_all | solution.py:247
  286.8 1.8 fusion.19
  (101 shorter events, 26.7 us)
Async XLA Ops:
  0.0 180.6 %copy-start = (f32[1792,8]{0,1:T(8,128)S(1)}, f32[1792,8]{0,1:T(8,128)}, u32[]{:S(2)}) copy-start(f32[1792,8]{0,1:T(8,128)} %param.13) | copy-start | bytes 172036
  0.0 46.8 %collective-permute-start = (bf16[128,8192]{1,0:T(8,128)(2,1)}, bf16[128,8192]{1,0:T(8,128)(2,1)}, u32[]{:S(2)}, u32[]{:S(2)}) collective-permute-start(bf16[128,8192]{1,0:T(8,128)(2,1)} %param.9), channel_id=1, source_target_pairs={{0,4},{2,6},{4,0},{6,2},{8,12},{10,14},{12,8},{14,10},{1,5},{3,7},... | collective-permute-start | bytes 6291464 | tf_op jit(solution)/shard_map/ppermute | solution.py:167
  1.3 48.4 %collective-permute-start.1 = (bf16[128,8192]{1,0:T(8,128)(2,1)}, bf16[128,8192]{1,0:T(8,128)(2,1)}, u32[]{:S(2)}, u32[]{:S(2)}) collective-permute-start(bf16[128,8192]{1,0:T(8,128)(2,1)} %param.9), channel_id=1, source_target_pairs={{4,8},{6,10},{8,4},{10,6},{5,9},{7,11},{9,5},{11,7},{20,24},{22,26... | collective-permute-start | bytes 6291464 | tf_op jit(solution)/shard_map/ppermute | solution.py:167
  5.9 23.5 %collective-permute-start.4 = (bf16[1152,448]{0,1:T(8,128)(2,1)S(1)}, bf16[1152,448]{0,1:T(8,128)(2,1)S(1)}, u32[]{:S(2)}, u32[]{:S(2)}) collective-permute-start(bf16[1152,448]{0,1:T(8,128)(2,1)S(1)} %get-tuple-element.23), channel_id=1, source_target_pairs={{0,2},{2,0},{4,6},{6,4},{8,10},{10,8},{12,14},{14,12},{1,3},{3,1},... | collective-permute-start | bytes 3096584 | tf_op jit(solution)/shard_map/ppermute | solution.py:184
  6.2 47.4 %collective-permute-start.6 = (bf16[1152,448]{0,1:T(8,128)(2,1)}, bf16[1152,448]{0,1:T(8,128)(2,1)S(1)}, u32[]{:S(2)}, u32[]{:S(2)}) collective-permute-start(bf16[1152,448]{0,1:T(8,128)(2,1)} %get-tuple-element.22), channel_id=1, source_target_pairs={{0,2},{2,0},{4,6},{6,4},{8,10},{10,8},{12,14},{14,12},{1,3},{3,1},... | collective-permute-start | bytes 3096584 | tf_op jit(solution)/shard_map/ppermute | solution.py:184
  29.4 43.0 %collective-permute-start.5 = (bf16[1152,448]{0,1:T(8,128)(2,1)S(1)}, bf16[1152,448]{0,1:T(8,128)(2,1)S(1)}, u32[]{:S(2)}, u32[]{:S(2)}) collective-permute-start(bf16[1152,448]{0,1:T(8,128)(2,1)S(1)} %collective-permute-done.4), channel_id=1, source_target_pairs={{0,16},{16,0},{1,17},{17,1},{2,18},{18,2},{3,19},{19,3},{4,20},{20... | collective-permute-start | bytes 3096584 | tf_op jit(solution)/shard_map/ppermute | solution.py:12
  46.8 24.3 %collective-permute-start.8 = (bf16[1024,448]{0,1:T(8,128)(2,1)}, bf16[1024,448]{0,1:T(8,128)(2,1)}, u32[]{:S(2)}, u32[]{:S(2)}) collective-permute-start(bf16[1024,448]{0,1:T(8,128)(2,1)} %constant_dynamic-slice_fusion.1), channel_id=1, source_target_pairs={{0,2},{2,0},{4,6},{6,4},{8,10},{10,8},{12,14},{14,12},{1,3},{3,1},... | collective-permute-start | bytes 2752520 | tf_op jit(solution)/shard_map/ppermute | solution.py:188
  47.1 50.0 %collective-permute-start.3 = (bf16[128,8192]{1,0:T(8,128)(2,1)}, bf16[128,8192]{1,0:T(8,128)(2,1)}, u32[]{:S(2)}, u32[]{:S(2)}) collective-permute-start(bf16[128,8192]{1,0:T(8,128)(2,1)} %collective-permute-done), channel_id=1, source_target_pairs={{4,8},{6,10},{8,4},{10,6},{5,9},{7,11},{9,5},{11,7},{20,24},{22,26... | collective-permute-start | bytes 6291464 | tf_op jit(solution)/shard_map/ppermute | solution.py:167
  49.7 50.1 %collective-permute-start.2 = (bf16[128,8192]{1,0:T(8,128)(2,1)}, bf16[128,8192]{1,0:T(8,128)(2,1)}, u32[]{:S(2)}, u32[]{:S(2)}) collective-permute-start(bf16[128,8192]{1,0:T(8,128)(2,1)} %collective-permute-done.1), channel_id=1, source_target_pairs={{4,0},{6,2},{8,12},{10,14},{5,1},{7,3},{9,13},{11,15},{20,16},{22,... | collective-permute-start | bytes 6291464 | tf_op jit(solution)/shard_map/ppermute | solution.py:167
  53.6 22.3 %collective-permute-start.7 = (bf16[1152,448]{0,1:T(8,128)(2,1)S(1)}, bf16[1152,448]{0,1:T(8,128)(2,1)}, u32[]{:S(2)}, u32[]{:S(2)}) collective-permute-start(bf16[1152,448]{0,1:T(8,128)(2,1)S(1)} %collective-permute-done.6), channel_id=1, source_target_pairs={{0,16},{16,0},{1,17},{17,1},{2,18},{18,2},{3,19},{19,3},{4,20},{20... | collective-permute-start | bytes 3096584 | tf_op jit(solution)/shard_map/ppermute | solution.py:12
  71.2 24.4 %collective-permute-start.9 = (bf16[1024,448]{0,1:T(8,128)(2,1)}, bf16[1024,448]{0,1:T(8,128)(2,1)S(1)}, u32[]{:S(2)}, u32[]{:S(2)}) collective-permute-start(bf16[1024,448]{0,1:T(8,128)(2,1)} %collective-permute-done.8), channel_id=1, source_target_pairs={{0,16},{16,0},{1,17},{17,1},{2,18},{18,2},{3,19},{19,3},{4,20},{20... | collective-permute-start | bytes 2752520 | tf_op jit(solution)/shard_map/ppermute | solution.py:12
  72.7 24.4 %collective-permute-start.10 = (bf16[768,448]{0,1:T(8,128)(2,1)S(1)}, bf16[768,448]{0,1:T(8,128)(2,1)S(1)}, u32[]{:S(2)}, u32[]{:S(2)}) collective-permute-start(bf16[768,448]{0,1:T(8,128)(2,1)S(1)} %constant_dynamic-slice_fusion), channel_id=1, source_target_pairs={{0,2},{2,0},{4,6},{6,4},{8,10},{10,8},{12,14},{14,12},{1,3},{3,1},... | collective-permute-start | bytes 2064392 | tf_op jit(solution)/shard_map/ppermute | solution.py:188
  97.1 14.1 %collective-permute-start.11 = (bf16[768,448]{0,1:T(8,128)(2,1)S(1)}, bf16[768,448]{0,1:T(8,128)(2,1)S(1)}, u32[]{:S(2)}, u32[]{:S(2)}) collective-permute-start(bf16[768,448]{0,1:T(8,128)(2,1)S(1)} %collective-permute-done.10), channel_id=1, source_target_pairs={{0,16},{16,0},{1,17},{17,1},{2,18},{18,2},{3,19},{19,3},{4,20},{20... | collective-permute-start | bytes 2064392 | tf_op jit(solution)/shard_map/ppermute | solution.py:12
  97.2 43.6 %collective-permute-start.12 = (bf16[128,8192]{1,0:T(8,128)(2,1)}, bf16[128,8192]{1,0:T(8,128)(2,1)}, u32[]{:S(2)}, u32[]{:S(2)}) collective-permute-start(bf16[128,8192]{1,0:T(8,128)(2,1)} %collective-permute-done.3), channel_id=1, source_target_pairs={{4,0},{6,2},{8,12},{10,14},{5,1},{7,3},{9,13},{11,15},{20,16},{22,... | collective-permute-start | bytes 6291464 | tf_op jit(solution)/shard_map/ppermute | solution.py:167
  99.8 14.2 %slice-start = ((s8[7340032]{0:T(1024)(128)(4,1)}), s8[4194304]{0:T(1024)(128)(4,1)S(1)}, s32[]{:S(2)}) async-start(s8[7340032]{0:T(1024)(128)(4,1)} %bitcast.50), calls=%async_computation.2 | async-start | bytes 8388608
  115.0 12.6 %copy-start.2 = (bf16[8192,448]{0,1:T(8,128)(2,1)}, bf16[8192,448]{0,1:T(8,128)(2,1)S(1)}, u32[]{:S(2)}) copy-start(bf16[8192,448]{0,1:T(8,128)(2,1)S(1)} %get-tuple-element.20) | copy-start | bytes 22020100
  115.1 12.6 %copy-start.3 = (bf16[8192,448]{0,1:T(8,128)(2,1)}, bf16[8192,448]{0,1:T(8,128)(2,1)S(1)}, u32[]{:S(2)}) copy-start(bf16[8192,448]{0,1:T(8,128)(2,1)S(1)} %get-tuple-element.21) | copy-start | bytes 22020100
  140.8 11.7 %collective-permute-start.13 = (f32[384,896]{1,0:T(8,128)S(1)}, f32[384,896]{1,0:T(8,128)}, u32[]{:S(2)}, u32[]{:S(2)}) collective-permute-start(f32[384,896]{1,0:T(8,128)S(1)} %pad_maximum_fusion.6), channel_id=1, source_target_pairs={{1,0},{3,2},{5,4},{7,6},{8,9},{10,11},{12,13},{14,15},{17,16},{19,... | collective-permute-start | bytes 4128776 | tf_op jit(solution)/shard_map/ppermute | solution.py:173
  142.5 9.9 %copy-start.5 = (s32[128,3]{0,1:T(4,128)S(1)}, s32[128,3]{0,1:T(4,128)}, u32[]{:S(2)}) copy-start(s32[128,3]{0,1:T(4,128)} %param.14) | copy-start | bytes 4612
  142.5 24.1 %copy-start.6 = (bf16[1792]{0:T(1024)(128)(2,1)S(1)}, bf16[1792]{0:T(1024)(128)(2,1)}, u32[]{:S(2)}) copy-start(bf16[1792]{0:T(1024)(128)(2,1)} %param.12) | copy-start | bytes 10756
  151.0 29.3 %copy-start.1 = (bf16[128,1792]{1,0:T(8,128)(2,1)S(1)}, bf16[128,1792]{1,0:T(8,128)(2,1)}, u32[]{:S(2)}) copy-start(bf16[128,1792]{1,0:T(8,128)(2,1)} %param.11) | copy-start | bytes 1376260
  151.0 13.4 %collective-permute-start.16 = (f32[128,896]{1,0:T(8,128)S(1)}, f32[128,896]{1,0:T(8,128)S(1)}, u32[]{:S(2)}, u32[]{:S(2)}) collective-permute-start(f32[128,896]{1,0:T(8,128)S(1)} %fusion.24), channel_id=1, source_target_pairs={{1,0},{3,2},{5,4},{7,6},{8,9},{10,11},{12,13},{14,15},{17,16},{19,... | collective-permute-start | bytes 1376264 | tf_op jit(solution)/shard_map/ppermute | solution.py:173
  154.8 24.3 %collective-permute-start.14 = (f32[128,896]{1,0:T(8,128)}, f32[128,896]{1,0:T(8,128)S(1)}, u32[]{:S(2)}, u32[]{:S(2)}) collective-permute-start(f32[128,896]{1,0:T(8,128)} %get-tuple-element.26), channel_id=1, source_target_pairs={{0,4},{2,6},{4,0},{6,2},{9,13},{11,15},{13,9},{15,11},{16,20},{18,... | collective-permute-start | bytes 1376264 | tf_op jit(solution)/shard_map/ppermute | solution.py:176
  158.9 20.2 %collective-permute-start.15 = (f32[128,896]{1,0:T(8,128)}, f32[128,896]{1,0:T(8,128)S(1)}, u32[]{:S(2)}, u32[]{:S(2)}) collective-permute-start(f32[128,896]{1,0:T(8,128)} %get-tuple-element.27), channel_id=1, source_target_pairs={{0,8},{2,10},{13,5},{15,7},{4,12},{6,14},{9,1},{11,3},{16,24},{18,... | collective-permute-start | bytes 1376264 | tf_op jit(solution)/shard_map/ppermute | solution.py:176
  165.2 13.9 %collective-permute-start.17 = (bf16[128,896]{1,0:T(8,128)(2,1)}, bf16[128,896]{1,0:T(8,128)(2,1)S(1)}, u32[]{:S(2)}, u32[]{:S(2)}) collective-permute-start(bf16[128,896]{1,0:T(8,128)(2,1)} %add_convert_fusion), channel_id=1, source_target_pairs={{0,12},{2,14},{13,1},{15,3},{4,8},{6,10},{9,5},{11,7},{16,28},{18,... | collective-permute-start | bytes 688136 | tf_op jit(solution)/shard_map/ppermute | solution.py:176
  180.6 50.8 %slice-start.2 = ((s8[7340032]{0:T(1024)(128)(4,1)}), s8[4194304]{0:T(1024)(128)(4,1)S(1)}, s32[]{:S(2)}) async-start(s8[7340032]{0:T(1024)(128)(4,1)} %bitcast.61), calls=%async_computation.4 | async-start | bytes 8388608
  181.4 4.5 %collective-permute-start.18 = (f32[128,9]{0,1:T(8,128)S(1)}, f32[128,9]{0,1:T(8,128)S(1)}, u32[]{:S(2)}, u32[]{:S(2)}) collective-permute-start(f32[128,9]{0,1:T(8,128)S(1)} %pad_maximum_fusion.11), channel_id=1, source_target_pairs={{0,1},{1,0},{2,3},{3,2},{4,5},{5,4},{6,7},{7,6},{8,9},{9,8},{10,11... | collective-permute-start | bytes 13832 | tf_op jit(solution)/shard_map/ppermute | solution.py:12
  186.6 44.7 %slice-start.3 = ((s8[7340032]{0:T(1024)(128)(4,1)}), s8[3145728]{0:T(1024)(128)(4,1)S(1)}, s32[]{:S(2)}) async-start(s8[7340032]{0:T(1024)(128)(4,1)} %bitcast.61), calls=%async_computation.5 | async-start | bytes 6291456
  226.9 3.9 %collective-permute-start.19 = (bf16[448,1792]{1,0:T(8,128)(2,1)S(1)}, bf16[448,1792]{1,0:T(8,128)(2,1)S(1)}, u32[]{:S(2)}, u32[]{:S(2)}) collective-permute-start(bf16[448,1792]{1,0:T(8,128)(2,1)S(1)} %bitcast.52), channel_id=1, source_target_pairs={{0,1},{1,0},{2,3},{3,2},{4,5},{5,4},{6,7},{7,6},{8,9},{9,8},{10,11... | collective-permute-start | bytes 4816904 | tf_op jit(solution)/shard_map/ppermute | solution.py:12
  231.4 9.8 %slice-start.6 = ((s8[7340032]{0:T(1024)(128)(4,1)}), s8[4194304]{0:T(1024)(128)(4,1)S(1)}, s32[]{:S(2)}) async-start(s8[7340032]{0:T(1024)(128)(4,1)} %bitcast.65), calls=%async_computation.8 | async-start | bytes 8388608
  238.5 2.5 collective-permute-start.20
  245.9 40.9 %all-to-all-start.1 = ((bf16[8,56,1792]{2,1,0:T(8,128)(2,1)}), bf16[8,56,1792]{2,1,0:T(8,128)(2,1)S(1)}, u32[]{:S(2)}, u32[]{:S(2)}) async-start(bf16[8,56,1792]{2,1,0:T(8,128)(2,1)} %bitcast.54), calls=%async_computation.1 | async-start | bytes 3211264 | tf_op jit(solution)/shard_map/all_to_all | solution.py:247
  (6 other events, 19.3 us)

commit v4 on v3

--- a/solution.py
+++ b/solution.py
@@ -187,8 +187,10 @@
     cross_far = hop(swap, CROSS)
     near += [lax.ppermute(after(p, swap), "expert", partner) for p in pieces[2:]]
     far += [swap_halves(after(near[1], swap), "groups"), swap_halves(near[2], "groups")]
-    out_far = hop(cross_far, OUTWARD)
-    far += [swap_halves(after(near[3], cross_far), "groups")]
+    most = depth // 4 * 3
+    ready = [cross_far[:, :most], cross_far[:, most:]]
+    out_far = [hop(block, OUTWARD) for block in ready]
+    far += [swap_halves(after(near[3], ready), "groups")]
 
     lower_half = group == 0
     passed_rows = jnp.concatenate(
@@ -206,15 +208,17 @@
     early = jnp.dot(blocks, columns, preferred_element_type=jnp.float32)
     third, fourth = early[2 * rows : 3 * rows], early[3 * rows :]
     early = jnp.concatenate([early[: 2 * rows], jnp.where(middle, fourth, third)], axis=0)
-    early = after(early, out_far)
+    early = after(early, out_far[0])
     from_core = to_owners(early)
     own_sum, swap_sum, cross_sum = (
         early[i * rows : (i + 1) * rows] + from_core[i * rows : (i + 1) * rows]
         for i in range(3)
     )
+    last = jnp.dot(out_far[0], columns[:most], preferred_element_type=jnp.float32)
+    out_far[1] = after(out_far[1], (swap_sum, cross_sum, last))
     swap_sum = give_back(swap_sum, SWAP)
     cross_sum = give_back(cross_sum, ((0, 2), (3, 1), (1, 3), (2, 0)))
-    last = jnp.dot(out_far, columns, preferred_element_type=jnp.float32)
+    last = last + jnp.dot(out_far[1], columns[most:], preferred_element_type=jnp.float32)
     last = jnp.where(middle, third, last)
     last = (last + to_owners(last)).astype(jnp.bfloat16)
     last_sum = give_back(last, ((0, 3), (3, 0), (1, 2), (2, 1))).astype(jnp.float32)

time: 294 us -> 288 us (0.980)
  waiting for transfers between devices: 146 us -> 137 us
  local copies, waits for them, and re-layouts: 9.35 us -> 13 us
    ppermute x5 -> x6, waiting for transfers between devices: 26.5 us -> 14.3 us  [hop(): return lax.ppermute(block, 'expert', chip_pairs(moves))]
    slice x1 -> x3, local copies, waits for them, and re-layouts: 0.21 us -> 4.77 us  [the longest x2 4.56 us: project_line(): ready = [cross_far[:, :most], cross_far[:, most:]]]
    ppermute x5 -> x6, starting transfers between devices: 11.7 us -> 13.8 us  [hop(): return lax.ppermute(block, 'expert', chip_pairs(moves))]
    dot_general x1 -> x2, matrix products: 8.47 us -> 7.42 us  [the longest x1 5.06 us: project_line(): jnp.dot(out_far[0], columns[:most], preferred_element_type=jnp.float32)]
  transfers between devices with their start and end apart: 22 -> 23, of which waited for: 13 -> 15; matrix products, arithmetic and copies ran while one was open for 14% -> 15% of each run, Pallas kernels for 0% -> 0%
where the time goes in v4:
time: 288 us; the launch traced here: 282 us
  waiting for transfers between devices  137 us (48%)
  starting transfers between devices  41 us (14%)
  blocking collectives  40.2 us (14%)
  matrix products  34.5 us (12%)
  other arithmetic  15.4 us (5%)
  local copies, waits for them, and re-layouts  13 us (5%)
    all_to_all x1, blocking collectives, exchange(): lax.all_to_all(split, 'expert', split_axis=0, concat_axis=0, tiled=True)  40.2 us
    ppermute x7, waiting for transfers between devices, swap_halves(): return lax.ppermute(array, axis_name, [(0, 1), (1, 0)])  38.6 us
    all_to_all x1, waiting for transfers between devices, exchange(): lax.all_to_all(split, 'expert', split_axis=0, concat_axis=0, tiled=True)  34.3 us
    ppermute x2, waiting for transfers between devices, project_line(): near = [lax.ppermute(p, 'expert', partner) for p in pieces[:2]]  22.2 us
    ppermute x6, waiting for transfers between devices, hop(): return lax.ppermute(block, 'expert', chip_pairs(moves))  14.3 us
    ppermute x2, waiting for transfers between devices, project_line(): lax.ppermute(after(p, swap), 'expert', partner)  14.1 us
    ppermute x6, starting transfers between devices, hop(): return lax.ppermute(block, 'expert', chip_pairs(moves))  13.8 us
    ppermute x3, waiting for transfers between devices, give_back(): return lax.ppermute(block, ('expert', 'tensor'), core_pairs(moves))  12.5 us
  transfers between devices with their start and end apart: 23, of which 15 were waited for; matrix products, arithmetic and copies ran while one was open for 15% of the time, Pallas kernels for 0%

profile of v4, /device:TPU:19, one launch (start us, length us, event | category | flops | bytes accessed | tf_op | source)
XLA Modules:
  0.0 282.0 jit_solution(2771015336063666562)
XLA Ops:
  1.3 1.9 collective-permute-start.1
  3.2 2.7 constant_dynamic-slice_fusion.2
  7.4 22.2 %collective-permute-done.4 = bf16[1152,448]{0,1:T(8,128)(2,1)S(1)} collective-permute-done((bf16[1152,448]{0,1:T(8,128)(2,1)}, bf16[1152,448]{0,1:T(8,128)(2,1)S(1)}, u32[]{:S(2)}, u32[]{:S(2)}) %collective-permute-start.4) | collective-permute-done | bytes 1032224 | tf_op jit(solution)/shard_map/ppermute | solution.py:184
  30.8 2.2 constant_dynamic-slice_fusion.1
  33.1 13.8 %collective-permute-done = bf16[128,8192]{1,0:T(8,128)(2,1)} collective-permute-done((bf16[128,8192]{1,0:T(8,128)(2,1)}, bf16[128,8192]{1,0:T(8,128)(2,1)}, u32[]{:S(2)}, u32[]{:S(2)}) %collective-permute-start) | collective-permute-done | bytes 2097184 | tf_op jit(solution)/shard_map/ppermute | solution.py:167
  47.1 2.1 collective-permute-start.3
  49.7 3.9 %collective-permute-start.2 = (bf16[128,8192]{1,0:T(8,128)(2,1)}, bf16[128,8192]{1,0:T(8,128)(2,1)}, u32[]{:S(2)}, u32[]{:S(2)}) collective-permute-start(bf16[128,8192]{1,0:T(8,128)(2,1)} %collective-permute-done.1), channel_id=1, source_target_pairs={{4,0},{6,2},{8,12},{10,14},{5,1},{7,3},{9,13},{11,15},{20,16},{22,... | collective-permute-start | bytes 6291464 | tf_op jit(solution)/shard_map/ppermute | solution.py:167
  57.2 14.1 %collective-permute-done.8 = bf16[1024,448]{0,1:T(8,128)(2,1)} collective-permute-done((bf16[1024,448]{0,1:T(8,128)(2,1)}, bf16[1024,448]{0,1:T(8,128)(2,1)}, u32[]{:S(2)}, u32[]{:S(2)}) %collective-permute-start.8) | collective-permute-done | bytes 917536 | tf_op jit(solution)/shard_map/ppermute | solution.py:188
  73.2 2.7 collective-permute-done.7
  76.3 19.3 %collective-permute-done.9 = bf16[1024,448]{0,1:T(8,128)(2,1)S(1)} collective-permute-done((bf16[1024,448]{0,1:T(8,128)(2,1)}, bf16[1024,448]{0,1:T(8,128)(2,1)S(1)}, u32[]{:S(2)}, u32[]{:S(2)}) %collective-permute-start.9) | collective-permute-done | bytes 917536 | tf_op jit(solution)/shard_map/ppermute | solution.py:12
  97.1 2.7 slice.68
  99.8 2.5 collective-permute-start.12
  102.3 1.9 slice.69
  104.2 2.1 collective-permute-start.16
  106.4 3.4 %broadcast_select_fusion.2 = bf16[128,8192]{1,0:T(8,128)(2,1)} fusion(bf16[128,8192]{1,0:T(8,128)(2,1)} %collective-permute-done.1, bf16[128,8192]{1,0:T(8,128)(2,1)} %collective-permute-done.2, pred[]{:T(512)S(6)} %or.3), kind=kLoop, calls=%fused_computation.31 | loop fusion | flops 1048576 | bytes 6291457 | tf_op jit(solution)/shard_map/jit(_where)/select_n | solution.py:206
  109.7 10.6 %collective-permute-done.11 = bf16[768,448]{0,1:T(8,128)(2,1)S(1)} collective-permute-done((bf16[768,448]{0,1:T(8,128)(2,1)S(1)}, bf16[768,448]{0,1:T(8,128)(2,1)S(1)}, u32[]{:S(2)}, u32[]{:S(2)}) %collective-permute-start.11) | collective-permute-done | bytes 688160 | tf_op jit(solution)/shard_map/ppermute | solution.py:12
  125.9 12.0 %fusion = f32[512,896]{1,0:T(8,128)S(1)} fusion(bf16[8192,448]{0,1:T(8,128)(2,1)S(1)} %get-tuple-element.23, bf16[8192,448]{0,1:T(8,128)(2,1)S(1)} %get-tuple-element.22, bf16[128,8192]{1,0:T(8,128)(2,1)} %collective-permute-done.3, bf16[128,8192]{1,0:T(8,128)(2,1)S(1)} %copy-done.2, bf16[128,8192]{1,0:T(8,128)(2,1)} %collective-permute-done, ...), kind=kOutput, calls=%fused_computation.5 | convolution fusion | flops 7579107328 | bytes 24903680 | tf_op jit(solution)/shard_map/dot_general | solution.py:208
  139.5 5.1 %fusion.28 = f32[128,896]{1,0:T(8,128)S(1)} fusion(bf16[128,6144]{1,0:T(8,128)(2,1)} %collective-permute-done.12, bf16[8192,448]{0,1:T(8,128)(2,1)S(1)} %get-tuple-element.22, bf16[8192,448]{0,1:T(8,128)(2,1)S(1)} %get-tuple-element.23), kind=kOutput, calls=%fused_computation.39 | convolution fusion | flops 1431306240 | bytes 16711680 | tf_op jit(solution)/shard_map/dot_general | solution.py:217
  147.0 2.4 fusion.34
  151.9 1.9 collective-permute-start.14
  153.9 4.7 %collective-permute-start.15 = (f32[128,896]{1,0:T(8,128)S(1)}, f32[128,896]{1,0:T(8,128)}, u32[]{:S(2)}, u32[]{:S(2)}) collective-permute-start(f32[128,896]{1,0:T(8,128)S(1)} %get-tuple-element.29), channel_id=1, source_target_pairs={{0,8},{2,10},{13,5},{15,7},{4,12},{6,14},{9,1},{11,3},{16,24},{18,... | collective-permute-start | bytes 1376264 | tf_op jit(solution)/shard_map/ppermute | solution.py:176
  161.5 9.2 %collective-permute-done.15 = f32[128,896]{1,0:T(8,128)} collective-permute-done((f32[128,896]{1,0:T(8,128)S(1)}, f32[128,896]{1,0:T(8,128)}, u32[]{:S(2)}, u32[]{:S(2)}) %collective-permute-start.15) | collective-permute-done | bytes 458784 | tf_op jit(solution)/shard_map/ppermute | solution.py:176
  170.6 2.5 collective-permute-done.18
  175.7 2.7 collective-permute-start.19
  180.0 40.2 %all_to_all.10 = bf16[8,56,1792]{2,1,0:T(8,128)(2,1)S(1)} all-to-all(bf16[8,56,1792]{2,1,0:T(8,128)(2,1)S(1)} %bitcast.52), channel_id=1, replica_groups=mesh['groups'=2,'expert'=8,'tensor'=2] {'expert'}, dimensions={0} | all-to-all | bytes 3211264 | tf_op jit(solution)/shard_map/all_to_all | solution.py:251
  221.1 3.1 %collective-permute-done.20 = bf16[448,1792]{1,0:T(8,128)(2,1)S(1)} collective-permute-done((bf16[448,1792]{1,0:T(8,128)(2,1)S(1)}, bf16[448,1792]{1,0:T(8,128)(2,1)S(1)}, u32[]{:S(2)}, u32[]{:S(2)}) %collective-permute-start.20) | collective-permute-done | bytes 1605664 | tf_op jit(solution)/shard_map/ppermute | solution.py:12
  224.7 3.5 %fusion.15 = f32[448,1024]{1,0:T(8,128)S(1)} fusion(bf16[1,3584,1024]{2,1,0:T(8,128)(2,1)S(1)} %bitcast.61, bf16[448,1792]{1,0:T(8,128)(2,1)S(1)} %get-tuple-element.27, bf16[448,1792]{1,0:T(8,128)(2,1)S(1)} %get-tuple-element.26), kind=kOutput, calls=%fused_computation.19 | convolution fusion | flops 3294756864 | bytes 12386304 | tf_op jit(solution)/shard_map/dot_general | solution.py:314
  228.2 3.6 %multiply_convert_fusion = bf16[448,1024]{1,0:T(8,128)(2,1)S(1)} fusion(f32[448,1024]{1,0:T(8,128)S(1)} %fusion.15, bf16[1,3584,1024]{2,1,0:T(8,128)(2,1)S(1)} %bitcast.63, bf16[448,1792]{1,0:T(8,128)(2,1)S(1)} %get-tuple-element.27, bf16[448,1792]{1,0:T(8,128)(2,1)S(1)} %get-tuple-element.26), kind=kOutput, calls=%fused_computation.35 | convolution fusion | flops 3297509376 | bytes 13303808 | tf_op jit(solution)/shard_map/dot_general | solution.py:315
  232.3 2.1 collective-permute-done.21
  234.6 4.7 %fusion.20 = bf16[448,1792]{1,0:T(8,128)(2,1)} fusion(bf16[1,2048,1792]{2,1,0:T(8,128)(2,1)S(1)} %bitcast.65, bf16[448,1024]{1,0:T(8,128)(2,1)S(1)} %get-tuple-element.31, bf16[448,1024]{1,0:T(8,128)(2,1)S(1)} %get-tuple-element.30), kind=kOutput, calls=%fused_computation.26 | convolution fusion | flops 3292807168 | bytes 10780672 | tf_op jit(solution)/shard_map/dot_general | solution.py:318
  239.2 6.4 %all-to-all-start.1 = ((bf16[8,56,1792]{2,1,0:T(8,128)(2,1)}), bf16[8,56,1792]{2,1,0:T(8,128)(2,1)S(1)}, u32[]{:S(2)}, u32[]{:S(2)}) async-start(bf16[8,56,1792]{2,1,0:T(8,128)(2,1)} %bitcast.53), calls=%async_computation.1 | async-start | bytes 3211264 | tf_op jit(solution)/shard_map/all_to_all | solution.py:251
  245.8 34.3 %all-to-all-done.1 = bf16[8,56,1792]{2,1,0:T(8,128)(2,1)S(1)} async-done(((bf16[8,56,1792]{2,1,0:T(8,128)(2,1)}), bf16[8,56,1792]{2,1,0:T(8,128)(2,1)S(1)}, u32[]{:S(2)}, u32[]{:S(2)}) %all-to-all-start.1) | async-done | bytes 1605664 | tf_op jit(solution)/shard_map/all_to_all | solution.py:251
  (102 shorter events, 35.0 us)
Async XLA Ops:
  0.0 174.9 %copy-start = (f32[1792,8]{0,1:T(8,128)S(1)}, f32[1792,8]{0,1:T(8,128)}, u32[]{:S(2)}) copy-start(f32[1792,8]{0,1:T(8,128)} %param.13) | copy-start | bytes 172036
  0.0 46.8 %collective-permute-start = (bf16[128,8192]{1,0:T(8,128)(2,1)}, bf16[128,8192]{1,0:T(8,128)(2,1)}, u32[]{:S(2)}, u32[]{:S(2)}) collective-permute-start(bf16[128,8192]{1,0:T(8,128)(2,1)} %param.9), channel_id=1, source_target_pairs={{0,4},{2,6},{4,0},{6,2},{8,12},{10,14},{12,8},{14,10},{1,5},{3,7},... | collective-permute-start | bytes 6291464 | tf_op jit(solution)/shard_map/ppermute | solution.py:167
  1.3 48.4 %collective-permute-start.1 = (bf16[128,8192]{1,0:T(8,128)(2,1)}, bf16[128,8192]{1,0:T(8,128)(2,1)}, u32[]{:S(2)}, u32[]{:S(2)}) collective-permute-start(bf16[128,8192]{1,0:T(8,128)(2,1)} %param.9), channel_id=1, source_target_pairs={{4,8},{6,10},{8,4},{10,6},{5,9},{7,11},{9,5},{11,7},{20,24},{22,26... | collective-permute-start | bytes 6291464 | tf_op jit(solution)/shard_map/ppermute | solution.py:167
  5.9 23.7 %collective-permute-start.4 = (bf16[1152,448]{0,1:T(8,128)(2,1)}, bf16[1152,448]{0,1:T(8,128)(2,1)S(1)}, u32[]{:S(2)}, u32[]{:S(2)}) collective-permute-start(bf16[1152,448]{0,1:T(8,128)(2,1)} %get-tuple-element.25), channel_id=1, source_target_pairs={{0,2},{2,0},{4,6},{6,4},{8,10},{10,8},{12,14},{14,12},{1,3},{3,1},... | collective-permute-start | bytes 3096584 | tf_op jit(solution)/shard_map/ppermute | solution.py:184
  6.2 47.5 %collective-permute-start.6 = (bf16[1152,448]{0,1:T(8,128)(2,1)S(1)}, bf16[1152,448]{0,1:T(8,128)(2,1)S(1)}, u32[]{:S(2)}, u32[]{:S(2)}) collective-permute-start(bf16[1152,448]{0,1:T(8,128)(2,1)S(1)} %get-tuple-element.24), channel_id=1, source_target_pairs={{0,2},{2,0},{4,6},{6,4},{8,10},{10,8},{12,14},{14,12},{1,3},{3,1},... | collective-permute-start | bytes 3096584 | tf_op jit(solution)/shard_map/ppermute | solution.py:184
  29.6 43.0 %collective-permute-start.5 = (bf16[1152,448]{0,1:T(8,128)(2,1)S(1)}, bf16[1152,448]{0,1:T(8,128)(2,1)}, u32[]{:S(2)}, u32[]{:S(2)}) collective-permute-start(bf16[1152,448]{0,1:T(8,128)(2,1)S(1)} %collective-permute-done.4), channel_id=1, source_target_pairs={{0,16},{16,0},{1,17},{17,1},{2,18},{18,2},{3,19},{19,3},{4,20},{20... | collective-permute-start | bytes 3096584 | tf_op jit(solution)/shard_map/ppermute | solution.py:12
  46.8 24.5 %collective-permute-start.8 = (bf16[1024,448]{0,1:T(8,128)(2,1)}, bf16[1024,448]{0,1:T(8,128)(2,1)}, u32[]{:S(2)}, u32[]{:S(2)}) collective-permute-start(bf16[1024,448]{0,1:T(8,128)(2,1)} %constant_dynamic-slice_fusion.1), channel_id=1, source_target_pairs={{0,2},{2,0},{4,6},{6,4},{8,10},{10,8},{12,14},{14,12},{1,3},{3,1},... | collective-permute-start | bytes 2752520 | tf_op jit(solution)/shard_map/ppermute | solution.py:188
  47.1 50.1 %collective-permute-start.3 = (bf16[128,8192]{1,0:T(8,128)(2,1)}, bf16[128,8192]{1,0:T(8,128)(2,1)}, u32[]{:S(2)}, u32[]{:S(2)}) collective-permute-start(bf16[128,8192]{1,0:T(8,128)(2,1)} %collective-permute-done), channel_id=1, source_target_pairs={{4,8},{6,10},{8,4},{10,6},{5,9},{7,11},{9,5},{11,7},{20,24},{22,26... | collective-permute-start | bytes 6291464 | tf_op jit(solution)/shard_map/ppermute | solution.py:167
  49.7 56.7 %collective-permute-start.2 = (bf16[128,8192]{1,0:T(8,128)(2,1)}, bf16[128,8192]{1,0:T(8,128)(2,1)}, u32[]{:S(2)}, u32[]{:S(2)}) collective-permute-start(bf16[128,8192]{1,0:T(8,128)(2,1)} %collective-permute-done.1), channel_id=1, source_target_pairs={{4,0},{6,2},{8,12},{10,14},{5,1},{7,3},{9,13},{11,15},{20,16},{22,... | collective-permute-start | bytes 6291464 | tf_op jit(solution)/shard_map/ppermute | solution.py:167
  53.6 22.3 %collective-permute-start.7 = (bf16[1152,448]{0,1:T(8,128)(2,1)S(1)}, bf16[1152,448]{0,1:T(8,128)(2,1)}, u32[]{:S(2)}, u32[]{:S(2)}) collective-permute-start(bf16[1152,448]{0,1:T(8,128)(2,1)S(1)} %collective-permute-done.6), channel_id=1, source_target_pairs={{0,16},{16,0},{1,17},{17,1},{2,18},{18,2},{3,19},{19,3},{4,20},{20... | collective-permute-start | bytes 3096584 | tf_op jit(solution)/shard_map/ppermute | solution.py:12
  71.4 24.2 %collective-permute-start.9 = (bf16[1024,448]{0,1:T(8,128)(2,1)}, bf16[1024,448]{0,1:T(8,128)(2,1)S(1)}, u32[]{:S(2)}, u32[]{:S(2)}) collective-permute-start(bf16[1024,448]{0,1:T(8,128)(2,1)} %collective-permute-done.8), channel_id=1, source_target_pairs={{0,16},{16,0},{1,17},{17,1},{2,18},{18,2},{3,19},{19,3},{4,20},{20... | collective-permute-start | bytes 2752520 | tf_op jit(solution)/shard_map/ppermute | solution.py:12
  72.9 33.4 %collective-permute-start.10 = (bf16[768,448]{0,1:T(8,128)(2,1)S(1)}, bf16[768,448]{0,1:T(8,128)(2,1)S(1)}, u32[]{:S(2)}, u32[]{:S(2)}) collective-permute-start(bf16[768,448]{0,1:T(8,128)(2,1)S(1)} %constant_dynamic-slice_fusion), channel_id=1, source_target_pairs={{0,2},{2,0},{4,6},{6,4},{8,10},{10,8},{12,14},{14,12},{1,3},{3,1},... | collective-permute-start | bytes 2064392 | tf_op jit(solution)/shard_map/ppermute | solution.py:188
  99.8 38.3 %collective-permute-start.12 = (bf16[128,6144]{1,0:T(8,128)(2,1)}, bf16[128,6144]{1,0:T(8,128)(2,1)}, u32[]{:S(2)}, u32[]{:S(2)}) collective-permute-start(bf16[128,6144]{1,0:T(8,128)(2,1)} %slice.68), channel_id=1, source_target_pairs={{4,0},{6,2},{8,12},{10,14},{5,1},{7,3},{9,13},{11,15},{20,16},{22,... | collective-permute-start | bytes 4718600 | tf_op jit(solution)/shard_map/ppermute | solution.py:167
  104.2 42.7 %collective-permute-start.16 = (bf16[128,2048]{1,0:T(8,128)(2,1)}, bf16[128,2048]{1,0:T(8,128)(2,1)}, u32[]{:S(2)}, u32[]{:S(2)}) collective-permute-start(bf16[128,2048]{1,0:T(8,128)(2,1)} %slice.69), channel_id=1, source_target_pairs={{4,0},{6,2},{8,12},{10,14},{5,1},{7,3},{9,13},{11,15},{20,16},{22,... | collective-permute-start | bytes 1572872 | tf_op jit(solution)/shard_map/ppermute | solution.py:167
  106.3 14.0 %collective-permute-start.11 = (bf16[768,448]{0,1:T(8,128)(2,1)S(1)}, bf16[768,448]{0,1:T(8,128)(2,1)S(1)}, u32[]{:S(2)}, u32[]{:S(2)}) collective-permute-start(bf16[768,448]{0,1:T(8,128)(2,1)S(1)} %collective-permute-done.10), channel_id=1, source_target_pairs={{0,16},{16,0},{1,17},{17,1},{2,18},{18,2},{3,19},{19,3},{4,20},{20... | collective-permute-start | bytes 2064392 | tf_op jit(solution)/shard_map/ppermute | solution.py:12
  106.4 17.9 %slice-start = ((s8[7340032]{0:T(1024)(128)(4,1)}), s8[4194304]{0:T(1024)(128)(4,1)S(1)}, s32[]{:S(2)}) async-start(s8[7340032]{0:T(1024)(128)(4,1)} %bitcast.49), calls=%async_computation.2 | async-start | bytes 8388608
  138.2 7.7 %collective-permute-start.13 = (f32[384,896]{1,0:T(8,128)S(1)}, f32[384,896]{1,0:T(8,128)S(1)}, u32[]{:S(2)}, u32[]{:S(2)}) collective-permute-start(f32[384,896]{1,0:T(8,128)S(1)} %pad_maximum_fusion.5), channel_id=1, source_target_pairs={{1,0},{3,2},{5,4},{7,6},{8,9},{10,11},{12,13},{14,15},{17,16},{19,... | collective-permute-start | bytes 4128776 | tf_op jit(solution)/shard_map/ppermute | solution.py:173
  147.0 5.0 %copy-start.4 = (s32[128,3]{0,1:T(4,128)S(1)}, s32[128,3]{0,1:T(4,128)}, u32[]{:S(2)}) copy-start(s32[128,3]{0,1:T(4,128)} %param.14) | copy-start | bytes 4612
  147.0 13.3 %copy-start.5 = (bf16[1792]{0:T(1024)(128)(2,1)S(1)}, bf16[1792]{0:T(1024)(128)(2,1)}, u32[]{:S(2)}) copy-start(bf16[1792]{0:T(1024)(128)(2,1)} %param.12) | copy-start | bytes 10756
  149.3 25.3 %copy-start.1 = (bf16[128,1792]{1,0:T(8,128)(2,1)S(1)}, bf16[128,1792]{1,0:T(8,128)(2,1)}, u32[]{:S(2)}) copy-start(bf16[128,1792]{1,0:T(8,128)(2,1)} %param.11) | copy-start | bytes 1376260
  149.3 9.3 %collective-permute-start.17 = (f32[128,896]{1,0:T(8,128)S(1)}, f32[128,896]{1,0:T(8,128)S(1)}, u32[]{:S(2)}, u32[]{:S(2)}) collective-permute-start(f32[128,896]{1,0:T(8,128)S(1)} %fusion.34), channel_id=1, source_target_pairs={{1,0},{3,2},{5,4},{7,6},{8,9},{10,11},{12,13},{14,15},{17,16},{19,... | collective-permute-start | bytes 1376264 | tf_op jit(solution)/shard_map/ppermute | solution.py:173
  151.9 9.5 %collective-permute-start.14 = (f32[128,896]{1,0:T(8,128)}, f32[128,896]{1,0:T(8,128)}, u32[]{:S(2)}, u32[]{:S(2)}) collective-permute-start(f32[128,896]{1,0:T(8,128)} %get-tuple-element.28), channel_id=1, source_target_pairs={{0,4},{2,6},{4,0},{6,2},{9,13},{11,15},{13,9},{15,11},{16,20},{18,... | collective-permute-start | bytes 1376264 | tf_op jit(solution)/shard_map/ppermute | solution.py:176
  153.9 16.8 %collective-permute-start.15 = (f32[128,896]{1,0:T(8,128)S(1)}, f32[128,896]{1,0:T(8,128)}, u32[]{:S(2)}, u32[]{:S(2)}) collective-permute-start(f32[128,896]{1,0:T(8,128)S(1)} %get-tuple-element.29), channel_id=1, source_target_pairs={{0,8},{2,10},{13,5},{15,7},{4,12},{6,14},{9,1},{11,3},{16,24},{18,... | collective-permute-start | bytes 1376264 | tf_op jit(solution)/shard_map/ppermute | solution.py:176
  158.6 14.4 %collective-permute-start.18 = (bf16[128,896]{1,0:T(8,128)(2,1)S(1)}, bf16[128,896]{1,0:T(8,128)(2,1)S(1)}, u32[]{:S(2)}, u32[]{:S(2)}) collective-permute-start(bf16[128,896]{1,0:T(8,128)(2,1)S(1)} %add_convert_fusion), channel_id=1, source_target_pairs={{0,12},{2,14},{13,1},{15,3},{4,8},{6,10},{9,5},{11,7},{16,28},{18,... | collective-permute-start | bytes 688136 | tf_op jit(solution)/shard_map/ppermute | solution.py:176
  174.9 49.8 %slice-start.2 = ((s8[7340032]{0:T(1024)(128)(4,1)}), s8[4194304]{0:T(1024)(128)(4,1)S(1)}, s32[]{:S(2)}) async-start(s8[7340032]{0:T(1024)(128)(4,1)} %bitcast.60), calls=%async_computation.4 | async-start | bytes 8388608
  175.7 3.6 %collective-permute-start.19 = (f32[128,9]{0,1:T(8,128)S(1)}, f32[128,9]{0,1:T(8,128)S(1)}, u32[]{:S(2)}, u32[]{:S(2)}) collective-permute-start(f32[128,9]{0,1:T(8,128)S(1)} %pad_maximum_fusion.6), channel_id=1, source_target_pairs={{0,1},{1,0},{2,3},{3,2},{4,5},{5,4},{6,7},{7,6},{8,9},{9,8},{10,11... | collective-permute-start | bytes 13832 | tf_op jit(solution)/shard_map/ppermute | solution.py:12
  180.0 44.7 %slice-start.3 = ((s8[7340032]{0:T(1024)(128)(4,1)}), s8[3145728]{0:T(1024)(128)(4,1)S(1)}, s32[]{:S(2)}) async-start(s8[7340032]{0:T(1024)(128)(4,1)} %bitcast.60), calls=%async_computation.5 | async-start | bytes 6291456
  220.2 3.9 %collective-permute-start.20 = (bf16[448,1792]{1,0:T(8,128)(2,1)S(1)}, bf16[448,1792]{1,0:T(8,128)(2,1)S(1)}, u32[]{:S(2)}, u32[]{:S(2)}) collective-permute-start(bf16[448,1792]{1,0:T(8,128)(2,1)S(1)} %bitcast.51), channel_id=1, source_target_pairs={{0,1},{1,0},{2,3},{3,2},{4,5},{5,4},{6,7},{7,6},{8,9},{9,8},{10,11... | collective-permute-start | bytes 4816904 | tf_op jit(solution)/shard_map/ppermute | solution.py:12
  224.7 9.8 %slice-start.6 = ((s8[7340032]{0:T(1024)(128)(4,1)}), s8[4194304]{0:T(1024)(128)(4,1)S(1)}, s32[]{:S(2)}) async-start(s8[7340032]{0:T(1024)(128)(4,1)} %bitcast.64), calls=%async_computation.8 | async-start | bytes 8388608
  228.2 6.3 %slice-start.7 = ((s8[7340032]{0:T(1024)(128)(4,1)}), s8[3145728]{0:T(1024)(128)(4,1)S(1)}, s32[]{:S(2)}) async-start(s8[7340032]{0:T(1024)(128)(4,1)} %bitcast.64), calls=%async_computation.9 | async-start | bytes 6291456
  231.9 2.5 collective-permute-start.21
  239.2 40.9 %all-to-all-start.1 = ((bf16[8,56,1792]{2,1,0:T(8,128)(2,1)}), bf16[8,56,1792]{2,1,0:T(8,128)(2,1)S(1)}, u32[]{:S(2)}, u32[]{:S(2)}) async-start(bf16[8,56,1792]{2,1,0:T(8,128)(2,1)} %bitcast.53), calls=%async_computation.1 | async-start | bytes 3211264 | tf_op jit(solution)/shard_map/all_to_all | solution.py:251
  (5 other events, 16.4 us)

commit v5 on v4

--- a/solution.py
+++ b/solution.py
@@ -246,10 +246,15 @@
     return project(attn_out, out_weight)
 
 
-def exchange(rows, expert_total):
-    split = rows.reshape(expert_total, rows.shape[0] // expert_total, -1)
-    moved = lax.all_to_all(split, "expert", split_axis=0, concat_axis=0, tiled=True)
-    return moved.reshape(rows.shape)
+def exchange(rows, turns, expert_count):
+    split = rows.reshape(len(turns), rows.shape[0] // len(turns), -1)
+    moved = [
+        split[i]
+        if k == 0
+        else lax.ppermute(split[i], "expert", [(e, e ^ k) for e in range(expert_count)])
+        for i, k in enumerate(turns)
+    ]
+    return jnp.concatenate(moved, axis=0)
 
 
 def on_device(
@@ -291,26 +296,34 @@
     earlier = jnp.cumsum(flat_hits, axis=0) - flat_hits
     slot_rank = jnp.sum(earlier * flat_hits, axis=1).reshape(token_count, per_token)
 
-    def slots_of(low, count):
-        rank = low + jnp.arange(count, dtype=jnp.int32)
-        hit = (routes.T[None, None] == experts[:, None, None, None]) & (
+    count = -(-capacity // 8) * 8
+    expert_count = lax.axis_size("expert")
+    me = lax.axis_index("expert").astype(jnp.int32)
+
+    def slots_of(turns):
+        rank = jnp.arange(count, dtype=jnp.int32)
+        partners = me ^ jnp.asarray(turns, dtype=jnp.int32)
+        hit = (routes.T[None, None] == partners[:, None, None, None]) & (
             slot_rank.T[None, None] == rank[None, :, None, None]
         )
-        return hit.reshape(expert_total * count, per_token, token_count)
-
-    parts = [(0, -(-capacity // 8) * 8)]
+        return hit.reshape(len(turns) * count, per_token, token_count)
+
+    quarter = expert_count // 4
+    turns = list(range(expert_count))
+    parts = [
+        turns[3 * quarter :] + turns[:quarter],
+        turns[2 * quarter : 3 * quarter] + turns[quarter : 2 * quarter],
+    ]
     arrived = []
-    for low, count in parts:
-        dispatch_matrix = jnp.any(slots_of(low, count), axis=1).astype(jnp.bfloat16)
+    for part in parts:
+        dispatch_matrix = jnp.any(slots_of(part), axis=1).astype(jnp.bfloat16)
         buffer = jnp.dot(
             dispatch_matrix, normed_rows, preferred_element_type=jnp.float32
         ).astype(jnp.bfloat16)
-        arrived.append(exchange(buffer, expert_total))
-    expert_sum, out_rows = hidden, None
-    for (low, count), part in zip(parts, arrived):
-        if out_rows is not None:
-            part = lax.optimization_barrier((part, out_rows))[0]
-        slot_rows = gather_tensor(part)
+        arrived.append(exchange(buffer, part, expert_count))
+    expert_sum = hidden
+    for part, block in zip(parts, arrived):
+        slot_rows = gather_tensor(block)
         gate_part = jnp.dot(slot_rows, gate_weight[0], preferred_element_type=jnp.float32)
         up_part = jnp.dot(slot_rows, up_weight[0], preferred_element_type=jnp.float32)
         activated = (jax.nn.silu(gate_part) * up_part).astype(jnp.bfloat16)
@@ -318,10 +331,8 @@
         out_rows = jnp.dot(
             whole_units, down_weight[0], preferred_element_type=jnp.float32
         ).astype(jnp.bfloat16)
-        returned = exchange(out_rows, expert_total).astype(jnp.float32)
-        gate_matrix = jnp.sum(
-            jnp.where(slots_of(low, count), gate_values.T[None], 0.0), axis=1
-        )
+        returned = exchange(out_rows, part, expert_count).astype(jnp.float32)
+        gate_matrix = jnp.sum(jnp.where(slots_of(part), gate_values.T[None], 0.0), axis=1)
         expert_sum = expert_sum + jnp.einsum(
             "st,sd->td", gate_matrix, returned, precision=lax.Precision.HIGHEST
         )

time: 288 us -> 274 us (0.951); the launches traced: 282 us -> 273 us
  blocking collectives: 40.2 us -> 0 us
  waiting for transfers between devices: 137 us -> 154 us
  starting transfers between devices: 41 us -> 53.9 us
    ppermute x0 -> x14, waiting for transfers between devices: none -> 56.2 us  [exchange(): lax.ppermute(split[i], 'expert', [(e, e ^ k) for e in range(expert_count)])]
    all_to_all x1 -> x0, blocking collectives: 40.2 us -> none  [exchange(): lax.all_to_all(split, 'expert', split_axis=0, concat_axis=0, tiled=True)]
    all_to_all x1 -> x0, waiting for transfers between devices: 34.3 us -> none  [exchange(): lax.all_to_all(split, 'expert', split_axis=0, concat_axis=0, tiled=True)]
    ppermute x0 -> x14, starting transfers between devices: none -> 18.1 us  [exchange(): lax.ppermute(split[i], 'expert', [(e, e ^ k) for e in range(expert_count)])]
    all_to_all x1 -> x0, starting transfers between devices: 6.45 us -> none  [exchange(): lax.all_to_all(split, 'expert', split_axis=0, concat_axis=0, tiled=True)]
    ppermute x7 -> x9, waiting for transfers between devices: 38.6 us -> 33.5 us  [swap_halves(): return lax.ppermute(array, axis_name, [(0, 1), (1, 0)])]
    ppermute x7 -> x9, starting transfers between devices: 7.81 us -> 9.06 us  [swap_halves(): return lax.ppermute(array, axis_name, [(0, 1), (1, 0)])]
  transfers between devices with their start and end apart: 23 -> 38, of which waited for: 15 -> 22; matrix products, arithmetic and copies ran while one was open for 15% -> 20% of each run, Pallas kernels for 0% -> 0%
where the time goes in v5:
time: 274 us; the launch traced here: 273 us
  waiting for transfers between devices  154 us (56%)
  starting transfers between devices  53.9 us (20%)
  matrix products  34.9 us (13%)
  other arithmetic  16.1 us (6%)
  local copies, waits for them, and re-layouts  13.7 us (5%)
    ppermute x14, waiting for transfers between devices, exchange(): lax.ppermute(split[i], 'expert', [(e, e ^ k) for e in range(expert_count)])  56.2 us
    ppermute x9, waiting for transfers between devices, swap_halves(): return lax.ppermute(array, axis_name, [(0, 1), (1, 0)])  33.5 us
    ppermute x2, waiting for transfers between devices, project_line(): near = [lax.ppermute(p, 'expert', partner) for p in pieces[:2]]  22.2 us
    ppermute x14, starting transfers between devices, exchange(): lax.ppermute(split[i], 'expert', [(e, e ^ k) for e in range(expert_count)])  18.1 us
    ppermute x6, waiting for transfers between devices, hop(): return lax.ppermute(block, 'expert', chip_pairs(moves))  14.4 us
    ppermute x2, waiting for transfers between devices, project_line(): lax.ppermute(after(p, swap), 'expert', partner)  14.1 us
    ppermute x6, starting transfers between devices, hop(): return lax.ppermute(block, 'expert', chip_pairs(moves))  13.8 us
    dot_general x1, matrix products, project_line(): early = jnp.dot(blocks, columns, preferred_element_type=jnp.float32)  12 us
  transfers between devices with their start and end apart: 38, of which 22 were waited for; matrix products, arithmetic and copies ran while one was open for 20% of the time, Pallas kernels for 0%

profile of v5, /device:TPU:19, one launch (start us, length us, event | category | flops | bytes accessed | tf_op | source)
XLA Modules:
  0.0 273.0 jit_solution(10299226242882261525)
XLA Ops:
  3.2 2.7 constant_dynamic-slice_fusion.2
  7.4 22.2 %collective-permute-done.4 = bf16[1152,448]{0,1:T(8,128)(2,1)S(1)} collective-permute-done((bf16[1152,448]{0,1:T(8,128)(2,1)}, bf16[1152,448]{0,1:T(8,128)(2,1)S(1)}, u32[]{:S(2)}, u32[]{:S(2)}) %collective-permute-start.4) | collective-permute-done | bytes 1032224 | tf_op jit(solution)/shard_map/ppermute | solution.py:184
  30.8 2.2 constant_dynamic-slice_fusion.1
  33.0 13.9 %collective-permute-done = bf16[128,8192]{1,0:T(8,128)(2,1)} collective-permute-done((bf16[128,8192]{1,0:T(8,128)(2,1)}, bf16[128,8192]{1,0:T(8,128)(2,1)}, u32[]{:S(2)}, u32[]{:S(2)}) %collective-permute-start) | collective-permute-done | bytes 2097184 | tf_op jit(solution)/shard_map/ppermute | solution.py:167
  49.7 4.0 %collective-permute-start.2 = (bf16[128,8192]{1,0:T(8,128)(2,1)}, bf16[128,8192]{1,0:T(8,128)(2,1)}, u32[]{:S(2)}, u32[]{:S(2)}) collective-permute-start(bf16[128,8192]{1,0:T(8,128)(2,1)} %collective-permute-done.1), channel_id=1, source_target_pairs={{4,0},{6,2},{8,12},{10,14},{5,1},{7,3},{9,13},{11,15},{20,16},{22,... | collective-permute-start | bytes 6291464 | tf_op jit(solution)/shard_map/ppermute | solution.py:167
  57.3 14.1 %collective-permute-done.8 = bf16[1024,448]{0,1:T(8,128)(2,1)} collective-permute-done((bf16[1024,448]{0,1:T(8,128)(2,1)}, bf16[1024,448]{0,1:T(8,128)(2,1)}, u32[]{:S(2)}, u32[]{:S(2)}) %collective-permute-start.8) | collective-permute-done | bytes 917536 | tf_op jit(solution)/shard_map/ppermute | solution.py:188
  73.2 2.8 %collective-permute-done.7 = bf16[1152,448]{0,1:T(8,128)(2,1)} collective-permute-done((bf16[1152,448]{0,1:T(8,128)(2,1)S(1)}, bf16[1152,448]{0,1:T(8,128)(2,1)}, u32[]{:S(2)}, u32[]{:S(2)}) %collective-permute-start.7) | collective-permute-done | bytes 1032224 | tf_op jit(solution)/shard_map/ppermute | solution.py:12
  76.3 19.3 %collective-permute-done.9 = bf16[1024,448]{0,1:T(8,128)(2,1)S(1)} collective-permute-done((bf16[1024,448]{0,1:T(8,128)(2,1)}, bf16[1024,448]{0,1:T(8,128)(2,1)S(1)}, u32[]{:S(2)}, u32[]{:S(2)}) %collective-permute-start.9) | collective-permute-done | bytes 917536 | tf_op jit(solution)/shard_map/ppermute | solution.py:12
  97.2 2.7 slice.148
  99.9 2.5 collective-permute-start.12
  106.4 3.3 %broadcast_select_fusion.2 = bf16[128,8192]{1,0:T(8,128)(2,1)} fusion(bf16[128,8192]{1,0:T(8,128)(2,1)} %collective-permute-done.1, bf16[128,8192]{1,0:T(8,128)(2,1)} %collective-permute-done.2, pred[]{:T(512)S(6)} %or.3), kind=kLoop, calls=%fused_computation.38 | loop fusion | flops 1048576 | bytes 6291457 | tf_op jit(solution)/shard_map/jit(_where)/select_n | solution.py:206
  109.7 10.7 %collective-permute-done.11 = bf16[768,448]{0,1:T(8,128)(2,1)S(1)} collective-permute-done((bf16[768,448]{0,1:T(8,128)(2,1)S(1)}, bf16[768,448]{0,1:T(8,128)(2,1)S(1)}, u32[]{:S(2)}, u32[]{:S(2)}) %collective-permute-start.11) | collective-permute-done | bytes 688160 | tf_op jit(solution)/shard_map/ppermute | solution.py:12
  125.9 12.0 %fusion = f32[512,896]{1,0:T(8,128)S(1)} fusion(bf16[8192,448]{0,1:T(8,128)(2,1)S(1)} %get-tuple-element.27, bf16[8192,448]{0,1:T(8,128)(2,1)S(1)} %get-tuple-element.26, bf16[128,8192]{1,0:T(8,128)(2,1)} %collective-permute-done.3, bf16[128,8192]{1,0:T(8,128)(2,1)S(1)} %copy-done.2, bf16[128,8192]{1,0:T(8,128)(2,1)} %collective-permute-done, ...), kind=kOutput, calls=%fused_computation.5 | convolution fusion | flops 7579107328 | bytes 24903680 | tf_op jit(solution)/shard_map/dot_general | solution.py:208
  139.5 5.1 %fusion.34 = f32[128,896]{1,0:T(8,128)S(1)} fusion(bf16[128,6144]{1,0:T(8,128)(2,1)} %collective-permute-done.12, bf16[8192,448]{0,1:T(8,128)(2,1)S(1)} %get-tuple-element.26, bf16[8192,448]{0,1:T(8,128)(2,1)S(1)} %get-tuple-element.27), kind=kOutput, calls=%fused_computation.42 | convolution fusion | flops 1431306240 | bytes 16711680 | tf_op jit(solution)/shard_map/dot_general | solution.py:217
  147.0 2.4 fusion.40
  153.4 4.7 %collective-permute-start.15 = (f32[128,896]{1,0:T(8,128)S(1)}, f32[128,896]{1,0:T(8,128)}, u32[]{:S(2)}, u32[]{:S(2)}) collective-permute-start(f32[128,896]{1,0:T(8,128)S(1)} %get-tuple-element.31), channel_id=1, source_target_pairs={{0,8},{2,10},{13,5},{15,7},{4,12},{6,14},{9,1},{11,3},{16,24},{18,... | collective-permute-start | bytes 1376264 | tf_op jit(solution)/shard_map/ppermute | solution.py:176
  161.0 9.2 %collective-permute-done.15 = f32[128,896]{1,0:T(8,128)} collective-permute-done((f32[128,896]{1,0:T(8,128)S(1)}, f32[128,896]{1,0:T(8,128)}, u32[]{:S(2)}, u32[]{:S(2)}) %collective-permute-start.15) | collective-permute-done | bytes 458784 | tf_op jit(solution)/shard_map/ppermute | solution.py:176
  170.2 2.6 collective-permute-done.18
  175.4 2.7 collective-permute-start.19
  180.0 3.3 %collective-permute-start.29 = (bf16[56,1792]{1,0:T(8,128)(2,1)S(1)}, bf16[56,1792]{1,0:T(8,128)(2,1)S(1)}, u32[]{:S(2)}, u32[]{:S(2)}) collective-permute-start(bf16[56,1792]{1,0:T(8,128)(2,1)S(1)} %get-tuple-element.54), channel_id=1, source_target_pairs={{0,10},{2,8},{4,14},{6,12},{8,2},{10,0},{12,6},{14,4},{1,11},{3,9}... | collective-permute-start | bytes 602120 | tf_op jit(solution)/shard_map/ppermute | solution.py:254
  184.8 8.2 %collective-permute-done.28 = bf16[56,1792]{1,0:T(8,128)(2,1)S(1)} collective-permute-done((bf16[56,1792]{1,0:T(8,128)(2,1)S(1)}, bf16[56,1792]{1,0:T(8,128)(2,1)S(1)}, u32[]{:S(2)}, u32[]{:S(2)}) %collective-permute-start.28) | collective-permute-done | bytes 200736 | tf_op jit(solution)/shard_map/ppermute | solution.py:254
  193.0 4.3 %collective-permute-done.29 = bf16[56,1792]{1,0:T(8,128)(2,1)S(1)} collective-permute-done((bf16[56,1792]{1,0:T(8,128)(2,1)S(1)}, bf16[56,1792]{1,0:T(8,128)(2,1)S(1)}, u32[]{:S(2)}, u32[]{:S(2)}) %collective-permute-start.29) | collective-permute-done | bytes 200736 | tf_op jit(solution)/shard_map/ppermute | solution.py:254
  200.4 2.1 collective-permute-start.20
  203.9 12.5 %collective-permute-done.20 = bf16[56,1792]{1,0:T(8,128)(2,1)S(1)} collective-permute-done((bf16[56,1792]{1,0:T(8,128)(2,1)S(1)}, bf16[56,1792]{1,0:T(8,128)(2,1)S(1)}, u32[]{:S(2)}, u32[]{:S(2)}) %collective-permute-start.20) | collective-permute-done | bytes 200736 | tf_op jit(solution)/shard_map/ppermute | solution.py:254
  216.4 4.3 %collective-permute-done.21 = bf16[56,1792]{1,0:T(8,128)(2,1)S(1)} collective-permute-done((bf16[56,1792]{1,0:T(8,128)(2,1)S(1)}, bf16[56,1792]{1,0:T(8,128)(2,1)S(1)}, u32[]{:S(2)}, u32[]{:S(2)}) %collective-permute-start.21) | collective-permute-done | bytes 200736 | tf_op jit(solution)/shard_map/ppermute | solution.py:254
  233.6 3.3 %collective-permute-start.35 = (bf16[56,1792]{1,0:T(8,128)(2,1)S(1)}, bf16[56,1792]{1,0:T(8,128)(2,1)S(1)}, u32[]{:S(2)}, u32[]{:S(2)}) collective-permute-start(bf16[56,1792]{1,0:T(8,128)(2,1)S(1)} %get-tuple-element.51), channel_id=1, source_target_pairs={{0,10},{2,8},{4,14},{6,12},{8,2},{10,0},{12,6},{14,4},{1,11},{3,9}... | collective-permute-start | bytes 602120 | tf_op jit(solution)/shard_map/ppermute | solution.py:254
  238.4 2.1 fusion.26
  242.1 4.7 %collective-permute-done.34 = bf16[56,1792]{1,0:T(8,128)(2,1)S(1)} collective-permute-done((bf16[56,1792]{1,0:T(8,128)(2,1)S(1)}, bf16[56,1792]{1,0:T(8,128)(2,1)S(1)}, u32[]{:S(2)}, u32[]{:S(2)}) %collective-permute-start.34) | collective-permute-done | bytes 200736 | tf_op jit(solution)/shard_map/ppermute | solution.py:254
  246.9 2.4 collective-permute-start.26
  252.4 2.9 %collective-permute-done.37 = bf16[56,1792]{1,0:T(8,128)(2,1)S(1)} collective-permute-done((bf16[56,1792]{1,0:T(8,128)(2,1)S(1)}, bf16[56,1792]{1,0:T(8,128)(2,1)S(1)}, u32[]{:S(2)}, u32[]{:S(2)}) %collective-permute-start.37) | collective-permute-done | bytes 200736 | tf_op jit(solution)/shard_map/ppermute | solution.py:254
  255.9 10.4 %collective-permute-done.25 = bf16[56,1792]{1,0:T(8,128)(2,1)S(1)} collective-permute-done((bf16[56,1792]{1,0:T(8,128)(2,1)S(1)}, bf16[56,1792]{1,0:T(8,128)(2,1)S(1)}, u32[]{:S(2)}, u32[]{:S(2)}) %collective-permute-start.25) | collective-permute-done | bytes 200736 | tf_op jit(solution)/shard_map/ppermute | solution.py:254
  266.3 5.2 %collective-permute-done.26 = bf16[56,1792]{1,0:T(8,128)(2,1)S(1)} collective-permute-done((bf16[56,1792]{1,0:T(8,128)(2,1)S(1)}, bf16[56,1792]{1,0:T(8,128)(2,1)S(1)}, u32[]{:S(2)}, u32[]{:S(2)}) %collective-permute-start.26) | collective-permute-done | bytes 200736 | tf_op jit(solution)/shard_map/ppermute | solution.py:254
  (158 shorter events, 67.9 us)
Async XLA Ops:
  0.0 46.8 %collective-permute-start = (bf16[128,8192]{1,0:T(8,128)(2,1)}, bf16[128,8192]{1,0:T(8,128)(2,1)}, u32[]{:S(2)}, u32[]{:S(2)}) collective-permute-start(bf16[128,8192]{1,0:T(8,128)(2,1)} %param.13), channel_id=1, source_target_pairs={{0,4},{2,6},{4,0},{6,2},{8,12},{10,14},{12,8},{14,10},{1,5},{3,7},... | collective-permute-start | bytes 6291464 | tf_op jit(solution)/shard_map/ppermute | solution.py:167
  1.3 48.4 %collective-permute-start.1 = (bf16[128,8192]{1,0:T(8,128)(2,1)}, bf16[128,8192]{1,0:T(8,128)(2,1)}, u32[]{:S(2)}, u32[]{:S(2)}) collective-permute-start(bf16[128,8192]{1,0:T(8,128)(2,1)} %param.13), channel_id=1, source_target_pairs={{4,8},{6,10},{8,4},{10,6},{5,9},{7,11},{9,5},{11,7},{20,24},{22,26... | collective-permute-start | bytes 6291464 | tf_op jit(solution)/shard_map/ppermute | solution.py:167
  5.9 23.7 %collective-permute-start.4 = (bf16[1152,448]{0,1:T(8,128)(2,1)}, bf16[1152,448]{0,1:T(8,128)(2,1)S(1)}, u32[]{:S(2)}, u32[]{:S(2)}) collective-permute-start(bf16[1152,448]{0,1:T(8,128)(2,1)} %get-tuple-element.29), channel_id=1, source_target_pairs={{0,2},{2,0},{4,6},{6,4},{8,10},{10,8},{12,14},{14,12},{1,3},{3,1},... | collective-permute-start | bytes 3096584 | tf_op jit(solution)/shard_map/ppermute | solution.py:184
  6.2 47.5 %collective-permute-start.6 = (bf16[1152,448]{0,1:T(8,128)(2,1)S(1)}, bf16[1152,448]{0,1:T(8,128)(2,1)S(1)}, u32[]{:S(2)}, u32[]{:S(2)}) collective-permute-start(bf16[1152,448]{0,1:T(8,128)(2,1)S(1)} %get-tuple-element.28), channel_id=1, source_target_pairs={{0,2},{2,0},{4,6},{6,4},{8,10},{10,8},{12,14},{14,12},{1,3},{3,1},... | collective-permute-start | bytes 3096584 | tf_op jit(solution)/shard_map/ppermute | solution.py:184
  29.6 43.0 %collective-permute-start.5 = (bf16[1152,448]{0,1:T(8,128)(2,1)S(1)}, bf16[1152,448]{0,1:T(8,128)(2,1)}, u32[]{:S(2)}, u32[]{:S(2)}) collective-permute-start(bf16[1152,448]{0,1:T(8,128)(2,1)S(1)} %collective-permute-done.4), channel_id=1, source_target_pairs={{0,16},{16,0},{1,17},{17,1},{2,18},{18,2},{3,19},{19,3},{4,20},{20... | collective-permute-start | bytes 3096584 | tf_op jit(solution)/shard_map/ppermute | solution.py:12
  46.8 24.5 %collective-permute-start.8 = (bf16[1024,448]{0,1:T(8,128)(2,1)}, bf16[1024,448]{0,1:T(8,128)(2,1)}, u32[]{:S(2)}, u32[]{:S(2)}) collective-permute-start(bf16[1024,448]{0,1:T(8,128)(2,1)} %constant_dynamic-slice_fusion.1), channel_id=1, source_target_pairs={{0,2},{2,0},{4,6},{6,4},{8,10},{10,8},{12,14},{14,12},{1,3},{3,1},... | collective-permute-start | bytes 2752520 | tf_op jit(solution)/shard_map/ppermute | solution.py:188
  47.1 50.1 %collective-permute-start.3 = (bf16[128,8192]{1,0:T(8,128)(2,1)}, bf16[128,8192]{1,0:T(8,128)(2,1)}, u32[]{:S(2)}, u32[]{:S(2)}) collective-permute-start(bf16[128,8192]{1,0:T(8,128)(2,1)} %collective-permute-done), channel_id=1, source_target_pairs={{4,8},{6,10},{8,4},{10,6},{5,9},{7,11},{9,5},{11,7},{20,24},{22,26... | collective-permute-start | bytes 6291464 | tf_op jit(solution)/shard_map/ppermute | solution.py:167
  49.7 56.7 %collective-permute-start.2 = (bf16[128,8192]{1,0:T(8,128)(2,1)}, bf16[128,8192]{1,0:T(8,128)(2,1)}, u32[]{:S(2)}, u32[]{:S(2)}) collective-permute-start(bf16[128,8192]{1,0:T(8,128)(2,1)} %collective-permute-done.1), channel_id=1, source_target_pairs={{4,0},{6,2},{8,12},{10,14},{5,1},{7,3},{9,13},{11,15},{20,16},{22,... | collective-permute-start | bytes 6291464 | tf_op jit(solution)/shard_map/ppermute | solution.py:167
  53.7 22.3 %collective-permute-start.7 = (bf16[1152,448]{0,1:T(8,128)(2,1)S(1)}, bf16[1152,448]{0,1:T(8,128)(2,1)}, u32[]{:S(2)}, u32[]{:S(2)}) collective-permute-start(bf16[1152,448]{0,1:T(8,128)(2,1)S(1)} %collective-permute-done.6), channel_id=1, source_target_pairs={{0,16},{16,0},{1,17},{17,1},{2,18},{18,2},{3,19},{19,3},{4,20},{20... | collective-permute-start | bytes 3096584 | tf_op jit(solution)/shard_map/ppermute | solution.py:12
  71.4 24.3 %collective-permute-start.9 = (bf16[1024,448]{0,1:T(8,128)(2,1)}, bf16[1024,448]{0,1:T(8,128)(2,1)S(1)}, u32[]{:S(2)}, u32[]{:S(2)}) collective-permute-start(bf16[1024,448]{0,1:T(8,128)(2,1)} %collective-permute-done.8), channel_id=1, source_target_pairs={{0,16},{16,0},{1,17},{17,1},{2,18},{18,2},{3,19},{19,3},{4,20},{20... | collective-permute-start | bytes 2752520 | tf_op jit(solution)/shard_map/ppermute | solution.py:12
  72.9 33.4 %collective-permute-start.10 = (bf16[768,448]{0,1:T(8,128)(2,1)S(1)}, bf16[768,448]{0,1:T(8,128)(2,1)S(1)}, u32[]{:S(2)}, u32[]{:S(2)}) collective-permute-start(bf16[768,448]{0,1:T(8,128)(2,1)S(1)} %constant_dynamic-slice_fusion), channel_id=1, source_target_pairs={{0,2},{2,0},{4,6},{6,4},{8,10},{10,8},{12,14},{14,12},{1,3},{3,1},... | collective-permute-start | bytes 2064392 | tf_op jit(solution)/shard_map/ppermute | solution.py:188
  99.9 38.3 %collective-permute-start.12 = (bf16[128,6144]{1,0:T(8,128)(2,1)}, bf16[128,6144]{1,0:T(8,128)(2,1)}, u32[]{:S(2)}, u32[]{:S(2)}) collective-permute-start(bf16[128,6144]{1,0:T(8,128)(2,1)} %slice.148), channel_id=1, source_target_pairs={{4,0},{6,2},{8,12},{10,14},{5,1},{7,3},{9,13},{11,15},{20,16},{22,... | collective-permute-start | bytes 4718600 | tf_op jit(solution)/shard_map/ppermute | solution.py:167
  104.2 42.8 %collective-permute-start.16 = (bf16[128,2048]{1,0:T(8,128)(2,1)}, bf16[128,2048]{1,0:T(8,128)(2,1)}, u32[]{:S(2)}, u32[]{:S(2)}) collective-permute-start(bf16[128,2048]{1,0:T(8,128)(2,1)} %slice.149), channel_id=1, source_target_pairs={{4,0},{6,2},{8,12},{10,14},{5,1},{7,3},{9,13},{11,15},{20,16},{22,... | collective-permute-start | bytes 1572872 | tf_op jit(solution)/shard_map/ppermute | solution.py:167
  106.3 14.0 %collective-permute-start.11 = (bf16[768,448]{0,1:T(8,128)(2,1)S(1)}, bf16[768,448]{0,1:T(8,128)(2,1)S(1)}, u32[]{:S(2)}, u32[]{:S(2)}) collective-permute-start(bf16[768,448]{0,1:T(8,128)(2,1)S(1)} %collective-permute-done.10), channel_id=1, source_target_pairs={{0,16},{16,0},{1,17},{17,1},{2,18},{18,2},{3,19},{19,3},{4,20},{20... | collective-permute-start | bytes 2064392 | tf_op jit(solution)/shard_map/ppermute | solution.py:12
  151.4 9.5 %collective-permute-start.14 = (f32[128,896]{1,0:T(8,128)}, f32[128,896]{1,0:T(8,128)}, u32[]{:S(2)}, u32[]{:S(2)}) collective-permute-start(f32[128,896]{1,0:T(8,128)} %get-tuple-element.30), channel_id=1, source_target_pairs={{0,4},{2,6},{4,0},{6,2},{9,13},{11,15},{13,9},{15,11},{16,20},{18,... | collective-permute-start | bytes 1376264 | tf_op jit(solution)/shard_map/ppermute | solution.py:176
  153.4 16.8 %collective-permute-start.15 = (f32[128,896]{1,0:T(8,128)S(1)}, f32[128,896]{1,0:T(8,128)}, u32[]{:S(2)}, u32[]{:S(2)}) collective-permute-start(f32[128,896]{1,0:T(8,128)S(1)} %get-tuple-element.31), channel_id=1, source_target_pairs={{0,8},{2,10},{13,5},{15,7},{4,12},{6,14},{9,1},{11,3},{16,24},{18,... | collective-permute-start | bytes 1376264 | tf_op jit(solution)/shard_map/ppermute | solution.py:176
  158.8 13.9 %collective-permute-start.18 = (bf16[128,896]{1,0:T(8,128)(2,1)}, bf16[128,896]{1,0:T(8,128)(2,1)S(1)}, u32[]{:S(2)}, u32[]{:S(2)}) collective-permute-start(bf16[128,896]{1,0:T(8,128)(2,1)} %add_convert_fusion), channel_id=1, source_target_pairs={{0,12},{2,14},{13,1},{15,3},{4,8},{6,10},{9,5},{11,7},{16,28},{18,... | collective-permute-start | bytes 688136 | tf_op jit(solution)/shard_map/ppermute | solution.py:176
  179.9 13.1 %collective-permute-start.28 = (bf16[56,1792]{1,0:T(8,128)(2,1)S(1)}, bf16[56,1792]{1,0:T(8,128)(2,1)S(1)}, u32[]{:S(2)}, u32[]{:S(2)}) collective-permute-start(bf16[56,1792]{1,0:T(8,128)(2,1)S(1)} %get-tuple-element.55), channel_id=1, source_target_pairs={{0,8},{2,10},{4,12},{6,14},{8,0},{10,2},{12,4},{14,6},{1,9},{3,11}... | collective-permute-start | bytes 602120 | tf_op jit(solution)/shard_map/ppermute | solution.py:254
  180.0 17.3 %collective-permute-start.29 = (bf16[56,1792]{1,0:T(8,128)(2,1)S(1)}, bf16[56,1792]{1,0:T(8,128)(2,1)S(1)}, u32[]{:S(2)}, u32[]{:S(2)}) collective-permute-start(bf16[56,1792]{1,0:T(8,128)(2,1)S(1)} %get-tuple-element.54), channel_id=1, source_target_pairs={{0,10},{2,8},{4,14},{6,12},{8,2},{10,0},{12,6},{14,4},{1,11},{3,9}... | collective-permute-start | bytes 602120 | tf_op jit(solution)/shard_map/ppermute | solution.py:254
  183.4 14.0 %collective-permute-start.30 = (bf16[56,1792]{1,0:T(8,128)(2,1)S(1)}, bf16[56,1792]{1,0:T(8,128)(2,1)S(1)}, u32[]{:S(2)}, u32[]{:S(2)}) collective-permute-start(bf16[56,1792]{1,0:T(8,128)(2,1)S(1)} %get-tuple-element.53), channel_id=1, source_target_pairs={{0,4},{2,6},{4,0},{6,2},{8,12},{10,14},{12,8},{14,10},{1,5},{3,7},... | collective-permute-start | bytes 602120 | tf_op jit(solution)/shard_map/ppermute | solution.py:254
  183.4 15.8 %collective-permute-start.31 = (bf16[56,1792]{1,0:T(8,128)(2,1)S(1)}, bf16[56,1792]{1,0:T(8,128)(2,1)S(1)}, u32[]{:S(2)}, u32[]{:S(2)}) collective-permute-start(bf16[56,1792]{1,0:T(8,128)(2,1)S(1)} %get-tuple-element.52), channel_id=1, source_target_pairs={{0,6},{2,4},{4,2},{6,0},{8,14},{10,12},{12,10},{14,8},{1,7},{3,5},... | collective-permute-start | bytes 602120 | tf_op jit(solution)/shard_map/ppermute | solution.py:254
  199.2 22.3 %collective-permute-start.32 = (bf16[224,1792]{1,0:T(8,128)(2,1)S(1)}, bf16[224,1792]{1,0:T(8,128)(2,1)S(1)}, u32[]{:S(2)}, u32[]{:S(2)}) collective-permute-start(bf16[224,1792]{1,0:T(8,128)(2,1)S(1)} %constant_dynamic-update-slice_fusion), channel_id=1, source_target_pairs={{0,1},{1,0},{2,3},{3,2},{4,5},{5,4},{6,7},{7,6},{8,9},{9,8},{10,11... | collective-permute-start | bytes 2408456 | tf_op jit(solution)/shard_map/ppermute | solution.py:12
  200.4 16.0 %collective-permute-start.20 = (bf16[56,1792]{1,0:T(8,128)(2,1)S(1)}, bf16[56,1792]{1,0:T(8,128)(2,1)S(1)}, u32[]{:S(2)}, u32[]{:S(2)}) collective-permute-start(bf16[56,1792]{1,0:T(8,128)(2,1)S(1)} %get-tuple-element.44), channel_id=1, source_target_pairs={{0,12},{2,14},{4,8},{6,10},{8,4},{10,6},{12,0},{14,2},{1,13},{3,15... | collective-permute-start | bytes 602120 | tf_op jit(solution)/shard_map/ppermute | solution.py:254
  202.5 18.1 %collective-permute-start.21 = (bf16[56,1792]{1,0:T(8,128)(2,1)S(1)}, bf16[56,1792]{1,0:T(8,128)(2,1)S(1)}, u32[]{:S(2)}, u32[]{:S(2)}) collective-permute-start(bf16[56,1792]{1,0:T(8,128)(2,1)S(1)} %get-tuple-element.47), channel_id=1, source_target_pairs={{0,14},{2,12},{4,10},{6,8},{8,6},{10,4},{12,2},{14,0},{1,15},{3,13... | collective-permute-start | bytes 602120 | tf_op jit(solution)/shard_map/ppermute | solution.py:254
  202.6 18.1 %collective-permute-start.22 = (bf16[56,1792]{1,0:T(8,128)(2,1)S(1)}, bf16[56,1792]{1,0:T(8,128)(2,1)S(1)}, u32[]{:S(2)}, u32[]{:S(2)}) collective-permute-start(bf16[56,1792]{1,0:T(8,128)(2,1)S(1)} %get-tuple-element.45), channel_id=1, source_target_pairs={{0,2},{2,0},{4,6},{6,4},{8,10},{10,8},{12,14},{14,12},{1,3},{3,1},... | collective-permute-start | bytes 602120 | tf_op jit(solution)/shard_map/ppermute | solution.py:254
  233.6 13.3 %collective-permute-start.34 = (bf16[56,1792]{1,0:T(8,128)(2,1)S(1)}, bf16[56,1792]{1,0:T(8,128)(2,1)S(1)}, u32[]{:S(2)}, u32[]{:S(2)}) collective-permute-start(bf16[56,1792]{1,0:T(8,128)(2,1)S(1)} %get-tuple-element.48), channel_id=1, source_target_pairs={{0,8},{2,10},{4,12},{6,14},{8,0},{10,2},{12,4},{14,6},{1,9},{3,11}... | collective-permute-start | bytes 602120 | tf_op jit(solution)/shard_map/ppermute | solution.py:254
  233.6 17.5 %collective-permute-start.35 = (bf16[56,1792]{1,0:T(8,128)(2,1)S(1)}, bf16[56,1792]{1,0:T(8,128)(2,1)S(1)}, u32[]{:S(2)}, u32[]{:S(2)}) collective-permute-start(bf16[56,1792]{1,0:T(8,128)(2,1)S(1)} %get-tuple-element.51), channel_id=1, source_target_pairs={{0,10},{2,8},{4,14},{6,12},{8,2},{10,0},{12,6},{14,4},{1,11},{3,9}... | collective-permute-start | bytes 602120 | tf_op jit(solution)/shard_map/ppermute | solution.py:254
  236.9 15.5 %collective-permute-start.36 = (bf16[56,1792]{1,0:T(8,128)(2,1)S(1)}, bf16[56,1792]{1,0:T(8,128)(2,1)S(1)}, u32[]{:S(2)}, u32[]{:S(2)}) collective-permute-start(bf16[56,1792]{1,0:T(8,128)(2,1)S(1)} %get-tuple-element.50), channel_id=1, source_target_pairs={{0,4},{2,6},{4,0},{6,2},{8,12},{10,14},{12,8},{14,10},{1,5},{3,7},... | collective-permute-start | bytes 602120 | tf_op jit(solution)/shard_map/ppermute | solution.py:254
  237.3 18.0 %collective-permute-start.37 = (bf16[56,1792]{1,0:T(8,128)(2,1)S(1)}, bf16[56,1792]{1,0:T(8,128)(2,1)S(1)}, u32[]{:S(2)}, u32[]{:S(2)}) collective-permute-start(bf16[56,1792]{1,0:T(8,128)(2,1)S(1)} %get-tuple-element.49), channel_id=1, source_target_pairs={{0,6},{2,4},{4,2},{6,0},{8,14},{10,12},{12,10},{14,8},{1,7},{3,5},... | collective-permute-start | bytes 602120 | tf_op jit(solution)/shard_map/ppermute | solution.py:254
  240.6 25.7 %collective-permute-start.25 = (bf16[56,1792]{1,0:T(8,128)(2,1)S(1)}, bf16[56,1792]{1,0:T(8,128)(2,1)S(1)}, u32[]{:S(2)}, u32[]{:S(2)}) collective-permute-start(bf16[56,1792]{1,0:T(8,128)(2,1)S(1)} %get-tuple-element.40), channel_id=1, source_target_pairs={{0,12},{2,14},{4,8},{6,10},{8,4},{10,6},{12,0},{14,2},{1,13},{3,15... | collective-permute-start | bytes 602120 | tf_op jit(solution)/shard_map/ppermute | solution.py:254
  246.9 24.6 %collective-permute-start.26 = (bf16[56,1792]{1,0:T(8,128)(2,1)S(1)}, bf16[56,1792]{1,0:T(8,128)(2,1)S(1)}, u32[]{:S(2)}, u32[]{:S(2)}) collective-permute-start(bf16[56,1792]{1,0:T(8,128)(2,1)S(1)} %get-tuple-element.43), channel_id=1, source_target_pairs={{0,14},{2,12},{4,10},{6,8},{8,6},{10,4},{12,2},{14,0},{1,15},{3,13... | collective-permute-start | bytes 602120 | tf_op jit(solution)/shard_map/ppermute | solution.py:254
  251.2 20.4 %collective-permute-start.27 = (bf16[56,1792]{1,0:T(8,128)(2,1)S(1)}, bf16[56,1792]{1,0:T(8,128)(2,1)S(1)}, u32[]{:S(2)}, u32[]{:S(2)}) collective-permute-start(bf16[56,1792]{1,0:T(8,128)(2,1)S(1)} %get-tuple-element.41), channel_id=1, source_target_pairs={{0,2},{2,0},{4,6},{6,4},{8,10},{10,8},{12,14},{14,12},{1,3},{3,1},... | collective-permute-start | bytes 602120 | tf_op jit(solution)/shard_map/ppermute | solution.py:254
  (25 other events, 464.3 us)

commit v6 on v5

--- a/solution.py
+++ b/solution.py
@@ -158,7 +158,7 @@
     rows, depth = attn_out.shape
     half = depth // 2
     unit = half // 32
-    bounds = [0, 9 * unit, 18 * unit, 26 * unit, half]
+    bounds = [0, 9 * unit, 18 * unit, 25 * unit, half]
     middle = (place == 1) | (place == 2)
     partner = [(i, i ^ 1) for i in range(8)]
     to_owner = [(2 * e + 1 - e // 4, 2 * e + e // 4) for e in range(8)]
@@ -216,8 +216,10 @@
     )
     last = jnp.dot(out_far[0], columns[:most], preferred_element_type=jnp.float32)
     out_far[1] = after(out_far[1], (swap_sum, cross_sum, last))
-    swap_sum = give_back(swap_sum, SWAP)
-    cross_sum = give_back(cross_sum, ((0, 2), (3, 1), (1, 3), (2, 0)))
+    swap_sum = give_back(swap_sum.astype(jnp.bfloat16), SWAP).astype(jnp.float32)
+    cross_sum = give_back(
+        cross_sum.astype(jnp.bfloat16), ((0, 2), (3, 1), (1, 3), (2, 0))
+    ).astype(jnp.float32)
     last = last + jnp.dot(out_far[1], columns[most:], preferred_element_type=jnp.float32)
     last = jnp.where(middle, third, last)
     last = (last + to_owners(last)).astype(jnp.bfloat16)

time: 274 us -> 267 us (0.974)
  waiting for transfers between devices: 154 us -> 149 us
    ppermute x3, waiting for transfers between devices: 11.9 us -> 6.18 us  [give_back(): return lax.ppermute(block, ('expert', 'tensor'), core_pairs(moves))]
    dynamic_slice x3 -> x2, local copies, waits for them, and re-layouts: 5.96 us -> 4.37 us  [project_line(): lax.dynamic_slice_in_dim(out_weight, group * half + lo, hi - lo, 0)]
  transfers between devices with their start and end apart: 38 -> 38, of which waited for: 22 -> 20; matrix products, arithmetic and copies ran while one was open for 20% -> 20% of each run, Pallas kernels for 0% -> 0%
where the time goes in v6:
time: 267 us
  waiting for transfers between devices  149 us (56%)
  starting transfers between devices  53.9 us (20%)
  matrix products  35.3 us (13%)
  other arithmetic  15.9 us (6%)
  local copies, waits for them, and re-layouts  11.6 us (4%)
    ppermute x14, waiting for transfers between devices, exchange(): lax.ppermute(split[i], 'expert', [(e, e ^ k) for e in range(expert_count)])  56.9 us
    ppermute x9, waiting for transfers between devices, swap_halves(): return lax.ppermute(array, axis_name, [(0, 1), (1, 0)])  36.1 us
    ppermute x2, waiting for transfers between devices, project_line(): near = [lax.ppermute(p, 'expert', partner) for p in pieces[:2]]  22 us
    ppermute x14, starting transfers between devices, exchange(): lax.ppermute(split[i], 'expert', [(e, e ^ k) for e in range(expert_count)])  17.5 us
    ppermute x6, waiting for transfers between devices, hop(): return lax.ppermute(block, 'expert', chip_pairs(moves))  15 us
    ppermute x6, starting transfers between devices, hop(): return lax.ppermute(block, 'expert', chip_pairs(moves))  13.8 us
    dot_general x1, matrix products, project_line(): early = jnp.dot(blocks, columns, preferred_element_type=jnp.float32)  12 us
    ppermute x2, waiting for transfers between devices, project_line(): lax.ppermute(after(p, swap), 'expert', partner)  11.7 us
  transfers between devices with their start and end apart: 38, of which 20 were waited for; matrix products, arithmetic and copies ran while one was open for 20% of the time, Pallas kernels for 0%

profile of v6, /device:TPU:19, one launch (start us, length us, event | category | flops | bytes accessed | tf_op | source)
XLA Modules:
  0.0 266.6 jit_solution(10400970682959104778)
XLA Ops:
  6.5 22.0 %collective-permute-done.4 = bf16[1152,448]{0,1:T(8,128)(2,1)S(1)} collective-permute-done((bf16[1152,448]{0,1:T(8,128)(2,1)S(1)}, bf16[1152,448]{0,1:T(8,128)(2,1)S(1)}, u32[]{:S(2)}, u32[]{:S(2)}) %collective-permute-start.4) | collective-permute-done | bytes 1032224 | tf_op jit(solution)/shard_map/ppermute | solution.py:184
  29.7 2.7 %constant_dynamic-slice_fusion = (bf16[896,448]{0,1:T(8,128)(2,1)}, bf16[896,448]{0,1:T(8,128)(2,1)}) fusion(bf16[8192,448]{0,1:T(8,128)(2,1)} %param.14, s32[]{:T(128)S(6)} %select_n.204, s32[]{:T(128)S(6)} %select_n.202), kind=kLoop, calls=%fused_computation.134 | loop fusion | bytes 3211272 | tf_op jit(solution)/shard_map/dynamic_slice | solution.py:179
  32.4 14.4 %collective-permute-done = bf16[128,8192]{1,0:T(8,128)(2,1)} collective-permute-done((bf16[128,8192]{1,0:T(8,128)(2,1)}, bf16[128,8192]{1,0:T(8,128)(2,1)}, u32[]{:S(2)}, u32[]{:S(2)}) %collective-permute-start) | collective-permute-done | bytes 2097184 | tf_op jit(solution)/shard_map/ppermute | solution.py:167
  49.7 4.0 %collective-permute-start.2 = (bf16[128,8192]{1,0:T(8,128)(2,1)}, bf16[128,8192]{1,0:T(8,128)(2,1)}, u32[]{:S(2)}, u32[]{:S(2)}) collective-permute-start(bf16[128,8192]{1,0:T(8,128)(2,1)} %collective-permute-done.1), channel_id=1, source_target_pairs={{4,0},{6,2},{8,12},{10,14},{5,1},{7,3},{9,13},{11,15},{20,16},{22,... | collective-permute-start | bytes 6291464 | tf_op jit(solution)/shard_map/ppermute | solution.py:167
  56.1 11.7 %collective-permute-done.8 = bf16[896,448]{0,1:T(8,128)(2,1)} collective-permute-done((bf16[896,448]{0,1:T(8,128)(2,1)}, bf16[896,448]{0,1:T(8,128)(2,1)}, u32[]{:S(2)}, u32[]{:S(2)}) %collective-permute-start.8) | collective-permute-done | bytes 802848 | tf_op jit(solution)/shard_map/ppermute | solution.py:188
  69.7 6.3 %collective-permute-done.7 = bf16[1152,448]{0,1:T(8,128)(2,1)} collective-permute-done((bf16[1152,448]{0,1:T(8,128)(2,1)S(1)}, bf16[1152,448]{0,1:T(8,128)(2,1)}, u32[]{:S(2)}, u32[]{:S(2)}) %collective-permute-start.7) | collective-permute-done | bytes 1032224 | tf_op jit(solution)/shard_map/ppermute | solution.py:12
  76.3 16.9 %collective-permute-done.9 = bf16[896,448]{0,1:T(8,128)(2,1)S(1)} collective-permute-done((bf16[896,448]{0,1:T(8,128)(2,1)}, bf16[896,448]{0,1:T(8,128)(2,1)S(1)}, u32[]{:S(2)}, u32[]{:S(2)}) %collective-permute-start.9) | collective-permute-done | bytes 802848 | tf_op jit(solution)/shard_map/ppermute | solution.py:12
  94.6 2.7 %slice.148 = bf16[128,6144]{1,0:T(8,128)(2,1)} slice(bf16[128,8192]{1,0:T(8,128)(2,1)} %collective-permute-done.3), slice={[0:128], [0:6144]} | slice | bytes 3145728 | tf_op jit(solution)/shard_map/slice | solution.py:191
  97.3 2.5 collective-permute-start.12
  101.7 2.1 collective-permute-start.16
  105.0 3.1 %broadcast_select_fusion.2 = bf16[128,8192]{1,0:T(8,128)(2,1)} fusion(bf16[128,8192]{1,0:T(8,128)(2,1)} %collective-permute-done.1, bf16[128,8192]{1,0:T(8,128)(2,1)} %collective-permute-done.2, pred[]{:T(512)S(6)} %or.3), kind=kLoop, calls=%fused_computation.38 | loop fusion | flops 1048576 | bytes 6291457 | tf_op jit(solution)/shard_map/jit(_where)/select_n | solution.py:206
  108.1 12.1 %collective-permute-done.11 = bf16[896,448]{0,1:T(8,128)(2,1)S(1)} collective-permute-done((bf16[896,448]{0,1:T(8,128)(2,1)S(1)}, bf16[896,448]{0,1:T(8,128)(2,1)S(1)}, u32[]{:S(2)}, u32[]{:S(2)}) %collective-permute-start.11) | collective-permute-done | bytes 802848 | tf_op jit(solution)/shard_map/ppermute | solution.py:12
  126.5 12.0 %fusion = f32[512,896]{1,0:T(8,128)S(1)} fusion(bf16[8192,448]{0,1:T(8,128)(2,1)S(1)} %get-tuple-element.26, bf16[8192,448]{0,1:T(8,128)(2,1)S(1)} %get-tuple-element.27, bf16[128,8192]{1,0:T(8,128)(2,1)} %collective-permute-done.3, bf16[128,8192]{1,0:T(8,128)(2,1)S(1)} %copy-done.3, bf16[128,8192]{1,0:T(8,128)(2,1)} %collective-permute-done, ...), kind=kOutput, calls=%fused_computation.5 | convolution fusion | flops 7579107328 | bytes 24903680 | tf_op jit(solution)/shard_map/dot_general | solution.py:208
  140.0 5.1 %fusion.34 = f32[128,896]{1,0:T(8,128)S(1)} fusion(bf16[128,6144]{1,0:T(8,128)(2,1)} %collective-permute-done.12, bf16[8192,448]{0,1:T(8,128)(2,1)S(1)} %get-tuple-element.27, bf16[8192,448]{0,1:T(8,128)(2,1)S(1)} %get-tuple-element.26), kind=kOutput, calls=%fused_computation.42 | convolution fusion | flops 1431306240 | bytes 16711680 | tf_op jit(solution)/shard_map/dot_general | solution.py:217
  146.6 2.7 %fusion.40 = f32[128,896]{1,0:T(8,128)S(1)} fusion(f32[128,896]{1,0:T(8,128)S(1)} %fusion.34, bf16[128,2048]{1,0:T(8,128)(2,1)} %collective-permute-done.16, bf16[8192,448]{0,1:T(8,128)(2,1)S(1)} %get-tuple-element.27, bf16[8192,448]{0,1:T(8,128)(2,1)S(1)} %get-tuple-element.26, f32[512,896]{1,0:T(8,128)S(1)} %fusion, pred[]{:T(512)S(6)} %or.3), kind=kOutput, calls=%fused_computation.44 | convolution fusion | flops 477331456 | bytes 16580609 | tf_op jit(solution)/shard_map/dot_general | solution.py:223
  153.3 2.5 collective-permute-start.15
  156.6 3.7 %collective-permute-start.18 = (bf16[128,896]{1,0:T(8,128)(2,1)}, bf16[128,896]{1,0:T(8,128)(2,1)S(1)}, u32[]{:S(2)}, u32[]{:S(2)}) collective-permute-start(bf16[128,896]{1,0:T(8,128)(2,1)} %add_convert_fusion), channel_id=1, source_target_pairs={{0,12},{2,14},{13,1},{15,3},{4,8},{6,10},{9,5},{11,7},{16,28},{18,... | collective-permute-start | bytes 688136 | tf_op jit(solution)/shard_map/ppermute | solution.py:176
  160.7 6.2 %collective-permute-done.18 = bf16[128,896]{1,0:T(8,128)(2,1)S(1)} collective-permute-done((bf16[128,896]{1,0:T(8,128)(2,1)}, bf16[128,896]{1,0:T(8,128)(2,1)S(1)}, u32[]{:S(2)}, u32[]{:S(2)}) %collective-permute-start.18) | collective-permute-done | bytes 229408 | tf_op jit(solution)/shard_map/ppermute | solution.py:176
  169.4 2.2 collective-permute-start.19
  173.6 3.3 %collective-permute-start.29 = (bf16[56,1792]{1,0:T(8,128)(2,1)S(1)}, bf16[56,1792]{1,0:T(8,128)(2,1)S(1)}, u32[]{:S(2)}, u32[]{:S(2)}) collective-permute-start(bf16[56,1792]{1,0:T(8,128)(2,1)S(1)} %get-tuple-element.56), channel_id=1, source_target_pairs={{0,10},{2,8},{4,14},{6,12},{8,2},{10,0},{12,6},{14,4},{1,11},{3,9}... | collective-permute-start | bytes 602120 | tf_op jit(solution)/shard_map/ppermute | solution.py:256
  178.4 8.2 %collective-permute-done.28 = bf16[56,1792]{1,0:T(8,128)(2,1)S(1)} collective-permute-done((bf16[56,1792]{1,0:T(8,128)(2,1)S(1)}, bf16[56,1792]{1,0:T(8,128)(2,1)S(1)}, u32[]{:S(2)}, u32[]{:S(2)}) %collective-permute-start.28) | collective-permute-done | bytes 200736 | tf_op jit(solution)/shard_map/ppermute | solution.py:256
  186.6 4.3 %collective-permute-done.29 = bf16[56,1792]{1,0:T(8,128)(2,1)S(1)} collective-permute-done((bf16[56,1792]{1,0:T(8,128)(2,1)S(1)}, bf16[56,1792]{1,0:T(8,128)(2,1)S(1)}, u32[]{:S(2)}, u32[]{:S(2)}) %collective-permute-start.29) | collective-permute-done | bytes 200736 | tf_op jit(solution)/shard_map/ppermute | solution.py:256
  190.9 2.6 collective-permute-done.31
  197.5 12.4 %collective-permute-done.20 = bf16[56,1792]{1,0:T(8,128)(2,1)S(1)} collective-permute-done((bf16[56,1792]{1,0:T(8,128)(2,1)S(1)}, bf16[56,1792]{1,0:T(8,128)(2,1)S(1)}, u32[]{:S(2)}, u32[]{:S(2)}) %collective-permute-start.20) | collective-permute-done | bytes 200736 | tf_op jit(solution)/shard_map/ppermute | solution.py:256
  209.9 4.3 %collective-permute-done.21 = bf16[56,1792]{1,0:T(8,128)(2,1)S(1)} collective-permute-done((bf16[56,1792]{1,0:T(8,128)(2,1)S(1)}, bf16[56,1792]{1,0:T(8,128)(2,1)S(1)}, u32[]{:S(2)}, u32[]{:S(2)}) %collective-permute-start.21) | collective-permute-done | bytes 200736 | tf_op jit(solution)/shard_map/ppermute | solution.py:256
  227.3 3.3 %collective-permute-start.35 = (bf16[56,1792]{1,0:T(8,128)(2,1)S(1)}, bf16[56,1792]{1,0:T(8,128)(2,1)S(1)}, u32[]{:S(2)}, u32[]{:S(2)}) collective-permute-start(bf16[56,1792]{1,0:T(8,128)(2,1)S(1)} %get-tuple-element.53), channel_id=1, source_target_pairs={{0,10},{2,8},{4,14},{6,12},{8,2},{10,0},{12,6},{14,4},{1,11},{3,9}... | collective-permute-start | bytes 602120 | tf_op jit(solution)/shard_map/ppermute | solution.py:256
  232.1 2.1 fusion.26
  235.7 4.8 %collective-permute-done.34 = bf16[56,1792]{1,0:T(8,128)(2,1)S(1)} collective-permute-done((bf16[56,1792]{1,0:T(8,128)(2,1)S(1)}, bf16[56,1792]{1,0:T(8,128)(2,1)S(1)}, u32[]{:S(2)}, u32[]{:S(2)}) %collective-permute-start.34) | collective-permute-done | bytes 200736 | tf_op jit(solution)/shard_map/ppermute | solution.py:256
  240.5 2.4 collective-permute-start.26
  246.0 2.9 %collective-permute-done.37 = bf16[56,1792]{1,0:T(8,128)(2,1)S(1)} collective-permute-done((bf16[56,1792]{1,0:T(8,128)(2,1)S(1)}, bf16[56,1792]{1,0:T(8,128)(2,1)S(1)}, u32[]{:S(2)}, u32[]{:S(2)}) %collective-permute-start.37) | collective-permute-done | bytes 200736 | tf_op jit(solution)/shard_map/ppermute | solution.py:256
  249.5 10.4 %collective-permute-done.25 = bf16[56,1792]{1,0:T(8,128)(2,1)S(1)} collective-permute-done((bf16[56,1792]{1,0:T(8,128)(2,1)S(1)}, bf16[56,1792]{1,0:T(8,128)(2,1)S(1)}, u32[]{:S(2)}, u32[]{:S(2)}) %collective-permute-start.25) | collective-permute-done | bytes 200736 | tf_op jit(solution)/shard_map/ppermute | solution.py:256
  259.9 5.2 %collective-permute-done.26 = bf16[56,1792]{1,0:T(8,128)(2,1)S(1)} collective-permute-done((bf16[56,1792]{1,0:T(8,128)(2,1)S(1)}, bf16[56,1792]{1,0:T(8,128)(2,1)S(1)}, u32[]{:S(2)}, u32[]{:S(2)}) %collective-permute-start.26) | collective-permute-done | bytes 200736 | tf_op jit(solution)/shard_map/ppermute | solution.py:256
  (159 shorter events, 65.1 us)
Async XLA Ops:
  0.0 46.8 %collective-permute-start = (bf16[128,8192]{1,0:T(8,128)(2,1)}, bf16[128,8192]{1,0:T(8,128)(2,1)}, u32[]{:S(2)}, u32[]{:S(2)}) collective-permute-start(bf16[128,8192]{1,0:T(8,128)(2,1)} %param.13), channel_id=1, source_target_pairs={{0,4},{2,6},{4,0},{6,2},{8,12},{10,14},{12,8},{14,10},{1,5},{3,7},... | collective-permute-start | bytes 6291464 | tf_op jit(solution)/shard_map/ppermute | solution.py:167
  1.3 48.4 %collective-permute-start.1 = (bf16[128,8192]{1,0:T(8,128)(2,1)}, bf16[128,8192]{1,0:T(8,128)(2,1)}, u32[]{:S(2)}, u32[]{:S(2)}) collective-permute-start(bf16[128,8192]{1,0:T(8,128)(2,1)} %param.13), channel_id=1, source_target_pairs={{4,8},{6,10},{8,4},{10,6},{5,9},{7,11},{9,5},{11,7},{20,24},{22,26... | collective-permute-start | bytes 6291464 | tf_op jit(solution)/shard_map/ppermute | solution.py:167
  4.9 23.5 %collective-permute-start.4 = (bf16[1152,448]{0,1:T(8,128)(2,1)S(1)}, bf16[1152,448]{0,1:T(8,128)(2,1)S(1)}, u32[]{:S(2)}, u32[]{:S(2)}) collective-permute-start(bf16[1152,448]{0,1:T(8,128)(2,1)S(1)} %get-tuple-element.31), channel_id=1, source_target_pairs={{0,2},{2,0},{4,6},{6,4},{8,10},{10,8},{12,14},{14,12},{1,3},{3,1},... | collective-permute-start | bytes 3096584 | tf_op jit(solution)/shard_map/ppermute | solution.py:184
  5.3 48.4 %collective-permute-start.6 = (bf16[1152,448]{0,1:T(8,128)(2,1)S(1)}, bf16[1152,448]{0,1:T(8,128)(2,1)S(1)}, u32[]{:S(2)}, u32[]{:S(2)}) collective-permute-start(bf16[1152,448]{0,1:T(8,128)(2,1)S(1)} %get-tuple-element.30), channel_id=1, source_target_pairs={{0,2},{2,0},{4,6},{6,4},{8,10},{10,8},{12,14},{14,12},{1,3},{3,1},... | collective-permute-start | bytes 3096584 | tf_op jit(solution)/shard_map/ppermute | solution.py:184
  28.5 40.6 %collective-permute-start.5 = (bf16[1152,448]{0,1:T(8,128)(2,1)S(1)}, bf16[1152,448]{0,1:T(8,128)(2,1)}, u32[]{:S(2)}, u32[]{:S(2)}) collective-permute-start(bf16[1152,448]{0,1:T(8,128)(2,1)S(1)} %collective-permute-done.4), channel_id=1, source_target_pairs={{0,16},{16,0},{1,17},{17,1},{2,18},{18,2},{3,19},{19,3},{4,20},{20... | collective-permute-start | bytes 3096584 | tf_op jit(solution)/shard_map/ppermute | solution.py:12
  46.8 21.0 %collective-permute-start.8 = (bf16[896,448]{0,1:T(8,128)(2,1)}, bf16[896,448]{0,1:T(8,128)(2,1)}, u32[]{:S(2)}, u32[]{:S(2)}) collective-permute-start(bf16[896,448]{0,1:T(8,128)(2,1)} %get-tuple-element.12), channel_id=1, source_target_pairs={{0,2},{2,0},{4,6},{6,4},{8,10},{10,8},{12,14},{14,12},{1,3},{3,1},... | collective-permute-start | bytes 2408456 | tf_op jit(solution)/shard_map/ppermute | solution.py:188
  47.1 47.5 %collective-permute-start.3 = (bf16[128,8192]{1,0:T(8,128)(2,1)}, bf16[128,8192]{1,0:T(8,128)(2,1)}, u32[]{:S(2)}, u32[]{:S(2)}) collective-permute-start(bf16[128,8192]{1,0:T(8,128)(2,1)} %collective-permute-done), channel_id=1, source_target_pairs={{4,8},{6,10},{8,4},{10,6},{5,9},{7,11},{9,5},{11,7},{20,24},{22,26... | collective-permute-start | bytes 6291464 | tf_op jit(solution)/shard_map/ppermute | solution.py:167
  49.7 55.3 %collective-permute-start.2 = (bf16[128,8192]{1,0:T(8,128)(2,1)}, bf16[128,8192]{1,0:T(8,128)(2,1)}, u32[]{:S(2)}, u32[]{:S(2)}) collective-permute-start(bf16[128,8192]{1,0:T(8,128)(2,1)} %collective-permute-done.1), channel_id=1, source_target_pairs={{4,0},{6,2},{8,12},{10,14},{5,1},{7,3},{9,13},{11,15},{20,16},{22,... | collective-permute-start | bytes 6291464 | tf_op jit(solution)/shard_map/ppermute | solution.py:167
  53.7 22.3 %collective-permute-start.7 = (bf16[1152,448]{0,1:T(8,128)(2,1)S(1)}, bf16[1152,448]{0,1:T(8,128)(2,1)}, u32[]{:S(2)}, u32[]{:S(2)}) collective-permute-start(bf16[1152,448]{0,1:T(8,128)(2,1)S(1)} %collective-permute-done.6), channel_id=1, source_target_pairs={{0,16},{16,0},{1,17},{17,1},{2,18},{18,2},{3,19},{19,3},{4,20},{20... | collective-permute-start | bytes 3096584 | tf_op jit(solution)/shard_map/ppermute | solution.py:12
  67.8 25.4 %collective-permute-start.9 = (bf16[896,448]{0,1:T(8,128)(2,1)}, bf16[896,448]{0,1:T(8,128)(2,1)S(1)}, u32[]{:S(2)}, u32[]{:S(2)}) collective-permute-start(bf16[896,448]{0,1:T(8,128)(2,1)} %collective-permute-done.8), channel_id=1, source_target_pairs={{0,16},{16,0},{1,17},{17,1},{2,18},{18,2},{3,19},{19,3},{4,20},{20... | collective-permute-start | bytes 2408456 | tf_op jit(solution)/shard_map/ppermute | solution.py:12
  69.3 34.4 %collective-permute-start.10 = (bf16[896,448]{0,1:T(8,128)(2,1)}, bf16[896,448]{0,1:T(8,128)(2,1)S(1)}, u32[]{:S(2)}, u32[]{:S(2)}) collective-permute-start(bf16[896,448]{0,1:T(8,128)(2,1)} %get-tuple-element.13), channel_id=1, source_target_pairs={{0,2},{2,0},{4,6},{6,4},{8,10},{10,8},{12,14},{14,12},{1,3},{3,1},... | collective-permute-start | bytes 2408456 | tf_op jit(solution)/shard_map/ppermute | solution.py:188
  97.3 41.4 %collective-permute-start.12 = (bf16[128,6144]{1,0:T(8,128)(2,1)}, bf16[128,6144]{1,0:T(8,128)(2,1)}, u32[]{:S(2)}, u32[]{:S(2)}) collective-permute-start(bf16[128,6144]{1,0:T(8,128)(2,1)} %slice.148), channel_id=1, source_target_pairs={{4,0},{6,2},{8,12},{10,14},{5,1},{7,3},{9,13},{11,15},{20,16},{22,... | collective-permute-start | bytes 4718600 | tf_op jit(solution)/shard_map/ppermute | solution.py:167
  101.7 44.9 %collective-permute-start.16 = (bf16[128,2048]{1,0:T(8,128)(2,1)}, bf16[128,2048]{1,0:T(8,128)(2,1)}, u32[]{:S(2)}, u32[]{:S(2)}) collective-permute-start(bf16[128,2048]{1,0:T(8,128)(2,1)} %slice.149), channel_id=1, source_target_pairs={{4,0},{6,2},{8,12},{10,14},{5,1},{7,3},{9,13},{11,15},{20,16},{22,... | collective-permute-start | bytes 1572872 | tf_op jit(solution)/shard_map/ppermute | solution.py:167
  103.8 16.5 %collective-permute-start.11 = (bf16[896,448]{0,1:T(8,128)(2,1)S(1)}, bf16[896,448]{0,1:T(8,128)(2,1)S(1)}, u32[]{:S(2)}, u32[]{:S(2)}) collective-permute-start(bf16[896,448]{0,1:T(8,128)(2,1)S(1)} %collective-permute-done.10), channel_id=1, source_target_pairs={{0,16},{16,0},{1,17},{17,1},{2,18},{18,2},{3,19},{19,3},{4,20},{20... | collective-permute-start | bytes 2408456 | tf_op jit(solution)/shard_map/ppermute | solution.py:12
  138.7 7.7 %collective-permute-start.13 = (f32[384,896]{1,0:T(8,128)S(1)}, f32[384,896]{1,0:T(8,128)S(1)}, u32[]{:S(2)}, u32[]{:S(2)}) collective-permute-start(f32[384,896]{1,0:T(8,128)S(1)} %pad_maximum_fusion.4), channel_id=1, source_target_pairs={{1,0},{3,2},{5,4},{7,6},{8,9},{10,11},{12,13},{14,15},{17,16},{19,... | collective-permute-start | bytes 4128776 | tf_op jit(solution)/shard_map/ppermute | solution.py:173
  151.4 9.3 %collective-permute-start.14 = (bf16[128,896]{1,0:T(8,128)(2,1)S(1)}, bf16[128,896]{1,0:T(8,128)(2,1)}, u32[]{:S(2)}, u32[]{:S(2)}) collective-permute-start(bf16[128,896]{1,0:T(8,128)(2,1)S(1)} %get-tuple-element.33), channel_id=1, source_target_pairs={{0,4},{2,6},{4,0},{6,2},{9,13},{11,15},{13,9},{15,11},{16,20},{18,... | collective-permute-start | bytes 688136 | tf_op jit(solution)/shard_map/ppermute | solution.py:176
  156.6 10.3 %collective-permute-start.18 = (bf16[128,896]{1,0:T(8,128)(2,1)}, bf16[128,896]{1,0:T(8,128)(2,1)S(1)}, u32[]{:S(2)}, u32[]{:S(2)}) collective-permute-start(bf16[128,896]{1,0:T(8,128)(2,1)} %add_convert_fusion), channel_id=1, source_target_pairs={{0,12},{2,14},{13,1},{15,3},{4,8},{6,10},{9,5},{11,7},{16,28},{18,... | collective-permute-start | bytes 688136 | tf_op jit(solution)/shard_map/ppermute | solution.py:176
  173.5 13.1 %collective-permute-start.28 = (bf16[56,1792]{1,0:T(8,128)(2,1)S(1)}, bf16[56,1792]{1,0:T(8,128)(2,1)S(1)}, u32[]{:S(2)}, u32[]{:S(2)}) collective-permute-start(bf16[56,1792]{1,0:T(8,128)(2,1)S(1)} %get-tuple-element.57), channel_id=1, source_target_pairs={{0,8},{2,10},{4,12},{6,14},{8,0},{10,2},{12,4},{14,6},{1,9},{3,11}... | collective-permute-start | bytes 602120 | tf_op jit(solution)/shard_map/ppermute | solution.py:256
  173.6 17.2 %collective-permute-start.29 = (bf16[56,1792]{1,0:T(8,128)(2,1)S(1)}, bf16[56,1792]{1,0:T(8,128)(2,1)S(1)}, u32[]{:S(2)}, u32[]{:S(2)}) collective-permute-start(bf16[56,1792]{1,0:T(8,128)(2,1)S(1)} %get-tuple-element.56), channel_id=1, source_target_pairs={{0,10},{2,8},{4,14},{6,12},{8,2},{10,0},{12,6},{14,4},{1,11},{3,9}... | collective-permute-start | bytes 602120 | tf_op jit(solution)/shard_map/ppermute | solution.py:256
  177.0 13.9 %collective-permute-start.30 = (bf16[56,1792]{1,0:T(8,128)(2,1)S(1)}, bf16[56,1792]{1,0:T(8,128)(2,1)S(1)}, u32[]{:S(2)}, u32[]{:S(2)}) collective-permute-start(bf16[56,1792]{1,0:T(8,128)(2,1)S(1)} %get-tuple-element.55), channel_id=1, source_target_pairs={{0,4},{2,6},{4,0},{6,2},{8,12},{10,14},{12,8},{14,10},{1,5},{3,7},... | collective-permute-start | bytes 602120 | tf_op jit(solution)/shard_map/ppermute | solution.py:256
  177.0 16.6 %collective-permute-start.31 = (bf16[56,1792]{1,0:T(8,128)(2,1)S(1)}, bf16[56,1792]{1,0:T(8,128)(2,1)S(1)}, u32[]{:S(2)}, u32[]{:S(2)}) collective-permute-start(bf16[56,1792]{1,0:T(8,128)(2,1)S(1)} %get-tuple-element.54), channel_id=1, source_target_pairs={{0,6},{2,4},{4,2},{6,0},{8,14},{10,12},{12,10},{14,8},{1,7},{3,5},... | collective-permute-start | bytes 602120 | tf_op jit(solution)/shard_map/ppermute | solution.py:256
  193.5 21.5 %collective-permute-start.32 = (bf16[224,1792]{1,0:T(8,128)(2,1)S(1)}, bf16[224,1792]{1,0:T(8,128)(2,1)S(1)}, u32[]{:S(2)}, u32[]{:S(2)}) collective-permute-start(bf16[224,1792]{1,0:T(8,128)(2,1)S(1)} %constant_dynamic-update-slice_fusion), channel_id=1, source_target_pairs={{0,1},{1,0},{2,3},{3,2},{4,5},{5,4},{6,7},{7,6},{8,9},{9,8},{10,11... | collective-permute-start | bytes 2408456 | tf_op jit(solution)/shard_map/ppermute | solution.py:12
  194.6 15.3 %collective-permute-start.20 = (bf16[56,1792]{1,0:T(8,128)(2,1)S(1)}, bf16[56,1792]{1,0:T(8,128)(2,1)S(1)}, u32[]{:S(2)}, u32[]{:S(2)}) collective-permute-start(bf16[56,1792]{1,0:T(8,128)(2,1)S(1)} %get-tuple-element.46), channel_id=1, source_target_pairs={{0,12},{2,14},{4,8},{6,10},{8,4},{10,6},{12,0},{14,2},{1,13},{3,15... | collective-permute-start | bytes 602120 | tf_op jit(solution)/shard_map/ppermute | solution.py:256
  196.1 18.0 %collective-permute-start.21 = (bf16[56,1792]{1,0:T(8,128)(2,1)S(1)}, bf16[56,1792]{1,0:T(8,128)(2,1)S(1)}, u32[]{:S(2)}, u32[]{:S(2)}) collective-permute-start(bf16[56,1792]{1,0:T(8,128)(2,1)S(1)} %get-tuple-element.49), channel_id=1, source_target_pairs={{0,14},{2,12},{4,10},{6,8},{8,6},{10,4},{12,2},{14,0},{1,15},{3,13... | collective-permute-start | bytes 602120 | tf_op jit(solution)/shard_map/ppermute | solution.py:256
  196.2 18.0 %collective-permute-start.22 = (bf16[56,1792]{1,0:T(8,128)(2,1)S(1)}, bf16[56,1792]{1,0:T(8,128)(2,1)S(1)}, u32[]{:S(2)}, u32[]{:S(2)}) collective-permute-start(bf16[56,1792]{1,0:T(8,128)(2,1)S(1)} %get-tuple-element.47), channel_id=1, source_target_pairs={{0,2},{2,0},{4,6},{6,4},{8,10},{10,8},{12,14},{14,12},{1,3},{3,1},... | collective-permute-start | bytes 602120 | tf_op jit(solution)/shard_map/ppermute | solution.py:256
  227.2 13.3 %collective-permute-start.34 = (bf16[56,1792]{1,0:T(8,128)(2,1)S(1)}, bf16[56,1792]{1,0:T(8,128)(2,1)S(1)}, u32[]{:S(2)}, u32[]{:S(2)}) collective-permute-start(bf16[56,1792]{1,0:T(8,128)(2,1)S(1)} %get-tuple-element.50), channel_id=1, source_target_pairs={{0,8},{2,10},{4,12},{6,14},{8,0},{10,2},{12,4},{14,6},{1,9},{3,11}... | collective-permute-start | bytes 602120 | tf_op jit(solution)/shard_map/ppermute | solution.py:256
  227.3 17.5 %collective-permute-start.35 = (bf16[56,1792]{1,0:T(8,128)(2,1)S(1)}, bf16[56,1792]{1,0:T(8,128)(2,1)S(1)}, u32[]{:S(2)}, u32[]{:S(2)}) collective-permute-start(bf16[56,1792]{1,0:T(8,128)(2,1)S(1)} %get-tuple-element.53), channel_id=1, source_target_pairs={{0,10},{2,8},{4,14},{6,12},{8,2},{10,0},{12,6},{14,4},{1,11},{3,9}... | collective-permute-start | bytes 602120 | tf_op jit(solution)/shard_map/ppermute | solution.py:256
  230.5 15.5 %collective-permute-start.36 = (bf16[56,1792]{1,0:T(8,128)(2,1)S(1)}, bf16[56,1792]{1,0:T(8,128)(2,1)S(1)}, u32[]{:S(2)}, u32[]{:S(2)}) collective-permute-start(bf16[56,1792]{1,0:T(8,128)(2,1)S(1)} %get-tuple-element.52), channel_id=1, source_target_pairs={{0,4},{2,6},{4,0},{6,2},{8,12},{10,14},{12,8},{14,10},{1,5},{3,7},... | collective-permute-start | bytes 602120 | tf_op jit(solution)/shard_map/ppermute | solution.py:256
  230.9 18.0 %collective-permute-start.37 = (bf16[56,1792]{1,0:T(8,128)(2,1)S(1)}, bf16[56,1792]{1,0:T(8,128)(2,1)S(1)}, u32[]{:S(2)}, u32[]{:S(2)}) collective-permute-start(bf16[56,1792]{1,0:T(8,128)(2,1)S(1)} %get-tuple-element.51), channel_id=1, source_target_pairs={{0,6},{2,4},{4,2},{6,0},{8,14},{10,12},{12,10},{14,8},{1,7},{3,5},... | collective-permute-start | bytes 602120 | tf_op jit(solution)/shard_map/ppermute | solution.py:256
  234.2 25.7 %collective-permute-start.25 = (bf16[56,1792]{1,0:T(8,128)(2,1)S(1)}, bf16[56,1792]{1,0:T(8,128)(2,1)S(1)}, u32[]{:S(2)}, u32[]{:S(2)}) collective-permute-start(bf16[56,1792]{1,0:T(8,128)(2,1)S(1)} %get-tuple-element.42), channel_id=1, source_target_pairs={{0,12},{2,14},{4,8},{6,10},{8,4},{10,6},{12,0},{14,2},{1,13},{3,15... | collective-permute-start | bytes 602120 | tf_op jit(solution)/shard_map/ppermute | solution.py:256
  240.5 24.6 %collective-permute-start.26 = (bf16[56,1792]{1,0:T(8,128)(2,1)S(1)}, bf16[56,1792]{1,0:T(8,128)(2,1)S(1)}, u32[]{:S(2)}, u32[]{:S(2)}) collective-permute-start(bf16[56,1792]{1,0:T(8,128)(2,1)S(1)} %get-tuple-element.45), channel_id=1, source_target_pairs={{0,14},{2,12},{4,10},{6,8},{8,6},{10,4},{12,2},{14,0},{1,15},{3,13... | collective-permute-start | bytes 602120 | tf_op jit(solution)/shard_map/ppermute | solution.py:256
  244.8 20.3 %collective-permute-start.27 = (bf16[56,1792]{1,0:T(8,128)(2,1)S(1)}, bf16[56,1792]{1,0:T(8,128)(2,1)S(1)}, u32[]{:S(2)}, u32[]{:S(2)}) collective-permute-start(bf16[56,1792]{1,0:T(8,128)(2,1)S(1)} %get-tuple-element.43), channel_id=1, source_target_pairs={{0,2},{2,0},{4,6},{6,4},{8,10},{10,8},{12,14},{14,12},{1,3},{3,1},... | collective-permute-start | bytes 602120 | tf_op jit(solution)/shard_map/ppermute | solution.py:256
  (26 other events, 446.9 us)

commit v7 on v6

--- a/solution.py
+++ b/solution.py
@@ -190,7 +190,7 @@
     most = depth // 4 * 3
     ready = [cross_far[:, :most], cross_far[:, most:]]
     out_far = [hop(block, OUTWARD) for block in ready]
-    far += [swap_halves(after(near[3], ready), "groups")]
+    far += [swap_halves(after(near[3], ready[0]), "groups")]
 
     lower_half = group == 0
     passed_rows = jnp.concatenate(

time: 267 us -> 266 us (level)
  waiting for transfers between devices: 149 us -> 146 us
    ppermute x9, waiting for transfers between devices: 36.1 us -> 32.1 us  [swap_halves(): return lax.ppermute(array, axis_name, [(0, 1), (1, 0)])]
  transfers between devices with their start and end apart: 38 -> 38, of which waited for: 20 -> 21; matrix products, arithmetic and copies ran while one was open for 20% -> 20% of each run, Pallas kernels for 0% -> 0%
where the time goes in v7:
time: 266 us; the launch traced here: 265 us
  waiting for transfers between devices  146 us (55%)
  starting transfers between devices  55.7 us (21%)
  matrix products  35.3 us (13%)
  other arithmetic  15.9 us (6%)
  local copies, waits for them, and re-layouts  11.6 us (4%)
    ppermute x14, waiting for transfers between devices, exchange(): lax.ppermute(split[i], 'expert', [(e, e ^ k) for e in range(expert_count)])  56.9 us
    ppermute x9, waiting for transfers between devices, swap_halves(): return lax.ppermute(array, axis_name, [(0, 1), (1, 0)])  32.1 us
    ppermute x2, waiting for transfers between devices, project_line(): near = [lax.ppermute(p, 'expert', partner) for p in pieces[:2]]  22 us
    ppermute x14, starting transfers between devices, exchange(): lax.ppermute(split[i], 'expert', [(e, e ^ k) for e in range(expert_count)])  17.6 us
    ppermute x6, waiting for transfers between devices, hop(): return lax.ppermute(block, 'expert', chip_pairs(moves))  15 us
    ppermute x6, starting transfers between devices, hop(): return lax.ppermute(block, 'expert', chip_pairs(moves))  13.8 us
    dot_general x1, matrix products, project_line(): early = jnp.dot(blocks, columns, preferred_element_type=jnp.float32)  12 us
    ppermute x2, waiting for transfers between devices, project_line(): lax.ppermute(after(p, swap), 'expert', partner)  11.7 us
  transfers between devices with their start and end apart: 38, of which 21 were waited for; matrix products, arithmetic and copies ran while one was open for 20% of the time, Pallas kernels for 0%

profile of v7, /device:TPU:19, one launch (start us, length us, event | category | flops | bytes accessed | tf_op | source)
XLA Modules:
  0.0 265.1 jit_solution(11659855515470449707)
XLA Ops:
  6.5 22.0 %collective-permute-done.4 = bf16[1152,448]{0,1:T(8,128)(2,1)S(1)} collective-permute-done((bf16[1152,448]{0,1:T(8,128)(2,1)S(1)}, bf16[1152,448]{0,1:T(8,128)(2,1)S(1)}, u32[]{:S(2)}, u32[]{:S(2)}) %collective-permute-start.4) | collective-permute-done | bytes 1032224 | tf_op jit(solution)/shard_map/ppermute | solution.py:184
  29.7 2.7 %constant_dynamic-slice_fusion = (bf16[896,448]{0,1:T(8,128)(2,1)}, bf16[896,448]{0,1:T(8,128)(2,1)}) fusion(bf16[8192,448]{0,1:T(8,128)(2,1)} %param.14, s32[]{:T(128)S(6)} %select_n.204, s32[]{:T(128)S(6)} %select_n.202), kind=kLoop, calls=%fused_computation.134 | loop fusion | bytes 3211272 | tf_op jit(solution)/shard_map/dynamic_slice | solution.py:179
  32.4 14.4 %collective-permute-done = bf16[128,8192]{1,0:T(8,128)(2,1)} collective-permute-done((bf16[128,8192]{1,0:T(8,128)(2,1)}, bf16[128,8192]{1,0:T(8,128)(2,1)}, u32[]{:S(2)}, u32[]{:S(2)}) %collective-permute-start) | collective-permute-done | bytes 2097184 | tf_op jit(solution)/shard_map/ppermute | solution.py:167
  49.7 4.0 %collective-permute-start.2 = (bf16[128,8192]{1,0:T(8,128)(2,1)}, bf16[128,8192]{1,0:T(8,128)(2,1)}, u32[]{:S(2)}, u32[]{:S(2)}) collective-permute-start(bf16[128,8192]{1,0:T(8,128)(2,1)} %collective-permute-done.1), channel_id=1, source_target_pairs={{4,0},{6,2},{8,12},{10,14},{5,1},{7,3},{9,13},{11,15},{20,16},{22,... | collective-permute-start | bytes 6291464 | tf_op jit(solution)/shard_map/ppermute | solution.py:167
  56.1 11.7 %collective-permute-done.8 = bf16[896,448]{0,1:T(8,128)(2,1)} collective-permute-done((bf16[896,448]{0,1:T(8,128)(2,1)}, bf16[896,448]{0,1:T(8,128)(2,1)}, u32[]{:S(2)}, u32[]{:S(2)}) %collective-permute-start.8) | collective-permute-done | bytes 802848 | tf_op jit(solution)/shard_map/ppermute | solution.py:188
  69.7 6.3 %collective-permute-done.7 = bf16[1152,448]{0,1:T(8,128)(2,1)} collective-permute-done((bf16[1152,448]{0,1:T(8,128)(2,1)S(1)}, bf16[1152,448]{0,1:T(8,128)(2,1)}, u32[]{:S(2)}, u32[]{:S(2)}) %collective-permute-start.7) | collective-permute-done | bytes 1032224 | tf_op jit(solution)/shard_map/ppermute | solution.py:12
  76.3 16.9 %collective-permute-done.9 = bf16[896,448]{0,1:T(8,128)(2,1)S(1)} collective-permute-done((bf16[896,448]{0,1:T(8,128)(2,1)}, bf16[896,448]{0,1:T(8,128)(2,1)S(1)}, u32[]{:S(2)}, u32[]{:S(2)}) %collective-permute-start.9) | collective-permute-done | bytes 802848 | tf_op jit(solution)/shard_map/ppermute | solution.py:12
  94.6 2.7 %slice.148 = bf16[128,6144]{1,0:T(8,128)(2,1)} slice(bf16[128,8192]{1,0:T(8,128)(2,1)} %collective-permute-done.3), slice={[0:128], [0:6144]} | slice | bytes 3145728 | tf_op jit(solution)/shard_map/slice | solution.py:191
  97.3 2.5 collective-permute-start.12
  102.9 2.1 collective-permute-start.16
  105.0 3.1 %broadcast_select_fusion.2 = bf16[128,8192]{1,0:T(8,128)(2,1)} fusion(bf16[128,8192]{1,0:T(8,128)(2,1)} %collective-permute-done.1, bf16[128,8192]{1,0:T(8,128)(2,1)} %collective-permute-done.2, pred[]{:T(512)S(6)} %or.3), kind=kLoop, calls=%fused_computation.38 | loop fusion | flops 1048576 | bytes 6291457 | tf_op jit(solution)/shard_map/jit(_where)/select_n | solution.py:206
  108.1 8.1 %collective-permute-done.11 = bf16[896,448]{0,1:T(8,128)(2,1)S(1)} collective-permute-done((bf16[896,448]{0,1:T(8,128)(2,1)S(1)}, bf16[896,448]{0,1:T(8,128)(2,1)S(1)}, u32[]{:S(2)}, u32[]{:S(2)}) %collective-permute-start.11) | collective-permute-done | bytes 802848 | tf_op jit(solution)/shard_map/ppermute | solution.py:12
  122.5 12.0 %fusion = f32[512,896]{1,0:T(8,128)S(1)} fusion(bf16[8192,448]{0,1:T(8,128)(2,1)S(1)} %get-tuple-element.26, bf16[8192,448]{0,1:T(8,128)(2,1)S(1)} %get-tuple-element.27, bf16[128,8192]{1,0:T(8,128)(2,1)} %collective-permute-done.3, bf16[128,8192]{1,0:T(8,128)(2,1)S(1)} %copy-done.3, bf16[128,8192]{1,0:T(8,128)(2,1)} %collective-permute-done, ...), kind=kOutput, calls=%fused_computation.5 | convolution fusion | flops 7579107328 | bytes 24903680 | tf_op jit(solution)/shard_map/dot_general | solution.py:208
  136.0 5.1 %fusion.34 = f32[128,896]{1,0:T(8,128)S(1)} fusion(bf16[128,6144]{1,0:T(8,128)(2,1)} %collective-permute-done.12, bf16[8192,448]{0,1:T(8,128)(2,1)S(1)} %get-tuple-element.27, bf16[8192,448]{0,1:T(8,128)(2,1)S(1)} %get-tuple-element.26), kind=kOutput, calls=%fused_computation.42 | convolution fusion | flops 1431306240 | bytes 16711680 | tf_op jit(solution)/shard_map/dot_general | solution.py:217
  142.7 2.7 %fusion.40 = f32[128,896]{1,0:T(8,128)S(1)} fusion(f32[128,896]{1,0:T(8,128)S(1)} %fusion.34, bf16[128,2048]{1,0:T(8,128)(2,1)} %collective-permute-done.16, bf16[8192,448]{0,1:T(8,128)(2,1)S(1)} %get-tuple-element.27, bf16[8192,448]{0,1:T(8,128)(2,1)S(1)} %get-tuple-element.26, f32[512,896]{1,0:T(8,128)S(1)} %fusion, pred[]{:T(512)S(6)} %or.3), kind=kOutput, calls=%fused_computation.44 | convolution fusion | flops 477331456 | bytes 16580609 | tf_op jit(solution)/shard_map/dot_general | solution.py:223
  147.4 2.3 collective-permute-start.14
  149.7 6.1 %collective-permute-start.15 = (bf16[128,896]{1,0:T(8,128)(2,1)S(1)}, bf16[128,896]{1,0:T(8,128)(2,1)}, u32[]{:S(2)}, u32[]{:S(2)}) collective-permute-start(bf16[128,896]{1,0:T(8,128)(2,1)S(1)} %get-tuple-element.32), channel_id=1, source_target_pairs={{0,8},{2,10},{13,5},{15,7},{4,12},{6,14},{9,1},{11,3},{16,24},{18,... | collective-permute-start | bytes 688136 | tf_op jit(solution)/shard_map/ppermute | solution.py:176
  158.5 4.3 %collective-permute-done.15 = bf16[128,896]{1,0:T(8,128)(2,1)} collective-permute-done((bf16[128,896]{1,0:T(8,128)(2,1)S(1)}, bf16[128,896]{1,0:T(8,128)(2,1)}, u32[]{:S(2)}, u32[]{:S(2)}) %collective-permute-start.15) | collective-permute-done | bytes 229408 | tf_op jit(solution)/shard_map/ppermute | solution.py:176
  162.8 2.6 collective-permute-done.18
  167.9 2.2 collective-permute-start.19
  172.1 3.3 %collective-permute-start.29 = (bf16[56,1792]{1,0:T(8,128)(2,1)S(1)}, bf16[56,1792]{1,0:T(8,128)(2,1)S(1)}, u32[]{:S(2)}, u32[]{:S(2)}) collective-permute-start(bf16[56,1792]{1,0:T(8,128)(2,1)S(1)} %get-tuple-element.56), channel_id=1, source_target_pairs={{0,10},{2,8},{4,14},{6,12},{8,2},{10,0},{12,6},{14,4},{1,11},{3,9}... | collective-permute-start | bytes 602120 | tf_op jit(solution)/shard_map/ppermute | solution.py:256
  176.9 8.2 %collective-permute-done.28 = bf16[56,1792]{1,0:T(8,128)(2,1)S(1)} collective-permute-done((bf16[56,1792]{1,0:T(8,128)(2,1)S(1)}, bf16[56,1792]{1,0:T(8,128)(2,1)S(1)}, u32[]{:S(2)}, u32[]{:S(2)}) %collective-permute-start.28) | collective-permute-done | bytes 200736 | tf_op jit(solution)/shard_map/ppermute | solution.py:256
  185.0 4.3 %collective-permute-done.29 = bf16[56,1792]{1,0:T(8,128)(2,1)S(1)} collective-permute-done((bf16[56,1792]{1,0:T(8,128)(2,1)S(1)}, bf16[56,1792]{1,0:T(8,128)(2,1)S(1)}, u32[]{:S(2)}, u32[]{:S(2)}) %collective-permute-start.29) | collective-permute-done | bytes 200736 | tf_op jit(solution)/shard_map/ppermute | solution.py:256
  189.4 2.6 collective-permute-done.31
  196.0 12.3 %collective-permute-done.20 = bf16[56,1792]{1,0:T(8,128)(2,1)S(1)} collective-permute-done((bf16[56,1792]{1,0:T(8,128)(2,1)S(1)}, bf16[56,1792]{1,0:T(8,128)(2,1)S(1)}, u32[]{:S(2)}, u32[]{:S(2)}) %collective-permute-start.20) | collective-permute-done | bytes 200736 | tf_op jit(solution)/shard_map/ppermute | solution.py:256
  208.3 4.3 %collective-permute-done.21 = bf16[56,1792]{1,0:T(8,128)(2,1)S(1)} collective-permute-done((bf16[56,1792]{1,0:T(8,128)(2,1)S(1)}, bf16[56,1792]{1,0:T(8,128)(2,1)S(1)}, u32[]{:S(2)}, u32[]{:S(2)}) %collective-permute-start.21) | collective-permute-done | bytes 200736 | tf_op jit(solution)/shard_map/ppermute | solution.py:256
  225.7 3.3 %collective-permute-start.35 = (bf16[56,1792]{1,0:T(8,128)(2,1)S(1)}, bf16[56,1792]{1,0:T(8,128)(2,1)S(1)}, u32[]{:S(2)}, u32[]{:S(2)}) collective-permute-start(bf16[56,1792]{1,0:T(8,128)(2,1)S(1)} %get-tuple-element.53), channel_id=1, source_target_pairs={{0,10},{2,8},{4,14},{6,12},{8,2},{10,0},{12,6},{14,4},{1,11},{3,9}... | collective-permute-start | bytes 602120 | tf_op jit(solution)/shard_map/ppermute | solution.py:256
  234.2 4.8 %collective-permute-done.34 = bf16[56,1792]{1,0:T(8,128)(2,1)S(1)} collective-permute-done((bf16[56,1792]{1,0:T(8,128)(2,1)S(1)}, bf16[56,1792]{1,0:T(8,128)(2,1)S(1)}, u32[]{:S(2)}, u32[]{:S(2)}) %collective-permute-start.34) | collective-permute-done | bytes 200736 | tf_op jit(solution)/shard_map/ppermute | solution.py:256
  239.0 2.4 collective-permute-start.26
  244.5 2.9 %collective-permute-done.37 = bf16[56,1792]{1,0:T(8,128)(2,1)S(1)} collective-permute-done((bf16[56,1792]{1,0:T(8,128)(2,1)S(1)}, bf16[56,1792]{1,0:T(8,128)(2,1)S(1)}, u32[]{:S(2)}, u32[]{:S(2)}) %collective-permute-start.37) | collective-permute-done | bytes 200736 | tf_op jit(solution)/shard_map/ppermute | solution.py:256
  248.0 10.4 %collective-permute-done.25 = bf16[56,1792]{1,0:T(8,128)(2,1)S(1)} collective-permute-done((bf16[56,1792]{1,0:T(8,128)(2,1)S(1)}, bf16[56,1792]{1,0:T(8,128)(2,1)S(1)}, u32[]{:S(2)}, u32[]{:S(2)}) %collective-permute-start.25) | collective-permute-done | bytes 200736 | tf_op jit(solution)/shard_map/ppermute | solution.py:256
  258.4 5.2 %collective-permute-done.26 = bf16[56,1792]{1,0:T(8,128)(2,1)S(1)} collective-permute-done((bf16[56,1792]{1,0:T(8,128)(2,1)S(1)}, bf16[56,1792]{1,0:T(8,128)(2,1)S(1)}, u32[]{:S(2)}, u32[]{:S(2)}) %collective-permute-start.26) | collective-permute-done | bytes 200736 | tf_op jit(solution)/shard_map/ppermute | solution.py:256
  (159 shorter events, 66.7 us)
Async XLA Ops:
  0.0 46.8 %collective-permute-start = (bf16[128,8192]{1,0:T(8,128)(2,1)}, bf16[128,8192]{1,0:T(8,128)(2,1)}, u32[]{:S(2)}, u32[]{:S(2)}) collective-permute-start(bf16[128,8192]{1,0:T(8,128)(2,1)} %param.13), channel_id=1, source_target_pairs={{0,4},{2,6},{4,0},{6,2},{8,12},{10,14},{12,8},{14,10},{1,5},{3,7},... | collective-permute-start | bytes 6291464 | tf_op jit(solution)/shard_map/ppermute | solution.py:167
  1.3 48.4 %collective-permute-start.1 = (bf16[128,8192]{1,0:T(8,128)(2,1)}, bf16[128,8192]{1,0:T(8,128)(2,1)}, u32[]{:S(2)}, u32[]{:S(2)}) collective-permute-start(bf16[128,8192]{1,0:T(8,128)(2,1)} %param.13), channel_id=1, source_target_pairs={{4,8},{6,10},{8,4},{10,6},{5,9},{7,11},{9,5},{11,7},{20,24},{22,26... | collective-permute-start | bytes 6291464 | tf_op jit(solution)/shard_map/ppermute | solution.py:167
  4.9 23.5 %collective-permute-start.4 = (bf16[1152,448]{0,1:T(8,128)(2,1)S(1)}, bf16[1152,448]{0,1:T(8,128)(2,1)S(1)}, u32[]{:S(2)}, u32[]{:S(2)}) collective-permute-start(bf16[1152,448]{0,1:T(8,128)(2,1)S(1)} %get-tuple-element.31), channel_id=1, source_target_pairs={{0,2},{2,0},{4,6},{6,4},{8,10},{10,8},{12,14},{14,12},{1,3},{3,1},... | collective-permute-start | bytes 3096584 | tf_op jit(solution)/shard_map/ppermute | solution.py:184
  5.3 48.4 %collective-permute-start.6 = (bf16[1152,448]{0,1:T(8,128)(2,1)S(1)}, bf16[1152,448]{0,1:T(8,128)(2,1)S(1)}, u32[]{:S(2)}, u32[]{:S(2)}) collective-permute-start(bf16[1152,448]{0,1:T(8,128)(2,1)S(1)} %get-tuple-element.30), channel_id=1, source_target_pairs={{0,2},{2,0},{4,6},{6,4},{8,10},{10,8},{12,14},{14,12},{1,3},{3,1},... | collective-permute-start | bytes 3096584 | tf_op jit(solution)/shard_map/ppermute | solution.py:184
  28.5 40.6 %collective-permute-start.5 = (bf16[1152,448]{0,1:T(8,128)(2,1)S(1)}, bf16[1152,448]{0,1:T(8,128)(2,1)}, u32[]{:S(2)}, u32[]{:S(2)}) collective-permute-start(bf16[1152,448]{0,1:T(8,128)(2,1)S(1)} %collective-permute-done.4), channel_id=1, source_target_pairs={{0,16},{16,0},{1,17},{17,1},{2,18},{18,2},{3,19},{19,3},{4,20},{20... | collective-permute-start | bytes 3096584 | tf_op jit(solution)/shard_map/ppermute | solution.py:12
  46.8 21.0 %collective-permute-start.8 = (bf16[896,448]{0,1:T(8,128)(2,1)}, bf16[896,448]{0,1:T(8,128)(2,1)}, u32[]{:S(2)}, u32[]{:S(2)}) collective-permute-start(bf16[896,448]{0,1:T(8,128)(2,1)} %get-tuple-element.12), channel_id=1, source_target_pairs={{0,2},{2,0},{4,6},{6,4},{8,10},{10,8},{12,14},{14,12},{1,3},{3,1},... | collective-permute-start | bytes 2408456 | tf_op jit(solution)/shard_map/ppermute | solution.py:188
  47.1 47.5 %collective-permute-start.3 = (bf16[128,8192]{1,0:T(8,128)(2,1)}, bf16[128,8192]{1,0:T(8,128)(2,1)}, u32[]{:S(2)}, u32[]{:S(2)}) collective-permute-start(bf16[128,8192]{1,0:T(8,128)(2,1)} %collective-permute-done), channel_id=1, source_target_pairs={{4,8},{6,10},{8,4},{10,6},{5,9},{7,11},{9,5},{11,7},{20,24},{22,26... | collective-permute-start | bytes 6291464 | tf_op jit(solution)/shard_map/ppermute | solution.py:167
  49.7 55.3 %collective-permute-start.2 = (bf16[128,8192]{1,0:T(8,128)(2,1)}, bf16[128,8192]{1,0:T(8,128)(2,1)}, u32[]{:S(2)}, u32[]{:S(2)}) collective-permute-start(bf16[128,8192]{1,0:T(8,128)(2,1)} %collective-permute-done.1), channel_id=1, source_target_pairs={{4,0},{6,2},{8,12},{10,14},{5,1},{7,3},{9,13},{11,15},{20,16},{22,... | collective-permute-start | bytes 6291464 | tf_op jit(solution)/shard_map/ppermute | solution.py:167
  53.7 22.3 %collective-permute-start.7 = (bf16[1152,448]{0,1:T(8,128)(2,1)S(1)}, bf16[1152,448]{0,1:T(8,128)(2,1)}, u32[]{:S(2)}, u32[]{:S(2)}) collective-permute-start(bf16[1152,448]{0,1:T(8,128)(2,1)S(1)} %collective-permute-done.6), channel_id=1, source_target_pairs={{0,16},{16,0},{1,17},{17,1},{2,18},{18,2},{3,19},{19,3},{4,20},{20... | collective-permute-start | bytes 3096584 | tf_op jit(solution)/shard_map/ppermute | solution.py:12
  67.8 25.4 %collective-permute-start.9 = (bf16[896,448]{0,1:T(8,128)(2,1)}, bf16[896,448]{0,1:T(8,128)(2,1)S(1)}, u32[]{:S(2)}, u32[]{:S(2)}) collective-permute-start(bf16[896,448]{0,1:T(8,128)(2,1)} %collective-permute-done.8), channel_id=1, source_target_pairs={{0,16},{16,0},{1,17},{17,1},{2,18},{18,2},{3,19},{19,3},{4,20},{20... | collective-permute-start | bytes 2408456 | tf_op jit(solution)/shard_map/ppermute | solution.py:12
  69.3 30.5 %collective-permute-start.10 = (bf16[896,448]{0,1:T(8,128)(2,1)}, bf16[896,448]{0,1:T(8,128)(2,1)S(1)}, u32[]{:S(2)}, u32[]{:S(2)}) collective-permute-start(bf16[896,448]{0,1:T(8,128)(2,1)} %get-tuple-element.13), channel_id=1, source_target_pairs={{0,2},{2,0},{4,6},{6,4},{8,10},{10,8},{12,14},{14,12},{1,3},{3,1},... | collective-permute-start | bytes 2408456 | tf_op jit(solution)/shard_map/ppermute | solution.py:188
  97.3 37.4 %collective-permute-start.12 = (bf16[128,6144]{1,0:T(8,128)(2,1)}, bf16[128,6144]{1,0:T(8,128)(2,1)}, u32[]{:S(2)}, u32[]{:S(2)}) collective-permute-start(bf16[128,6144]{1,0:T(8,128)(2,1)} %slice.148), channel_id=1, source_target_pairs={{4,0},{6,2},{8,12},{10,14},{5,1},{7,3},{9,13},{11,15},{20,16},{22,... | collective-permute-start | bytes 4718600 | tf_op jit(solution)/shard_map/ppermute | solution.py:167
  99.8 16.5 %collective-permute-start.11 = (bf16[896,448]{0,1:T(8,128)(2,1)S(1)}, bf16[896,448]{0,1:T(8,128)(2,1)S(1)}, u32[]{:S(2)}, u32[]{:S(2)}) collective-permute-start(bf16[896,448]{0,1:T(8,128)(2,1)S(1)} %collective-permute-done.10), channel_id=1, source_target_pairs={{0,16},{16,0},{1,17},{17,1},{2,18},{18,2},{3,19},{19,3},{4,20},{20... | collective-permute-start | bytes 2408456 | tf_op jit(solution)/shard_map/ppermute | solution.py:12
  102.9 39.7 %collective-permute-start.16 = (bf16[128,2048]{1,0:T(8,128)(2,1)}, bf16[128,2048]{1,0:T(8,128)(2,1)}, u32[]{:S(2)}, u32[]{:S(2)}) collective-permute-start(bf16[128,2048]{1,0:T(8,128)(2,1)} %slice.157), channel_id=1, source_target_pairs={{4,0},{6,2},{8,12},{10,14},{5,1},{7,3},{9,13},{11,15},{20,16},{22,... | collective-permute-start | bytes 1572872 | tf_op jit(solution)/shard_map/ppermute | solution.py:167
  145.4 10.4 %collective-permute-start.17 = (f32[128,896]{1,0:T(8,128)S(1)}, f32[128,896]{1,0:T(8,128)S(1)}, u32[]{:S(2)}, u32[]{:S(2)}) collective-permute-start(f32[128,896]{1,0:T(8,128)S(1)} %fusion.40), channel_id=1, source_target_pairs={{1,0},{3,2},{5,4},{7,6},{8,9},{10,11},{12,13},{14,15},{17,16},{19,... | collective-permute-start | bytes 1376264 | tf_op jit(solution)/shard_map/ppermute | solution.py:173
  147.4 11.1 %collective-permute-start.14 = (bf16[128,896]{1,0:T(8,128)(2,1)S(1)}, bf16[128,896]{1,0:T(8,128)(2,1)}, u32[]{:S(2)}, u32[]{:S(2)}) collective-permute-start(bf16[128,896]{1,0:T(8,128)(2,1)S(1)} %get-tuple-element.33), channel_id=1, source_target_pairs={{0,4},{2,6},{4,0},{6,2},{9,13},{11,15},{13,9},{15,11},{16,20},{18,... | collective-permute-start | bytes 688136 | tf_op jit(solution)/shard_map/ppermute | solution.py:176
  149.7 13.0 %collective-permute-start.15 = (bf16[128,896]{1,0:T(8,128)(2,1)S(1)}, bf16[128,896]{1,0:T(8,128)(2,1)}, u32[]{:S(2)}, u32[]{:S(2)}) collective-permute-start(bf16[128,896]{1,0:T(8,128)(2,1)S(1)} %get-tuple-element.32), channel_id=1, source_target_pairs={{0,8},{2,10},{13,5},{15,7},{4,12},{6,14},{9,1},{11,3},{16,24},{18,... | collective-permute-start | bytes 688136 | tf_op jit(solution)/shard_map/ppermute | solution.py:176
  172.0 13.1 %collective-permute-start.28 = (bf16[56,1792]{1,0:T(8,128)(2,1)S(1)}, bf16[56,1792]{1,0:T(8,128)(2,1)S(1)}, u32[]{:S(2)}, u32[]{:S(2)}) collective-permute-start(bf16[56,1792]{1,0:T(8,128)(2,1)S(1)} %get-tuple-element.57), channel_id=1, source_target_pairs={{0,8},{2,10},{4,12},{6,14},{8,0},{10,2},{12,4},{14,6},{1,9},{3,11}... | collective-permute-start | bytes 602120 | tf_op jit(solution)/shard_map/ppermute | solution.py:256
  172.1 17.2 %collective-permute-start.29 = (bf16[56,1792]{1,0:T(8,128)(2,1)S(1)}, bf16[56,1792]{1,0:T(8,128)(2,1)S(1)}, u32[]{:S(2)}, u32[]{:S(2)}) collective-permute-start(bf16[56,1792]{1,0:T(8,128)(2,1)S(1)} %get-tuple-element.56), channel_id=1, source_target_pairs={{0,10},{2,8},{4,14},{6,12},{8,2},{10,0},{12,6},{14,4},{1,11},{3,9}... | collective-permute-start | bytes 602120 | tf_op jit(solution)/shard_map/ppermute | solution.py:256
  175.4 13.9 %collective-permute-start.30 = (bf16[56,1792]{1,0:T(8,128)(2,1)S(1)}, bf16[56,1792]{1,0:T(8,128)(2,1)S(1)}, u32[]{:S(2)}, u32[]{:S(2)}) collective-permute-start(bf16[56,1792]{1,0:T(8,128)(2,1)S(1)} %get-tuple-element.55), channel_id=1, source_target_pairs={{0,4},{2,6},{4,0},{6,2},{8,12},{10,14},{12,8},{14,10},{1,5},{3,7},... | collective-permute-start | bytes 602120 | tf_op jit(solution)/shard_map/ppermute | solution.py:256
  175.4 16.6 %collective-permute-start.31 = (bf16[56,1792]{1,0:T(8,128)(2,1)S(1)}, bf16[56,1792]{1,0:T(8,128)(2,1)S(1)}, u32[]{:S(2)}, u32[]{:S(2)}) collective-permute-start(bf16[56,1792]{1,0:T(8,128)(2,1)S(1)} %get-tuple-element.54), channel_id=1, source_target_pairs={{0,6},{2,4},{4,2},{6,0},{8,14},{10,12},{12,10},{14,8},{1,7},{3,5},... | collective-permute-start | bytes 602120 | tf_op jit(solution)/shard_map/ppermute | solution.py:256
  192.0 21.5 %collective-permute-start.32 = (bf16[224,1792]{1,0:T(8,128)(2,1)S(1)}, bf16[224,1792]{1,0:T(8,128)(2,1)S(1)}, u32[]{:S(2)}, u32[]{:S(2)}) collective-permute-start(bf16[224,1792]{1,0:T(8,128)(2,1)S(1)} %constant_dynamic-update-slice_fusion), channel_id=1, source_target_pairs={{0,1},{1,0},{2,3},{3,2},{4,5},{5,4},{6,7},{7,6},{8,9},{9,8},{10,11... | collective-permute-start | bytes 2408456 | tf_op jit(solution)/shard_map/ppermute | solution.py:12
  193.1 15.2 %collective-permute-start.20 = (bf16[56,1792]{1,0:T(8,128)(2,1)S(1)}, bf16[56,1792]{1,0:T(8,128)(2,1)S(1)}, u32[]{:S(2)}, u32[]{:S(2)}) collective-permute-start(bf16[56,1792]{1,0:T(8,128)(2,1)S(1)} %get-tuple-element.46), channel_id=1, source_target_pairs={{0,12},{2,14},{4,8},{6,10},{8,4},{10,6},{12,0},{14,2},{1,13},{3,15... | collective-permute-start | bytes 602120 | tf_op jit(solution)/shard_map/ppermute | solution.py:256
  194.6 18.0 %collective-permute-start.21 = (bf16[56,1792]{1,0:T(8,128)(2,1)S(1)}, bf16[56,1792]{1,0:T(8,128)(2,1)S(1)}, u32[]{:S(2)}, u32[]{:S(2)}) collective-permute-start(bf16[56,1792]{1,0:T(8,128)(2,1)S(1)} %get-tuple-element.49), channel_id=1, source_target_pairs={{0,14},{2,12},{4,10},{6,8},{8,6},{10,4},{12,2},{14,0},{1,15},{3,13... | collective-permute-start | bytes 602120 | tf_op jit(solution)/shard_map/ppermute | solution.py:256
  194.6 18.0 %collective-permute-start.22 = (bf16[56,1792]{1,0:T(8,128)(2,1)S(1)}, bf16[56,1792]{1,0:T(8,128)(2,1)S(1)}, u32[]{:S(2)}, u32[]{:S(2)}) collective-permute-start(bf16[56,1792]{1,0:T(8,128)(2,1)S(1)} %get-tuple-element.47), channel_id=1, source_target_pairs={{0,2},{2,0},{4,6},{6,4},{8,10},{10,8},{12,14},{14,12},{1,3},{3,1},... | collective-permute-start | bytes 602120 | tf_op jit(solution)/shard_map/ppermute | solution.py:256
  225.6 13.3 %collective-permute-start.34 = (bf16[56,1792]{1,0:T(8,128)(2,1)S(1)}, bf16[56,1792]{1,0:T(8,128)(2,1)S(1)}, u32[]{:S(2)}, u32[]{:S(2)}) collective-permute-start(bf16[56,1792]{1,0:T(8,128)(2,1)S(1)} %get-tuple-element.50), channel_id=1, source_target_pairs={{0,8},{2,10},{4,12},{6,14},{8,0},{10,2},{12,4},{14,6},{1,9},{3,11}... | collective-permute-start | bytes 602120 | tf_op jit(solution)/shard_map/ppermute | solution.py:256
  225.7 17.5 %collective-permute-start.35 = (bf16[56,1792]{1,0:T(8,128)(2,1)S(1)}, bf16[56,1792]{1,0:T(8,128)(2,1)S(1)}, u32[]{:S(2)}, u32[]{:S(2)}) collective-permute-start(bf16[56,1792]{1,0:T(8,128)(2,1)S(1)} %get-tuple-element.53), channel_id=1, source_target_pairs={{0,10},{2,8},{4,14},{6,12},{8,2},{10,0},{12,6},{14,4},{1,11},{3,9}... | collective-permute-start | bytes 602120 | tf_op jit(solution)/shard_map/ppermute | solution.py:256
  229.0 15.5 %collective-permute-start.36 = (bf16[56,1792]{1,0:T(8,128)(2,1)S(1)}, bf16[56,1792]{1,0:T(8,128)(2,1)S(1)}, u32[]{:S(2)}, u32[]{:S(2)}) collective-permute-start(bf16[56,1792]{1,0:T(8,128)(2,1)S(1)} %get-tuple-element.52), channel_id=1, source_target_pairs={{0,4},{2,6},{4,0},{6,2},{8,12},{10,14},{12,8},{14,10},{1,5},{3,7},... | collective-permute-start | bytes 602120 | tf_op jit(solution)/shard_map/ppermute | solution.py:256
  229.4 18.0 %collective-permute-start.37 = (bf16[56,1792]{1,0:T(8,128)(2,1)S(1)}, bf16[56,1792]{1,0:T(8,128)(2,1)S(1)}, u32[]{:S(2)}, u32[]{:S(2)}) collective-permute-start(bf16[56,1792]{1,0:T(8,128)(2,1)S(1)} %get-tuple-element.51), channel_id=1, source_target_pairs={{0,6},{2,4},{4,2},{6,0},{8,14},{10,12},{12,10},{14,8},{1,7},{3,5},... | collective-permute-start | bytes 602120 | tf_op jit(solution)/shard_map/ppermute | solution.py:256
  232.7 25.7 %collective-permute-start.25 = (bf16[56,1792]{1,0:T(8,128)(2,1)S(1)}, bf16[56,1792]{1,0:T(8,128)(2,1)S(1)}, u32[]{:S(2)}, u32[]{:S(2)}) collective-permute-start(bf16[56,1792]{1,0:T(8,128)(2,1)S(1)} %get-tuple-element.42), channel_id=1, source_target_pairs={{0,12},{2,14},{4,8},{6,10},{8,4},{10,6},{12,0},{14,2},{1,13},{3,15... | collective-permute-start | bytes 602120 | tf_op jit(solution)/shard_map/ppermute | solution.py:256
  239.0 24.6 %collective-permute-start.26 = (bf16[56,1792]{1,0:T(8,128)(2,1)S(1)}, bf16[56,1792]{1,0:T(8,128)(2,1)S(1)}, u32[]{:S(2)}, u32[]{:S(2)}) collective-permute-start(bf16[56,1792]{1,0:T(8,128)(2,1)S(1)} %get-tuple-element.45), channel_id=1, source_target_pairs={{0,14},{2,12},{4,10},{6,8},{8,6},{10,4},{12,2},{14,0},{1,15},{3,13... | collective-permute-start | bytes 602120 | tf_op jit(solution)/shard_map/ppermute | solution.py:256
  243.3 20.3 %collective-permute-start.27 = (bf16[56,1792]{1,0:T(8,128)(2,1)S(1)}, bf16[56,1792]{1,0:T(8,128)(2,1)S(1)}, u32[]{:S(2)}, u32[]{:S(2)}) collective-permute-start(bf16[56,1792]{1,0:T(8,128)(2,1)S(1)} %get-tuple-element.43), channel_id=1, source_target_pairs={{0,2},{2,0},{4,6},{6,4},{8,10},{10,8},{12,14},{14,12},{1,3},{3,1},... | collective-permute-start | bytes 602120 | tf_op jit(solution)/shard_map/ppermute | solution.py:256
  (26 other events, 452.3 us)

commit v8 on v7

--- a/solution.py
+++ b/solution.py
@@ -312,10 +312,7 @@
 
     quarter = expert_count // 4
     turns = list(range(expert_count))
-    parts = [
-        turns[3 * quarter :] + turns[:quarter],
-        turns[2 * quarter : 3 * quarter] + turns[quarter : 2 * quarter],
-    ]
+    parts = [turns[2 * quarter :], turns[: 2 * quarter]]
     arrived = []
     for part in parts:
         dispatch_matrix = jnp.any(slots_of(part), axis=1).astype(jnp.bfloat16)

time: 266 us -> 266 us (level)
  no operation moved by 1% of the time
where the time goes in v8:
time: 266 us; the launch traced here: 263 us
  waiting for transfers between devices  145 us (55%)
  starting transfers between devices  55.4 us (21%)
  matrix products  35 us (13%)
  other arithmetic  15.8 us (6%)
  local copies, waits for them, and re-layouts  11.5 us (4%)
    ppermute x14, waiting for transfers between devices, exchange(): lax.ppermute(split[i], 'expert', [(e, e ^ k) for e in range(expert_count)])  55.6 us
    ppermute x9, waiting for transfers between devices, swap_halves(): return lax.ppermute(array, axis_name, [(0, 1), (1, 0)])  32.1 us
    ppermute x2, waiting for transfers between devices, project_line(): near = [lax.ppermute(p, 'expert', partner) for p in pieces[:2]]  22 us
    ppermute x14, starting transfers between devices, exchange(): lax.ppermute(split[i], 'expert', [(e, e ^ k) for e in range(expert_count)])  16.3 us
    ppermute x6, waiting for transfers between devices, hop(): return lax.ppermute(block, 'expert', chip_pairs(moves))  15 us
    ppermute x6, starting transfers between devices, hop(): return lax.ppermute(block, 'expert', chip_pairs(moves))  13.8 us
    dot_general x1, matrix products, project_line(): early = jnp.dot(blocks, columns, preferred_element_type=jnp.float32)  12 us
    ppermute x2, waiting for transfers between devices, project_line(): lax.ppermute(after(p, swap), 'expert', partner)  11.7 us
  transfers between devices with their start and end apart: 38, of which 21 were waited for; matrix products, arithmetic and copies ran while one was open for 20% of the time, Pallas kernels for 0%

profile of v8, /device:TPU:19, one launch (start us, length us, event | category | flops | bytes accessed | tf_op | source)
XLA Modules:
  0.0 263.0 jit_solution(7220208780242948140)
XLA Ops:
  6.5 22.0 %collective-permute-done.4 = bf16[1152,448]{0,1:T(8,128)(2,1)S(1)} collective-permute-done((bf16[1152,448]{0,1:T(8,128)(2,1)S(1)}, bf16[1152,448]{0,1:T(8,128)(2,1)S(1)}, u32[]{:S(2)}, u32[]{:S(2)}) %collective-permute-start.4) | collective-permute-done | bytes 1032224 | tf_op jit(solution)/shard_map/ppermute | solution.py:184
  29.7 2.7 %constant_dynamic-slice_fusion = (bf16[896,448]{0,1:T(8,128)(2,1)}, bf16[896,448]{0,1:T(8,128)(2,1)}) fusion(bf16[8192,448]{0,1:T(8,128)(2,1)} %param.14, s32[]{:T(128)S(6)} %select_n.204, s32[]{:T(128)S(6)} %select_n.202), kind=kLoop, calls=%fused_computation.134 | loop fusion | bytes 3211272 | tf_op jit(solution)/shard_map/dynamic_slice | solution.py:179
  32.4 14.4 %collective-permute-done = bf16[128,8192]{1,0:T(8,128)(2,1)} collective-permute-done((bf16[128,8192]{1,0:T(8,128)(2,1)}, bf16[128,8192]{1,0:T(8,128)(2,1)}, u32[]{:S(2)}, u32[]{:S(2)}) %collective-permute-start) | collective-permute-done | bytes 2097184 | tf_op jit(solution)/shard_map/ppermute | solution.py:167
  49.7 4.0 %collective-permute-start.2 = (bf16[128,8192]{1,0:T(8,128)(2,1)}, bf16[128,8192]{1,0:T(8,128)(2,1)}, u32[]{:S(2)}, u32[]{:S(2)}) collective-permute-start(bf16[128,8192]{1,0:T(8,128)(2,1)} %collective-permute-done.1), channel_id=1, source_target_pairs={{4,0},{6,2},{8,12},{10,14},{5,1},{7,3},{9,13},{11,15},{20,16},{22,... | collective-permute-start | bytes 6291464 | tf_op jit(solution)/shard_map/ppermute | solution.py:167
  56.1 11.7 %collective-permute-done.8 = bf16[896,448]{0,1:T(8,128)(2,1)} collective-permute-done((bf16[896,448]{0,1:T(8,128)(2,1)}, bf16[896,448]{0,1:T(8,128)(2,1)}, u32[]{:S(2)}, u32[]{:S(2)}) %collective-permute-start.8) | collective-permute-done | bytes 802848 | tf_op jit(solution)/shard_map/ppermute | solution.py:188
  69.7 6.3 %collective-permute-done.7 = bf16[1152,448]{0,1:T(8,128)(2,1)} collective-permute-done((bf16[1152,448]{0,1:T(8,128)(2,1)S(1)}, bf16[1152,448]{0,1:T(8,128)(2,1)}, u32[]{:S(2)}, u32[]{:S(2)}) %collective-permute-start.7) | collective-permute-done | bytes 1032224 | tf_op jit(solution)/shard_map/ppermute | solution.py:12
  76.3 16.9 %collective-permute-done.9 = bf16[896,448]{0,1:T(8,128)(2,1)S(1)} collective-permute-done((bf16[896,448]{0,1:T(8,128)(2,1)}, bf16[896,448]{0,1:T(8,128)(2,1)S(1)}, u32[]{:S(2)}, u32[]{:S(2)}) %collective-permute-start.9) | collective-permute-done | bytes 802848 | tf_op jit(solution)/shard_map/ppermute | solution.py:12
  94.6 2.7 %slice.148 = bf16[128,6144]{1,0:T(8,128)(2,1)} slice(bf16[128,8192]{1,0:T(8,128)(2,1)} %collective-permute-done.3), slice={[0:128], [0:6144]} | slice | bytes 3145728 | tf_op jit(solution)/shard_map/slice | solution.py:191
  97.3 2.5 collective-permute-start.12
  102.9 2.1 collective-permute-start.16
  105.0 3.1 %broadcast_select_fusion.2 = bf16[128,8192]{1,0:T(8,128)(2,1)} fusion(bf16[128,8192]{1,0:T(8,128)(2,1)} %collective-permute-done.1, bf16[128,8192]{1,0:T(8,128)(2,1)} %collective-permute-done.2, pred[]{:T(512)S(6)} %or.3), kind=kLoop, calls=%fused_computation.38 | loop fusion | flops 1048576 | bytes 6291457 | tf_op jit(solution)/shard_map/jit(_where)/select_n | solution.py:206
  108.1 8.1 %collective-permute-done.11 = bf16[896,448]{0,1:T(8,128)(2,1)S(1)} collective-permute-done((bf16[896,448]{0,1:T(8,128)(2,1)S(1)}, bf16[896,448]{0,1:T(8,128)(2,1)S(1)}, u32[]{:S(2)}, u32[]{:S(2)}) %collective-permute-start.11) | collective-permute-done | bytes 802848 | tf_op jit(solution)/shard_map/ppermute | solution.py:12
  122.4 12.0 %fusion = f32[512,896]{1,0:T(8,128)S(1)} fusion(bf16[8192,448]{0,1:T(8,128)(2,1)S(1)} %get-tuple-element.26, bf16[8192,448]{0,1:T(8,128)(2,1)S(1)} %get-tuple-element.27, bf16[128,8192]{1,0:T(8,128)(2,1)} %collective-permute-done.3, bf16[128,8192]{1,0:T(8,128)(2,1)S(1)} %copy-done.3, bf16[128,8192]{1,0:T(8,128)(2,1)} %collective-permute-done, ...), kind=kOutput, calls=%fused_computation.5 | convolution fusion | flops 7579107328 | bytes 24903680 | tf_op jit(solution)/shard_map/dot_general | solution.py:208
  136.0 5.1 %fusion.34 = f32[128,896]{1,0:T(8,128)S(1)} fusion(bf16[128,6144]{1,0:T(8,128)(2,1)} %collective-permute-done.12, bf16[8192,448]{0,1:T(8,128)(2,1)S(1)} %get-tuple-element.27, bf16[8192,448]{0,1:T(8,128)(2,1)S(1)} %get-tuple-element.26), kind=kOutput, calls=%fused_computation.42 | convolution fusion | flops 1431306240 | bytes 16711680 | tf_op jit(solution)/shard_map/dot_general | solution.py:217
  142.6 2.7 %fusion.40 = f32[128,896]{1,0:T(8,128)S(1)} fusion(f32[128,896]{1,0:T(8,128)S(1)} %fusion.34, bf16[128,2048]{1,0:T(8,128)(2,1)} %collective-permute-done.16, bf16[8192,448]{0,1:T(8,128)(2,1)S(1)} %get-tuple-element.27, bf16[8192,448]{0,1:T(8,128)(2,1)S(1)} %get-tuple-element.26, f32[512,896]{1,0:T(8,128)S(1)} %fusion, pred[]{:T(512)S(6)} %or.3), kind=kOutput, calls=%fused_computation.44 | convolution fusion | flops 477331456 | bytes 16580609 | tf_op jit(solution)/shard_map/dot_general | solution.py:223
  147.4 2.3 collective-permute-start.14
  149.7 6.1 %collective-permute-start.15 = (bf16[128,896]{1,0:T(8,128)(2,1)S(1)}, bf16[128,896]{1,0:T(8,128)(2,1)}, u32[]{:S(2)}, u32[]{:S(2)}) collective-permute-start(bf16[128,896]{1,0:T(8,128)(2,1)S(1)} %get-tuple-element.32), channel_id=1, source_target_pairs={{0,8},{2,10},{13,5},{15,7},{4,12},{6,14},{9,1},{11,3},{16,24},{18,... | collective-permute-start | bytes 688136 | tf_op jit(solution)/shard_map/ppermute | solution.py:176
  158.5 4.3 %collective-permute-done.15 = bf16[128,896]{1,0:T(8,128)(2,1)} collective-permute-done((bf16[128,896]{1,0:T(8,128)(2,1)S(1)}, bf16[128,896]{1,0:T(8,128)(2,1)}, u32[]{:S(2)}, u32[]{:S(2)}) %collective-permute-start.15) | collective-permute-done | bytes 229408 | tf_op jit(solution)/shard_map/ppermute | solution.py:176
  162.7 2.6 collective-permute-done.18
  167.8 2.2 collective-permute-start.19
  171.5 3.3 %collective-permute-start.21 = (bf16[56,1792]{1,0:T(8,128)(2,1)S(1)}, bf16[56,1792]{1,0:T(8,128)(2,1)S(1)}, u32[]{:S(2)}, u32[]{:S(2)}) collective-permute-start(bf16[56,1792]{1,0:T(8,128)(2,1)S(1)} %get-tuple-element.48), channel_id=1, source_target_pairs={{0,10},{2,8},{4,14},{6,12},{8,2},{10,0},{12,6},{14,4},{1,11},{3,9}... | collective-permute-start | bytes 602120 | tf_op jit(solution)/shard_map/ppermute | solution.py:256
  175.7 2.4 collective-permute-start.32
  178.2 6.9 %collective-permute-done.30 = bf16[56,1792]{1,0:T(8,128)(2,1)S(1)} collective-permute-done((bf16[56,1792]{1,0:T(8,128)(2,1)S(1)}, bf16[56,1792]{1,0:T(8,128)(2,1)S(1)}, u32[]{:S(2)}, u32[]{:S(2)}) %collective-permute-start.30) | collective-permute-done | bytes 200736 | tf_op jit(solution)/shard_map/ppermute | solution.py:256
  186.3 2.2 collective-permute-start.23
  188.6 3.0 %collective-permute-done.32 = bf16[56,1792]{1,0:T(8,128)(2,1)S(1)} collective-permute-done((bf16[56,1792]{1,0:T(8,128)(2,1)S(1)}, bf16[56,1792]{1,0:T(8,128)(2,1)S(1)}, u32[]{:S(2)}, u32[]{:S(2)}) %collective-permute-start.32) | collective-permute-done | bytes 200736 | tf_op jit(solution)/shard_map/ppermute | solution.py:256
  193.3 8.9 %collective-permute-done.22 = bf16[56,1792]{1,0:T(8,128)(2,1)S(1)} collective-permute-done((bf16[56,1792]{1,0:T(8,128)(2,1)S(1)}, bf16[56,1792]{1,0:T(8,128)(2,1)S(1)}, u32[]{:S(2)}, u32[]{:S(2)}) %collective-permute-start.22) | collective-permute-done | bytes 200736 | tf_op jit(solution)/shard_map/ppermute | solution.py:256
  202.2 5.2 %collective-permute-done.23 = bf16[56,1792]{1,0:T(8,128)(2,1)S(1)} collective-permute-done((bf16[56,1792]{1,0:T(8,128)(2,1)S(1)}, bf16[56,1792]{1,0:T(8,128)(2,1)S(1)}, u32[]{:S(2)}, u32[]{:S(2)}) %collective-permute-start.23) | collective-permute-done | bytes 200736 | tf_op jit(solution)/shard_map/ppermute | solution.py:256
  220.7 2.4 collective-permute-start.37
  230.2 4.4 %collective-permute-done.37 = bf16[56,1792]{1,0:T(8,128)(2,1)S(1)} collective-permute-done((bf16[56,1792]{1,0:T(8,128)(2,1)S(1)}, bf16[56,1792]{1,0:T(8,128)(2,1)S(1)}, u32[]{:S(2)}, u32[]{:S(2)}) %collective-permute-start.37) | collective-permute-done | bytes 200736 | tf_op jit(solution)/shard_map/ppermute | solution.py:256
  236.8 15.1 %collective-permute-done.27 = bf16[56,1792]{1,0:T(8,128)(2,1)S(1)} collective-permute-done((bf16[56,1792]{1,0:T(8,128)(2,1)S(1)}, bf16[56,1792]{1,0:T(8,128)(2,1)S(1)}, u32[]{:S(2)}, u32[]{:S(2)}) %collective-permute-start.27) | collective-permute-done | bytes 200736 | tf_op jit(solution)/shard_map/ppermute | solution.py:256
  251.9 5.3 %collective-permute-done.28 = bf16[56,1792]{1,0:T(8,128)(2,1)S(1)} collective-permute-done((bf16[56,1792]{1,0:T(8,128)(2,1)S(1)}, bf16[56,1792]{1,0:T(8,128)(2,1)S(1)}, u32[]{:S(2)}, u32[]{:S(2)}) %collective-permute-start.28) | collective-permute-done | bytes 200736 | tf_op jit(solution)/shard_map/ppermute | solution.py:256
  257.2 4.3 %collective-permute-done.29 = bf16[56,1792]{1,0:T(8,128)(2,1)S(1)} collective-permute-done((bf16[56,1792]{1,0:T(8,128)(2,1)S(1)}, bf16[56,1792]{1,0:T(8,128)(2,1)S(1)}, u32[]{:S(2)}, u32[]{:S(2)}) %collective-permute-start.29) | collective-permute-done | bytes 200736 | tf_op jit(solution)/shard_map/ppermute | solution.py:256
  (157 shorter events, 65.3 us)
Async XLA Ops:
  0.0 46.8 %collective-permute-start = (bf16[128,8192]{1,0:T(8,128)(2,1)}, bf16[128,8192]{1,0:T(8,128)(2,1)}, u32[]{:S(2)}, u32[]{:S(2)}) collective-permute-start(bf16[128,8192]{1,0:T(8,128)(2,1)} %param.13), channel_id=1, source_target_pairs={{0,4},{2,6},{4,0},{6,2},{8,12},{10,14},{12,8},{14,10},{1,5},{3,7},... | collective-permute-start | bytes 6291464 | tf_op jit(solution)/shard_map/ppermute | solution.py:167
  1.3 48.4 %collective-permute-start.1 = (bf16[128,8192]{1,0:T(8,128)(2,1)}, bf16[128,8192]{1,0:T(8,128)(2,1)}, u32[]{:S(2)}, u32[]{:S(2)}) collective-permute-start(bf16[128,8192]{1,0:T(8,128)(2,1)} %param.13), channel_id=1, source_target_pairs={{4,8},{6,10},{8,4},{10,6},{5,9},{7,11},{9,5},{11,7},{20,24},{22,26... | collective-permute-start | bytes 6291464 | tf_op jit(solution)/shard_map/ppermute | solution.py:167
  4.9 23.5 %collective-permute-start.4 = (bf16[1152,448]{0,1:T(8,128)(2,1)S(1)}, bf16[1152,448]{0,1:T(8,128)(2,1)S(1)}, u32[]{:S(2)}, u32[]{:S(2)}) collective-permute-start(bf16[1152,448]{0,1:T(8,128)(2,1)S(1)} %get-tuple-element.31), channel_id=1, source_target_pairs={{0,2},{2,0},{4,6},{6,4},{8,10},{10,8},{12,14},{14,12},{1,3},{3,1},... | collective-permute-start | bytes 3096584 | tf_op jit(solution)/shard_map/ppermute | solution.py:184
  5.3 48.4 %collective-permute-start.6 = (bf16[1152,448]{0,1:T(8,128)(2,1)S(1)}, bf16[1152,448]{0,1:T(8,128)(2,1)S(1)}, u32[]{:S(2)}, u32[]{:S(2)}) collective-permute-start(bf16[1152,448]{0,1:T(8,128)(2,1)S(1)} %get-tuple-element.30), channel_id=1, source_target_pairs={{0,2},{2,0},{4,6},{6,4},{8,10},{10,8},{12,14},{14,12},{1,3},{3,1},... | collective-permute-start | bytes 3096584 | tf_op jit(solution)/shard_map/ppermute | solution.py:184
  28.5 40.6 %collective-permute-start.5 = (bf16[1152,448]{0,1:T(8,128)(2,1)S(1)}, bf16[1152,448]{0,1:T(8,128)(2,1)}, u32[]{:S(2)}, u32[]{:S(2)}) collective-permute-start(bf16[1152,448]{0,1:T(8,128)(2,1)S(1)} %collective-permute-done.4), channel_id=1, source_target_pairs={{0,16},{16,0},{1,17},{17,1},{2,18},{18,2},{3,19},{19,3},{4,20},{20... | collective-permute-start | bytes 3096584 | tf_op jit(solution)/shard_map/ppermute | solution.py:12
  46.8 21.0 %collective-permute-start.8 = (bf16[896,448]{0,1:T(8,128)(2,1)}, bf16[896,448]{0,1:T(8,128)(2,1)}, u32[]{:S(2)}, u32[]{:S(2)}) collective-permute-start(bf16[896,448]{0,1:T(8,128)(2,1)} %get-tuple-element.12), channel_id=1, source_target_pairs={{0,2},{2,0},{4,6},{6,4},{8,10},{10,8},{12,14},{14,12},{1,3},{3,1},... | collective-permute-start | bytes 2408456 | tf_op jit(solution)/shard_map/ppermute | solution.py:188
  47.1 47.5 %collective-permute-start.3 = (bf16[128,8192]{1,0:T(8,128)(2,1)}, bf16[128,8192]{1,0:T(8,128)(2,1)}, u32[]{:S(2)}, u32[]{:S(2)}) collective-permute-start(bf16[128,8192]{1,0:T(8,128)(2,1)} %collective-permute-done), channel_id=1, source_target_pairs={{4,8},{6,10},{8,4},{10,6},{5,9},{7,11},{9,5},{11,7},{20,24},{22,26... | collective-permute-start | bytes 6291464 | tf_op jit(solution)/shard_map/ppermute | solution.py:167
  49.7 55.3 %collective-permute-start.2 = (bf16[128,8192]{1,0:T(8,128)(2,1)}, bf16[128,8192]{1,0:T(8,128)(2,1)}, u32[]{:S(2)}, u32[]{:S(2)}) collective-permute-start(bf16[128,8192]{1,0:T(8,128)(2,1)} %collective-permute-done.1), channel_id=1, source_target_pairs={{4,0},{6,2},{8,12},{10,14},{5,1},{7,3},{9,13},{11,15},{20,16},{22,... | collective-permute-start | bytes 6291464 | tf_op jit(solution)/shard_map/ppermute | solution.py:167
  53.7 22.3 %collective-permute-start.7 = (bf16[1152,448]{0,1:T(8,128)(2,1)S(1)}, bf16[1152,448]{0,1:T(8,128)(2,1)}, u32[]{:S(2)}, u32[]{:S(2)}) collective-permute-start(bf16[1152,448]{0,1:T(8,128)(2,1)S(1)} %collective-permute-done.6), channel_id=1, source_target_pairs={{0,16},{16,0},{1,17},{17,1},{2,18},{18,2},{3,19},{19,3},{4,20},{20... | collective-permute-start | bytes 3096584 | tf_op jit(solution)/shard_map/ppermute | solution.py:12
  67.8 25.4 %collective-permute-start.9 = (bf16[896,448]{0,1:T(8,128)(2,1)}, bf16[896,448]{0,1:T(8,128)(2,1)S(1)}, u32[]{:S(2)}, u32[]{:S(2)}) collective-permute-start(bf16[896,448]{0,1:T(8,128)(2,1)} %collective-permute-done.8), channel_id=1, source_target_pairs={{0,16},{16,0},{1,17},{17,1},{2,18},{18,2},{3,19},{19,3},{4,20},{20... | collective-permute-start | bytes 2408456 | tf_op jit(solution)/shard_map/ppermute | solution.py:12
  69.3 30.4 %collective-permute-start.10 = (bf16[896,448]{0,1:T(8,128)(2,1)}, bf16[896,448]{0,1:T(8,128)(2,1)S(1)}, u32[]{:S(2)}, u32[]{:S(2)}) collective-permute-start(bf16[896,448]{0,1:T(8,128)(2,1)} %get-tuple-element.13), channel_id=1, source_target_pairs={{0,2},{2,0},{4,6},{6,4},{8,10},{10,8},{12,14},{14,12},{1,3},{3,1},... | collective-permute-start | bytes 2408456 | tf_op jit(solution)/shard_map/ppermute | solution.py:188
  97.3 37.4 %collective-permute-start.12 = (bf16[128,6144]{1,0:T(8,128)(2,1)}, bf16[128,6144]{1,0:T(8,128)(2,1)}, u32[]{:S(2)}, u32[]{:S(2)}) collective-permute-start(bf16[128,6144]{1,0:T(8,128)(2,1)} %slice.148), channel_id=1, source_target_pairs={{4,0},{6,2},{8,12},{10,14},{5,1},{7,3},{9,13},{11,15},{20,16},{22,... | collective-permute-start | bytes 4718600 | tf_op jit(solution)/shard_map/ppermute | solution.py:167
  99.8 16.5 %collective-permute-start.11 = (bf16[896,448]{0,1:T(8,128)(2,1)S(1)}, bf16[896,448]{0,1:T(8,128)(2,1)S(1)}, u32[]{:S(2)}, u32[]{:S(2)}) collective-permute-start(bf16[896,448]{0,1:T(8,128)(2,1)S(1)} %collective-permute-done.10), channel_id=1, source_target_pairs={{0,16},{16,0},{1,17},{17,1},{2,18},{18,2},{3,19},{19,3},{4,20},{20... | collective-permute-start | bytes 2408456 | tf_op jit(solution)/shard_map/ppermute | solution.py:12
  102.9 39.7 %collective-permute-start.16 = (bf16[128,2048]{1,0:T(8,128)(2,1)}, bf16[128,2048]{1,0:T(8,128)(2,1)}, u32[]{:S(2)}, u32[]{:S(2)}) collective-permute-start(bf16[128,2048]{1,0:T(8,128)(2,1)} %slice.157), channel_id=1, source_target_pairs={{4,0},{6,2},{8,12},{10,14},{5,1},{7,3},{9,13},{11,15},{20,16},{22,... | collective-permute-start | bytes 1572872 | tf_op jit(solution)/shard_map/ppermute | solution.py:167
  145.4 10.4 %collective-permute-start.17 = (f32[128,896]{1,0:T(8,128)S(1)}, f32[128,896]{1,0:T(8,128)S(1)}, u32[]{:S(2)}, u32[]{:S(2)}) collective-permute-start(f32[128,896]{1,0:T(8,128)S(1)} %fusion.40), channel_id=1, source_target_pairs={{1,0},{3,2},{5,4},{7,6},{8,9},{10,11},{12,13},{14,15},{17,16},{19,... | collective-permute-start | bytes 1376264 | tf_op jit(solution)/shard_map/ppermute | solution.py:173
  147.4 11.1 %collective-permute-start.14 = (bf16[128,896]{1,0:T(8,128)(2,1)S(1)}, bf16[128,896]{1,0:T(8,128)(2,1)}, u32[]{:S(2)}, u32[]{:S(2)}) collective-permute-start(bf16[128,896]{1,0:T(8,128)(2,1)S(1)} %get-tuple-element.33), channel_id=1, source_target_pairs={{0,4},{2,6},{4,0},{6,2},{9,13},{11,15},{13,9},{15,11},{16,20},{18,... | collective-permute-start | bytes 688136 | tf_op jit(solution)/shard_map/ppermute | solution.py:176
  149.7 13.0 %collective-permute-start.15 = (bf16[128,896]{1,0:T(8,128)(2,1)S(1)}, bf16[128,896]{1,0:T(8,128)(2,1)}, u32[]{:S(2)}, u32[]{:S(2)}) collective-permute-start(bf16[128,896]{1,0:T(8,128)(2,1)S(1)} %get-tuple-element.32), channel_id=1, source_target_pairs={{0,8},{2,10},{13,5},{15,7},{4,12},{6,14},{9,1},{11,3},{16,24},{18,... | collective-permute-start | bytes 688136 | tf_op jit(solution)/shard_map/ppermute | solution.py:176
  156.5 8.8 %collective-permute-start.18 = (bf16[128,896]{1,0:T(8,128)(2,1)}, bf16[128,896]{1,0:T(8,128)(2,1)S(1)}, u32[]{:S(2)}, u32[]{:S(2)}) collective-permute-start(bf16[128,896]{1,0:T(8,128)(2,1)} %add_convert_fusion), channel_id=1, source_target_pairs={{0,12},{2,14},{13,1},{15,3},{4,8},{6,10},{9,5},{11,7},{16,28},{18,... | collective-permute-start | bytes 688136 | tf_op jit(solution)/shard_map/ppermute | solution.py:176
  171.5 21.8 %collective-permute-start.20 = (bf16[56,1792]{1,0:T(8,128)(2,1)S(1)}, bf16[56,1792]{1,0:T(8,128)(2,1)S(1)}, u32[]{:S(2)}, u32[]{:S(2)}) collective-permute-start(bf16[56,1792]{1,0:T(8,128)(2,1)S(1)} %get-tuple-element.49), channel_id=1, source_target_pairs={{0,8},{2,10},{4,12},{6,14},{8,0},{10,2},{12,4},{14,6},{1,9},{3,11}... | collective-permute-start | bytes 602120 | tf_op jit(solution)/shard_map/ppermute | solution.py:256
  171.5 21.7 %collective-permute-start.21 = (bf16[56,1792]{1,0:T(8,128)(2,1)S(1)}, bf16[56,1792]{1,0:T(8,128)(2,1)S(1)}, u32[]{:S(2)}, u32[]{:S(2)}) collective-permute-start(bf16[56,1792]{1,0:T(8,128)(2,1)S(1)} %get-tuple-element.48), channel_id=1, source_target_pairs={{0,10},{2,8},{4,14},{6,12},{8,2},{10,0},{12,6},{14,4},{1,11},{3,9}... | collective-permute-start | bytes 602120 | tf_op jit(solution)/shard_map/ppermute | solution.py:256
  175.4 9.7 %collective-permute-start.30 = (bf16[56,1792]{1,0:T(8,128)(2,1)S(1)}, bf16[56,1792]{1,0:T(8,128)(2,1)S(1)}, u32[]{:S(2)}, u32[]{:S(2)}) collective-permute-start(bf16[56,1792]{1,0:T(8,128)(2,1)S(1)} %get-tuple-element.57), channel_id=1, source_target_pairs={{0,2},{2,0},{4,6},{6,4},{8,10},{10,8},{12,14},{14,12},{1,3},{3,1},... | collective-permute-start | bytes 602120 | tf_op jit(solution)/shard_map/ppermute | solution.py:256
  175.7 10.7 %collective-permute-start.31 = (bf16[56,1792]{1,0:T(8,128)(2,1)S(1)}, bf16[56,1792]{1,0:T(8,128)(2,1)S(1)}, u32[]{:S(2)}, u32[]{:S(2)}) collective-permute-start(bf16[56,1792]{1,0:T(8,128)(2,1)S(1)} %get-tuple-element.56), channel_id=1, source_target_pairs={{0,4},{2,6},{4,0},{6,2},{8,12},{10,14},{12,8},{14,10},{1,5},{3,7},... | collective-permute-start | bytes 602120 | tf_op jit(solution)/shard_map/ppermute | solution.py:256
  175.7 15.9 %collective-permute-start.32 = (bf16[56,1792]{1,0:T(8,128)(2,1)S(1)}, bf16[56,1792]{1,0:T(8,128)(2,1)S(1)}, u32[]{:S(2)}, u32[]{:S(2)}) collective-permute-start(bf16[56,1792]{1,0:T(8,128)(2,1)S(1)} %get-tuple-element.55), channel_id=1, source_target_pairs={{0,6},{2,4},{4,2},{6,0},{8,14},{10,12},{12,10},{14,8},{1,7},{3,5},... | collective-permute-start | bytes 602120 | tf_op jit(solution)/shard_map/ppermute | solution.py:256
  185.1 17.1 %collective-permute-start.22 = (bf16[56,1792]{1,0:T(8,128)(2,1)S(1)}, bf16[56,1792]{1,0:T(8,128)(2,1)S(1)}, u32[]{:S(2)}, u32[]{:S(2)}) collective-permute-start(bf16[56,1792]{1,0:T(8,128)(2,1)S(1)} %get-tuple-element.47), channel_id=1, source_target_pairs={{0,12},{2,14},{4,8},{6,10},{8,4},{10,6},{12,0},{14,2},{1,13},{3,15... | collective-permute-start | bytes 602120 | tf_op jit(solution)/shard_map/ppermute | solution.py:256
  186.3 21.1 %collective-permute-start.23 = (bf16[56,1792]{1,0:T(8,128)(2,1)S(1)}, bf16[56,1792]{1,0:T(8,128)(2,1)S(1)}, u32[]{:S(2)}, u32[]{:S(2)}) collective-permute-start(bf16[56,1792]{1,0:T(8,128)(2,1)S(1)} %get-tuple-element.46), channel_id=1, source_target_pairs={{0,14},{2,12},{4,10},{6,8},{8,6},{10,4},{12,2},{14,0},{1,15},{3,13... | collective-permute-start | bytes 602120 | tf_op jit(solution)/shard_map/ppermute | solution.py:256
  191.6 17.0 %collective-permute-start.33 = (bf16[224,1792]{1,0:T(8,128)(2,1)S(1)}, bf16[224,1792]{1,0:T(8,128)(2,1)S(1)}, u32[]{:S(2)}, u32[]{:S(2)}) collective-permute-start(bf16[224,1792]{1,0:T(8,128)(2,1)S(1)} %pad_maximum_fusion.9), channel_id=1, source_target_pairs={{0,1},{1,0},{2,3},{3,2},{4,5},{5,4},{6,7},{7,6},{8,9},{9,8},{10,11... | collective-permute-start | bytes 2408456 | tf_op jit(solution)/shard_map/ppermute | solution.py:12
  220.7 8.5 %collective-permute-start.36 = (bf16[56,1792]{1,0:T(8,128)(2,1)S(1)}, bf16[56,1792]{1,0:T(8,128)(2,1)S(1)}, u32[]{:S(2)}, u32[]{:S(2)}) collective-permute-start(bf16[56,1792]{1,0:T(8,128)(2,1)S(1)} %get-tuple-element.52), channel_id=1, source_target_pairs={{0,4},{2,6},{4,0},{6,2},{8,12},{10,14},{12,8},{14,10},{1,5},{3,7},... | collective-permute-start | bytes 602120 | tf_op jit(solution)/shard_map/ppermute | solution.py:256
  220.7 13.8 %collective-permute-start.37 = (bf16[56,1792]{1,0:T(8,128)(2,1)S(1)}, bf16[56,1792]{1,0:T(8,128)(2,1)S(1)}, u32[]{:S(2)}, u32[]{:S(2)}) collective-permute-start(bf16[56,1792]{1,0:T(8,128)(2,1)S(1)} %get-tuple-element.51), channel_id=1, source_target_pairs={{0,6},{2,4},{4,2},{6,0},{8,14},{10,12},{12,10},{14,8},{1,7},{3,5},... | collective-permute-start | bytes 602120 | tf_op jit(solution)/shard_map/ppermute | solution.py:256
  225.3 11.5 %collective-permute-start.26 = (bf16[56,1792]{1,0:T(8,128)(2,1)S(1)}, bf16[56,1792]{1,0:T(8,128)(2,1)S(1)}, u32[]{:S(2)}, u32[]{:S(2)}) collective-permute-start(bf16[56,1792]{1,0:T(8,128)(2,1)S(1)} %get-tuple-element.42), channel_id=1, source_target_pairs={{0,8},{2,10},{4,12},{6,14},{8,0},{10,2},{12,4},{14,6},{1,9},{3,11}... | collective-permute-start | bytes 602120 | tf_op jit(solution)/shard_map/ppermute | solution.py:256
  226.5 25.4 %collective-permute-start.27 = (bf16[56,1792]{1,0:T(8,128)(2,1)S(1)}, bf16[56,1792]{1,0:T(8,128)(2,1)S(1)}, u32[]{:S(2)}, u32[]{:S(2)}) collective-permute-start(bf16[56,1792]{1,0:T(8,128)(2,1)S(1)} %get-tuple-element.45), channel_id=1, source_target_pairs={{0,10},{2,8},{4,14},{6,12},{8,2},{10,0},{12,6},{14,4},{1,11},{3,9}... | collective-permute-start | bytes 602120 | tf_op jit(solution)/shard_map/ppermute | solution.py:256
  227.7 29.5 %collective-permute-start.28 = (bf16[56,1792]{1,0:T(8,128)(2,1)S(1)}, bf16[56,1792]{1,0:T(8,128)(2,1)S(1)}, u32[]{:S(2)}, u32[]{:S(2)}) collective-permute-start(bf16[56,1792]{1,0:T(8,128)(2,1)S(1)} %get-tuple-element.44), channel_id=1, source_target_pairs={{0,12},{2,14},{4,8},{6,10},{8,4},{10,6},{12,0},{14,2},{1,13},{3,15... | collective-permute-start | bytes 602120 | tf_op jit(solution)/shard_map/ppermute | solution.py:256
  229.2 32.3 %collective-permute-start.29 = (bf16[56,1792]{1,0:T(8,128)(2,1)S(1)}, bf16[56,1792]{1,0:T(8,128)(2,1)S(1)}, u32[]{:S(2)}, u32[]{:S(2)}) collective-permute-start(bf16[56,1792]{1,0:T(8,128)(2,1)S(1)} %get-tuple-element.43), channel_id=1, source_target_pairs={{0,14},{2,12},{4,10},{6,8},{8,6},{10,4},{12,2},{14,0},{1,15},{3,13... | collective-permute-start | bytes 602120 | tf_op jit(solution)/shard_map/ppermute | solution.py:256
  (25 other events, 441.5 us)
